TPU v7x, 32 devices: a whole 2x2x4 slice. The times are simulated.
32 devices in a mesh: lon: 8 (over z, y), lat: 4 (over x, core).
Axes of the slice: x: 2, y: 2, z: 4, core: 2. Of those that a mesh axis runs over, the one named last changes fastest.
Arguments:
- forcing: float32 [256, 2048], P('lat', 'lon'), may hold values from -27 to 27
- surface_term: float32 [256, 2048], P('lat', 'lon'), may hold values from 0.001 to 0.025
- sea_cells: int32 [256, 2048], P('lat', 'lon'), may hold values from 0 to 1, as said below
- levels: int32 [256, 2048], P('lat', 'lon'), may hold values from 4 to 60
Outputs:
- solution: float32 [256, 2048], P('lat', 'lon')
- residual: float32 [256, 2048], P('lat', 'lon')
Inputs may be any that keep to these rules, and one draw needn't show every extreme that they name: `sea_cells`: land (0) lies only at cells whose row and longitude index, counted from 0, are both even.
All inputs are finite; a program needn't handle non-finite values.
Results may differ from a plain program's by a relative error of at most 0.0003.
Values sent between devices are 32-bit elements; how exact they have to be, the bound alone decides.
No kernel may reach another device: no remote copies, remote signals or barrier semaphores. Data moves between devices by JAX's collectives and lax.ppermute only.
A program may use at most 64 MiB of HBM per device.

v0:
```python
import jax
import jax.numpy as jnp
from jax import lax
from jax.sharding import PartitionSpec as P

LEVELS = 3
SWEEPS = 2
BOTTOM_ITERS = 6


DAMPING = 0.8
ROW_STEP = 150.0 / 8640.0
BAND_SOUTH = -50.0


def with_halo(block, sides, width, periodic):
    for axis, dim in sides:
        count = lax.axis_size(axis)
        forward = [(i, i + 1) for i in range(count - 1)]
        if periodic:
            forward.append((count - 1, 0))
        backward = [(target, source) for source, target in forward]
        low = lax.ppermute(
            lax.slice_in_dim(block, block.shape[dim] - width, None, axis=dim), axis, forward
        )
        high = lax.ppermute(lax.slice_in_dim(block, 0, width, axis=dim), axis, backward)
        block = jnp.concatenate([low, block, high], axis=dim)
    return block


def depth_of(levels, sea_mask):
    layers = levels.astype(jnp.float32)
    return sea_mask * ((layers + layers * (layers - 1.0) / 20.0) / 200.0)


def metric(first_row, row_count):
    row_index = first_row + jnp.arange(row_count, dtype=jnp.float32)[:, None]
    center = jnp.cos(jnp.deg2rad(BAND_SOUTH + ROW_STEP * (row_index + 0.5)))
    northern = jnp.cos(jnp.deg2rad(BAND_SOUTH + ROW_STEP * (row_index + 1.0)))
    return (center, northern)


def stencil(field, east_val, west_val, north_val, south_val, coeffs):
    return coeffs[4] * field - (
        coeffs[0] * east_val + coeffs[1] * west_val + coeffs[2] * north_val + coeffs[3] * south_val
    )


def coarsen(east_face, north_face, source_term, sea_mask):
    east_next = east_face[0::2, 1::2] + east_face[1::2, 1::2]
    north_next = north_face[1::2, 0::2] + north_face[1::2, 1::2]
    source_next = (
        source_term[0::2, 0::2]
        + source_term[1::2, 0::2]
        + source_term[0::2, 1::2]
        + source_term[1::2, 1::2]
    )
    mask_next = jnp.maximum(
        jnp.maximum(sea_mask[0::2, 0::2], sea_mask[1::2, 0::2]),
        jnp.maximum(sea_mask[0::2, 1::2], sea_mask[1::2, 1::2]),
    )
    return (east_next, north_next, source_next, mask_next)


def restrict(field):
    return field[0::2, 0::2] + field[1::2, 0::2] + field[0::2, 1::2] + field[1::2, 1::2]


def prolong(field, sea_mask):
    return jnp.repeat(jnp.repeat(field, 2, axis=0), 2, axis=1) * sea_mask


def with_diagonal(east_face, west_face, north_face, south_face, source_term, sea_mask):
    diagonal = sea_mask * (source_term + east_face + west_face + north_face + south_face) + (
        1.0 - sea_mask
    )
    return (east_face, west_face, north_face, south_face, diagonal, 1.0 / diagonal)


def with_rims(stacked):
    widened = with_halo(stacked, (("lon", 2),), 1, True)
    return with_halo(widened, (("lat", 1),), 1, False)


def apply_grid(field, coeffs):
    padded = with_rims(field[None])[0]
    return stencil(
        field, padded[1:-1, 2:], padded[1:-1, :-2], padded[2:, 1:-1], padded[:-2, 1:-1], coeffs
    )


def apply_strip(field, coeffs):
    padded = with_halo(field[None], (("lat", 1),), 1, False)[0]
    east_val = jnp.roll(field, -1, axis=1)
    west_val = jnp.roll(field, 1, axis=1)
    return stencil(field, east_val, west_val, padded[2:], padded[:-2], coeffs)


def finish(east_face, north_face, source_term, sea_mask):
    padded = with_rims(jnp.stack([east_face, north_face]))
    west_face = padded[0, 1:-1, :-2]
    south_face = padded[1, :-2, 1:-1]
    return with_diagonal(east_face, west_face, north_face, south_face, source_term, sea_mask)


def smooth(field, source, coeffs):
    return field + DAMPING * coeffs[5] * (source - apply_grid(field, coeffs))


def conjugate(source, coeffs, apply_fn, total_fn):
    iterate = jnp.zeros_like(source)
    remain = source
    direction = source
    norm_now = total_fn(jnp.sum(remain * remain))
    for sweep_index in range(BOTTOM_ITERS):
        image = apply_fn(direction, coeffs)
        step_size = norm_now / total_fn(jnp.sum(direction * image))
        iterate = iterate + step_size * direction
        remain = remain - step_size * image
        norm_next = total_fn(jnp.sum(remain * remain))
        direction = remain + norm_next / norm_now * direction
        norm_now = norm_next
    return iterate


def strip_total(value):
    return lax.psum(value, "lat")


def on_device(forcing, surface_term, sea_cells, levels):
    row_count = forcing.shape[0]
    first_row = (lax.axis_index("lat") * row_count).astype(jnp.float32)
    sea_mask = sea_cells.astype(jnp.float32)
    depth = depth_of(levels, sea_mask)
    center, northern = metric(first_row, row_count)
    padded = with_rims(depth[None])[0]
    east_face = jnp.minimum(depth, padded[1:-1, 2:]) / center
    north_face = jnp.minimum(depth, padded[2:, 1:-1]) * northern
    source_term = surface_term * center * sea_mask
    coeff_list = []
    mask_list = []
    for level_index in range(LEVELS + 1):
        coeff_list.append(finish(east_face, north_face, source_term, sea_mask))
        mask_list.append(sea_mask)
        if level_index < LEVELS:
            east_face, north_face, source_term, sea_mask = coarsen(
                east_face, north_face, source_term, sea_mask
            )
    source = forcing * mask_list[0]
    first_source = source
    sources = []
    iterates = []
    for level_index in range(LEVELS):
        coeffs = coeff_list[level_index]
        field = DAMPING * coeffs[5] * source
        field = smooth(field, source, coeffs)
        image = apply_grid(field, coeffs)
        sources.append(source)
        iterates.append(field)
        source = restrict(source - image)
    coeffs = coeff_list[LEVELS]
    width = source.shape[1]
    stacked = jnp.stack([coeffs[0], coeffs[1], coeffs[2], coeffs[3], coeffs[4], source])
    gathered = lax.all_gather(stacked, "lon", axis=2, tiled=True)
    strip_coeffs = (gathered[0], gathered[1], gathered[2], gathered[3], gathered[4])
    strip_value = conjugate(gathered[5], strip_coeffs, apply_strip, strip_total)
    correction = lax.dynamic_slice_in_dim(
        strip_value, (lax.axis_index("lon") * width).astype(jnp.int32), width, 1
    )
    for level_index in range(LEVELS - 1, -1, -1):
        coeffs = coeff_list[level_index]
        field = iterates[level_index] + prolong(correction, mask_list[level_index])
        for sweep_index in range(SWEEPS):
            field = smooth(field, sources[level_index], coeffs)
        correction = field
    residual = first_source - apply_grid(correction, coeff_list[0])
    return (correction, residual)


def solution(mesh):
    return jax.shard_map(
        on_device,
        mesh=mesh,
        in_specs=(P("lat", "lon"), P("lat", "lon"), P("lat", "lon"), P("lat", "lon")),
        out_specs=(P("lat", "lon"), P("lat", "lon")),
        check_vma=False,
    )
```

profile of v0, /device:TPU:0, one launch (start us, length us, event | category | flops | bytes accessed | tf_op | source)
XLA Modules:
  0.0 420.6 jit_solution(9909669072662154750)
XLA Ops:
  30.3 6.3 %collective-permute-done.33 = f32[2,8,1]{2,1,0:T(8,128)S(1)} collective-permute-done((f32[2,8,1]{2,1,0:T(8,128)S(1)}, f32[2,8,1]{2,1,0:T(8,128)S(1)}, u32[]{:S(2)}, u32[]{:S(2)}) %collective-permute-start.33) | collective-permute-done | bytes 96 | tf_op jit(solution)/shard_map/ppermute | solution.py:23
  36.8 4.8 %collective-permute-start.23 = (f32[2,16,1]{2,1,0:T(8,128)S(1)}, f32[2,16,1]{2,1,0:T(8,128)S(1)}, u32[]{:S(2)}, u32[]{:S(2)}) collective-permute-start(f32[2,16,1]{2,1,0:T(8,128)S(1)} %get-tuple-element.133), channel_id=1, source_target_pairs={{4,0},{8,4},{12,8},{16,12},{20,16},{24,20},{28,24},{0,28},{5,1},{9... | collective-permute-start | bytes 392 | tf_op jit(solution)/shard_map/ppermute | solution.py:26
  48.4 9.2 %collective-permute-start.35 = (f32[2,1,34]{1,2,0:T(8,128)}, f32[2,1,34]{1,2,0:T(8,128)}, u32[]{:S(2)}, u32[]{:S(2)}) collective-permute-start(f32[2,1,34]{1,2,0:T(8,128)} %slice.1020), channel_id=1, source_target_pairs={{0,1},{1,2},{2,3},{4,5},{5,6},{6,7},{8,9},{9,10},{10,11},{12,13},{... | collective-permute-start | bytes 824 | tf_op jit(solution)/shard_map/ppermute | solution.py:23
  79.5 4.9 %collective-permute-start.16 = (f32[1,1,258]{1,2,0:T(8,128)S(1)}, f32[1,1,258]{1,2,0:T(8,128)S(1)}, u32[]{:S(2)}, u32[]{:S(2)}) collective-permute-start(f32[1,1,258]{1,2,0:T(8,128)S(1)} %get-tuple-element.81), channel_id=1, source_target_pairs={{0,1},{1,2},{2,3},{4,5},{5,6},{6,7},{8,9},{9,10},{10,11},{12,13},{... | collective-permute-start | bytes 3104 | tf_op jit(solution)/shard_map/ppermute | solution.py:23
  121.2 4.8 %collective-permute-start.30 = (f32[1,16,1]{1,2,0:T(1,128)S(1)}, f32[1,16,1]{1,2,0:T(1,128)S(1)}, u32[]{:S(2)}, u32[]{:S(2)}) collective-permute-start(f32[1,16,1]{1,2,0:T(1,128)S(1)} %get-tuple-element.130), channel_id=1, source_target_pairs={{4,0},{8,4},{12,8},{16,12},{20,16},{24,20},{28,24},{0,28},{5,1},{9... | collective-permute-start | bytes 200 | tf_op jit(solution)/shard_map/ppermute | solution.py:26
  135.2 4.8 %collective-permute-start.37 = (f32[1,16,1]{1,2,0:T(1,128)S(1)}, f32[1,16,1]{1,2,0:T(1,128)S(1)}, u32[]{:S(2)}, u32[]{:S(2)}) collective-permute-start(f32[1,16,1]{1,2,0:T(1,128)S(1)} %get-tuple-element.128), channel_id=1, source_target_pairs={{4,0},{8,4},{12,8},{16,12},{20,16},{24,20},{28,24},{0,28},{5,1},{9... | collective-permute-start | bytes 200 | tf_op jit(solution)/shard_map/ppermute | solution.py:26
  149.5 34.8 %all_gather.3 = f32[6,8,256]{1,0,2:T(8,128)S(1)} all-gather(f32[6,8,32]{1,0,2:T(8,128)S(1)} %copy.484), channel_id=1, replica_groups=mesh['lon'=8,'lat'=4] {'lon'}, dimensions={2}, use_global_device_ids=true | all-gather | bytes 55296 | tf_op jit(solution)/shard_map/all_gather | solution.py:164
  191.4 8.4 %all-reduce = (f32[]{:T(128)}, f32[]{:T(128)}) all-reduce(f32[]{:T(128)} %get-tuple-element.17, f32[]{:T(128)} %get-tuple-element.16), channel_id=1, replica_groups=mesh['lon'=8,'lat'=4] {'lat'}, use_global_device_ids=true, to_apply=%region_1.0 | all-reduce | flops 2 | bytes 16 | tf_op jit(solution)/shard_map/psum | solution.py:127
  201.7 7.5 %psum.86 = f32[]{:T(128)} all-reduce(f32[]{:T(128)} %multiply_reduce_fusion.8), channel_id=1, replica_groups=mesh['lon'=8,'lat'=4] {'lat'}, use_global_device_ids=true, to_apply=%region_5.6 | all-reduce | flops 1 | bytes 8 | tf_op jit(solution)/shard_map/psum | solution.py:127
  216.6 6.9 %psum.87 = f32[]{:T(128)} all-reduce(f32[]{:T(128)} %get-tuple-element.36), channel_id=1, replica_groups=mesh['lon'=8,'lat'=4] {'lat'}, use_global_device_ids=true, to_apply=%region_7.8 | all-reduce | flops 1 | bytes 8 | tf_op jit(solution)/shard_map/psum | solution.py:127
  225.4 7.5 %psum.88 = f32[]{:T(128)} all-reduce(f32[]{:T(128)} %get-tuple-element.34), channel_id=1, replica_groups=mesh['lon'=8,'lat'=4] {'lat'}, use_global_device_ids=true, to_apply=%region_9.10 | all-reduce | flops 1 | bytes 8 | tf_op jit(solution)/shard_map/psum | solution.py:127
  240.3 6.9 %psum.89 = f32[]{:T(128)} all-reduce(f32[]{:T(128)} %get-tuple-element.30), channel_id=1, replica_groups=mesh['lon'=8,'lat'=4] {'lat'}, use_global_device_ids=true, to_apply=%region_11.12 | all-reduce | flops 1 | bytes 8 | tf_op jit(solution)/shard_map/psum | solution.py:127
  249.1 7.5 %psum.90 = f32[]{:T(128)} all-reduce(f32[]{:T(128)} %get-tuple-element.28), channel_id=1, replica_groups=mesh['lon'=8,'lat'=4] {'lat'}, use_global_device_ids=true, to_apply=%region_13.14 | all-reduce | flops 1 | bytes 8 | tf_op jit(solution)/shard_map/psum | solution.py:127
  264.0 6.9 %psum.91 = f32[]{:T(128)} all-reduce(f32[]{:T(128)} %get-tuple-element.24), channel_id=1, replica_groups=mesh['lon'=8,'lat'=4] {'lat'}, use_global_device_ids=true, to_apply=%region_15.16 | all-reduce | flops 1 | bytes 8 | tf_op jit(solution)/shard_map/psum | solution.py:127
  272.8 7.7 %psum.92 = f32[]{:T(128)} all-reduce(f32[]{:T(128)} %get-tuple-element.22), channel_id=1, replica_groups=mesh['lon'=8,'lat'=4] {'lat'}, use_global_device_ids=true, to_apply=%region_17.18 | all-reduce | flops 1 | bytes 8 | tf_op jit(solution)/shard_map/psum | solution.py:127
  287.9 6.9 %psum.93 = f32[]{:T(128)} all-reduce(f32[]{:T(128)} %get-tuple-element.20), channel_id=1, replica_groups=mesh['lon'=8,'lat'=4] {'lat'}, use_global_device_ids=true, to_apply=%region_19.20 | all-reduce | flops 1 | bytes 8 | tf_op jit(solution)/shard_map/psum | solution.py:127
  296.7 7.5 %psum.94 = f32[]{:T(128)} all-reduce(f32[]{:T(128)} %multiply_reduce_fusion), channel_id=1, replica_groups=mesh['lon'=8,'lat'=4] {'lat'}, use_global_device_ids=true, to_apply=%region_21.22 | all-reduce | flops 1 | bytes 8 | tf_op jit(solution)/shard_map/psum | solution.py:127
  311.5 6.9 %psum.95 = f32[]{:T(128)} all-reduce(f32[]{:T(128)} %fusion.118), channel_id=1, replica_groups=mesh['lon'=8,'lat'=4] {'lat'}, use_global_device_ids=true, to_apply=%region_23.24 | all-reduce | flops 1 | bytes 8 | tf_op jit(solution)/shard_map/psum | solution.py:127
  333.2 4.8 %collective-permute-start.57 = (f32[1,16,1]{1,2,0:T(1,128)S(1)}, f32[1,16,1]{1,2,0:T(1,128)S(1)}, u32[]{:S(2)}, u32[]{:S(2)}) collective-permute-start(f32[1,16,1]{1,2,0:T(1,128)S(1)} %get-tuple-element.124), channel_id=1, source_target_pairs={{4,0},{8,4},{12,8},{16,12},{20,16},{24,20},{28,24},{0,28},{5,1},{9... | collective-permute-start | bytes 200 | tf_op jit(solution)/shard_map/ppermute | solution.py:26
  347.2 4.8 %collective-permute-start.61 = (f32[1,32,1]{1,2,0:T(1,128)S(1)}, f32[1,32,1]{1,2,0:T(1,128)S(1)}, u32[]{:S(2)}, u32[]{:S(2)}) collective-permute-start(f32[1,32,1]{1,2,0:T(1,128)S(1)} %get-tuple-element.110), channel_id=1, source_target_pairs={{4,0},{8,4},{12,8},{16,12},{20,16},{24,20},{28,24},{0,28},{5,1},{9... | collective-permute-start | bytes 392 | tf_op jit(solution)/shard_map/ppermute | solution.py:26
  361.2 4.8 %collective-permute-start.65 = (f32[1,32,1]{1,2,0:T(1,128)S(1)}, f32[1,32,1]{1,2,0:T(1,128)S(1)}, u32[]{:S(2)}, u32[]{:S(2)}) collective-permute-start(f32[1,32,1]{1,2,0:T(1,128)S(1)} %get-tuple-element.108), channel_id=1, source_target_pairs={{4,0},{8,4},{12,8},{16,12},{20,16},{24,20},{28,24},{0,28},{5,1},{9... | collective-permute-start | bytes 392 | tf_op jit(solution)/shard_map/ppermute | solution.py:26
  375.6 4.8 %collective-permute-start.69 = (f32[1,64,1]{1,2,0:T(1,128)S(1)}, f32[1,64,1]{1,2,0:T(1,128)S(1)}, u32[]{:S(2)}, u32[]{:S(2)}) collective-permute-start(f32[1,64,1]{1,2,0:T(1,128)S(1)} %get-tuple-element.92), channel_id=1, source_target_pairs={{4,0},{8,4},{12,8},{16,12},{20,16},{24,20},{28,24},{0,28},{5,1},{9... | collective-permute-start | bytes 776 | tf_op jit(solution)/shard_map/ppermute | solution.py:26
  390.1 4.8 %collective-permute-start.73 = (f32[1,64,1]{1,2,0:T(1,128)S(1)}, f32[1,64,1]{1,2,0:T(1,128)S(1)}, u32[]{:S(2)}, u32[]{:S(2)}) collective-permute-start(f32[1,64,1]{1,2,0:T(1,128)S(1)} %get-tuple-element.90), channel_id=1, source_target_pairs={{4,0},{8,4},{12,8},{16,12},{20,16},{24,20},{28,24},{0,28},{5,1},{9... | collective-permute-start | bytes 776 | tf_op jit(solution)/shard_map/ppermute | solution.py:26
  405.0 4.8 %collective-permute-start.77 = (f32[1,64,1]{1,2,0:T(1,128)S(1)}, f32[1,64,1]{1,2,0:T(1,128)S(1)}, u32[]{:S(2)}, u32[]{:S(2)}) collective-permute-start(f32[1,64,1]{1,2,0:T(1,128)S(1)} %get-tuple-element.88), channel_id=1, source_target_pairs={{4,0},{8,4},{12,8},{16,12},{20,16},{24,20},{28,24},{0,28},{5,1},{9... | collective-permute-start | bytes 776 | tf_op jit(solution)/shard_map/ppermute | solution.py:26
  (398 shorter events, 224.3 us)
Async XLA Ops:
  1.8 7.6 %collective-permute-start = (f32[1,64,1]{1,2,0:T(1,128)S(1)}, f32[1,64,1]{1,2,0:T(1,128)S(1)}, u32[]{:S(2)}, u32[]{:S(2)}) collective-permute-start(f32[1,64,1]{1,2,0:T(1,128)S(1)} %get-tuple-element.97), channel_id=1, source_target_pairs={{0,4},{4,8},{8,12},{12,16},{16,20},{20,24},{24,28},{28,0},{1,5},{5... | collective-permute-start | bytes 776 | tf_op jit(solution)/shard_map/ppermute | solution.py:23
  9.5 6.3 %collective-permute-start.2 = (f32[1,1,258]{1,2,0:T(8,128)S(1)}, f32[1,1,258]{1,2,0:T(8,128)S(1)}, u32[]{:S(2)}, u32[]{:S(2)}) collective-permute-start(f32[1,1,258]{1,2,0:T(8,128)S(1)} %get-tuple-element.85), channel_id=1, source_target_pairs={{0,1},{1,2},{2,3},{4,5},{5,6},{6,7},{8,9},{9,10},{10,11},{12,13},{... | collective-permute-start | bytes 3104 | tf_op jit(solution)/shard_map/ppermute | solution.py:23
  20.1 16.7 %collective-permute-start.4 = (f32[2,64,1]{1,2,0:T(1,128)S(1)}, f32[2,64,1]{1,2,0:T(1,128)S(1)}, u32[]{:S(2)}, u32[]{:S(2)}) collective-permute-start(f32[2,64,1]{1,2,0:T(1,128)S(1)} %get-tuple-element.74), channel_id=1, source_target_pairs={{0,4},{4,8},{8,12},{12,16},{16,20},{20,24},{24,28},{28,0},{1,5},{5... | collective-permute-start | bytes 1544 | tf_op jit(solution)/shard_map/ppermute | solution.py:23
  21.4 20.1 %collective-permute-start.5 = (f32[2,64,1]{1,2,0:T(1,128)S(1)}, f32[2,64,1]{1,2,0:T(1,128)S(1)}, u32[]{:S(2)}, u32[]{:S(2)}) collective-permute-start(f32[2,64,1]{1,2,0:T(1,128)S(1)} %get-tuple-element.73), channel_id=1, source_target_pairs={{4,0},{8,4},{12,8},{16,12},{20,16},{24,20},{28,24},{0,28},{5,1},{9... | collective-permute-start | bytes 1544 | tf_op jit(solution)/shard_map/ppermute | solution.py:26
  25.1 43.7 %collective-permute-start.11 = (f32[2,32,1]{2,1,0:T(8,128)S(1)}, f32[2,32,1]{2,1,0:T(8,128)S(1)}, u32[]{:S(2)}, u32[]{:S(2)}) collective-permute-start(f32[2,32,1]{2,1,0:T(8,128)S(1)} %get-tuple-element.132), channel_id=1, source_target_pairs={{0,4},{4,8},{8,12},{12,16},{16,20},{20,24},{24,28},{28,0},{1,5},{5... | collective-permute-start | bytes 776 | tf_op jit(solution)/shard_map/ppermute | solution.py:23
  25.2 43.7 %collective-permute-start.12 = (f32[2,32,1]{2,1,0:T(8,128)S(1)}, f32[2,32,1]{2,1,0:T(8,128)S(1)}, u32[]{:S(2)}, u32[]{:S(2)}) collective-permute-start(f32[2,32,1]{2,1,0:T(8,128)S(1)} %get-tuple-element.131), channel_id=1, source_target_pairs={{4,0},{8,4},{12,8},{16,12},{20,16},{24,20},{28,24},{0,28},{5,1},{9... | collective-permute-start | bytes 776 | tf_op jit(solution)/shard_map/ppermute | solution.py:26
  30.2 6.4 %collective-permute-start.33 = (f32[2,8,1]{2,1,0:T(8,128)S(1)}, f32[2,8,1]{2,1,0:T(8,128)S(1)}, u32[]{:S(2)}, u32[]{:S(2)}) collective-permute-start(f32[2,8,1]{2,1,0:T(8,128)S(1)} %get-tuple-element.190), channel_id=1, source_target_pairs={{0,4},{4,8},{8,12},{12,16},{16,20},{20,24},{24,28},{28,0},{1,5},{5... | collective-permute-start | bytes 200 | tf_op jit(solution)/shard_map/ppermute | solution.py:23
  36.6 21.2 %collective-permute-start.22 = (f32[2,16,1]{2,1,0:T(8,128)S(1)}, f32[2,16,1]{2,1,0:T(8,128)S(1)}, u32[]{:S(2)}, u32[]{:S(2)}) collective-permute-start(f32[2,16,1]{2,1,0:T(8,128)S(1)} %get-tuple-element.134), channel_id=1, source_target_pairs={{0,4},{4,8},{8,12},{12,16},{16,20},{20,24},{24,28},{28,0},{1,5},{5... | collective-permute-start | bytes 392 | tf_op jit(solution)/shard_map/ppermute | solution.py:23
  36.8 21.1 %collective-permute-start.23 = (f32[2,16,1]{2,1,0:T(8,128)S(1)}, f32[2,16,1]{2,1,0:T(8,128)S(1)}, u32[]{:S(2)}, u32[]{:S(2)}) collective-permute-start(f32[2,16,1]{2,1,0:T(8,128)S(1)} %get-tuple-element.133), channel_id=1, source_target_pairs={{4,0},{8,4},{12,8},{16,12},{20,16},{24,20},{28,24},{0,28},{5,1},{9... | collective-permute-start | bytes 392 | tf_op jit(solution)/shard_map/ppermute | solution.py:26
  48.4 62.4 %collective-permute-start.35 = (f32[2,1,34]{1,2,0:T(8,128)}, f32[2,1,34]{1,2,0:T(8,128)}, u32[]{:S(2)}, u32[]{:S(2)}) collective-permute-start(f32[2,1,34]{1,2,0:T(8,128)} %slice.1020), channel_id=1, source_target_pairs={{0,1},{1,2},{2,3},{4,5},{5,6},{6,7},{8,9},{9,10},{10,11},{12,13},{... | collective-permute-start | bytes 824 | tf_op jit(solution)/shard_map/ppermute | solution.py:23
  70.2 9.2 %collective-permute-start.14 = (f32[1,64,1]{1,2,0:T(1,128)S(1)}, f32[1,64,1]{1,2,0:T(1,128)S(1)}, u32[]{:S(2)}, u32[]{:S(2)}) collective-permute-start(f32[1,64,1]{1,2,0:T(1,128)S(1)} %get-tuple-element.93), channel_id=1, source_target_pairs={{0,4},{4,8},{8,12},{12,16},{16,20},{20,24},{24,28},{28,0},{1,5},{5... | collective-permute-start | bytes 776 | tf_op jit(solution)/shard_map/ppermute | solution.py:23
  70.2 9.1 %collective-permute-start.15 = (f32[1,64,1]{1,2,0:T(1,128)S(1)}, f32[1,64,1]{1,2,0:T(1,128)S(1)}, u32[]{:S(2)}, u32[]{:S(2)}) collective-permute-start(f32[1,64,1]{1,2,0:T(1,128)S(1)} %get-tuple-element.94), channel_id=1, source_target_pairs={{4,0},{8,4},{12,8},{16,12},{20,16},{24,20},{28,24},{0,28},{5,1},{9... | collective-permute-start | bytes 776 | tf_op jit(solution)/shard_map/ppermute | solution.py:26
  75.2 16.2 %collective-permute-start.13 = (f32[2,1,130]{1,2,0:T(8,128)S(1)}, f32[2,1,130]{1,2,0:T(8,128)S(1)}, u32[]{:S(2)}, u32[]{:S(2)}) collective-permute-start(f32[2,1,130]{1,2,0:T(8,128)S(1)} %copy.472), channel_id=1, source_target_pairs={{0,1},{1,2},{2,3},{4,5},{5,6},{6,7},{8,9},{9,10},{10,11},{12,13},{... | collective-permute-start | bytes 3128 | tf_op jit(solution)/shard_map/ppermute | solution.py:23
  79.5 9.0 %collective-permute-start.16 = (f32[1,1,258]{1,2,0:T(8,128)S(1)}, f32[1,1,258]{1,2,0:T(8,128)S(1)}, u32[]{:S(2)}, u32[]{:S(2)}) collective-permute-start(f32[1,1,258]{1,2,0:T(8,128)S(1)} %get-tuple-element.81), channel_id=1, source_target_pairs={{0,1},{1,2},{2,3},{4,5},{5,6},{6,7},{8,9},{9,10},{10,11},{12,13},{... | collective-permute-start | bytes 3104 | tf_op jit(solution)/shard_map/ppermute | solution.py:23
  91.5 8.3 %collective-permute-start.18 = (f32[1,32,1]{1,2,0:T(1,128)S(1)}, f32[1,32,1]{1,2,0:T(1,128)S(1)}, u32[]{:S(2)}, u32[]{:S(2)}) collective-permute-start(f32[1,32,1]{1,2,0:T(1,128)S(1)} %get-tuple-element.113), channel_id=1, source_target_pairs={{0,4},{4,8},{8,12},{12,16},{16,20},{20,24},{24,28},{28,0},{1,5},{5... | collective-permute-start | bytes 392 | tf_op jit(solution)/shard_map/ppermute | solution.py:23
  91.6 8.2 %collective-permute-start.19 = (f32[1,32,1]{1,2,0:T(1,128)S(1)}, f32[1,32,1]{1,2,0:T(1,128)S(1)}, u32[]{:S(2)}, u32[]{:S(2)}) collective-permute-start(f32[1,32,1]{1,2,0:T(1,128)S(1)} %get-tuple-element.114), channel_id=1, source_target_pairs={{4,0},{8,4},{12,8},{16,12},{20,16},{24,20},{28,24},{0,28},{5,1},{9... | collective-permute-start | bytes 392 | tf_op jit(solution)/shard_map/ppermute | solution.py:26
  96.3 24.3 %collective-permute-start.24 = (f32[2,1,66]{1,2,0:T(8,128)S(1)}, f32[2,1,66]{1,2,0:T(8,128)S(1)}, u32[]{:S(2)}, u32[]{:S(2)}) collective-permute-start(f32[2,1,66]{1,2,0:T(8,128)S(1)} %copy-done.2), channel_id=1, source_target_pairs={{0,1},{1,2},{2,3},{4,5},{5,6},{6,7},{8,9},{9,10},{10,11},{12,13},{... | collective-permute-start | bytes 1592 | tf_op jit(solution)/shard_map/ppermute | solution.py:23
  135.2 6.4 %collective-permute-start.36 = (f32[1,16,1]{1,2,0:T(1,128)S(1)}, f32[1,16,1]{1,2,0:T(1,128)S(1)}, u32[]{:S(2)}, u32[]{:S(2)}) collective-permute-start(f32[1,16,1]{1,2,0:T(1,128)S(1)} %get-tuple-element.127), channel_id=1, source_target_pairs={{0,4},{4,8},{8,12},{12,16},{16,20},{20,24},{24,28},{28,0},{1,5},{5... | collective-permute-start | bytes 200 | tf_op jit(solution)/shard_map/ppermute | solution.py:23
  347.1 6.4 %collective-permute-start.60 = (f32[1,32,1]{1,2,0:T(1,128)S(1)}, f32[1,32,1]{1,2,0:T(1,128)S(1)}, u32[]{:S(2)}, u32[]{:S(2)}) collective-permute-start(f32[1,32,1]{1,2,0:T(1,128)S(1)} %get-tuple-element.109), channel_id=1, source_target_pairs={{0,4},{4,8},{8,12},{12,16},{16,20},{20,24},{24,28},{28,0},{1,5},{5... | collective-permute-start | bytes 392 | tf_op jit(solution)/shard_map/ppermute | solution.py:23
  361.1 6.4 %collective-permute-start.64 = (f32[1,32,1]{1,2,0:T(1,128)S(1)}, f32[1,32,1]{1,2,0:T(1,128)S(1)}, u32[]{:S(2)}, u32[]{:S(2)}) collective-permute-start(f32[1,32,1]{1,2,0:T(1,128)S(1)} %get-tuple-element.107), channel_id=1, source_target_pairs={{0,4},{4,8},{8,12},{12,16},{16,20},{20,24},{24,28},{28,0},{1,5},{5... | collective-permute-start | bytes 392 | tf_op jit(solution)/shard_map/ppermute | solution.py:23
  375.6 6.4 %collective-permute-start.68 = (f32[1,64,1]{1,2,0:T(1,128)S(1)}, f32[1,64,1]{1,2,0:T(1,128)S(1)}, u32[]{:S(2)}, u32[]{:S(2)}) collective-permute-start(f32[1,64,1]{1,2,0:T(1,128)S(1)} %get-tuple-element.91), channel_id=1, source_target_pairs={{0,4},{4,8},{8,12},{12,16},{16,20},{20,24},{24,28},{28,0},{1,5},{5... | collective-permute-start | bytes 776 | tf_op jit(solution)/shard_map/ppermute | solution.py:23
  390.0 6.4 %collective-permute-start.72 = (f32[1,64,1]{1,2,0:T(1,128)S(1)}, f32[1,64,1]{1,2,0:T(1,128)S(1)}, u32[]{:S(2)}, u32[]{:S(2)}) collective-permute-start(f32[1,64,1]{1,2,0:T(1,128)S(1)} %get-tuple-element.89), channel_id=1, source_target_pairs={{0,4},{4,8},{8,12},{12,16},{16,20},{20,24},{24,28},{28,0},{1,5},{5... | collective-permute-start | bytes 776 | tf_op jit(solution)/shard_map/ppermute | solution.py:23
  405.0 6.4 %collective-permute-start.76 = (f32[1,64,1]{1,2,0:T(1,128)S(1)}, f32[1,64,1]{1,2,0:T(1,128)S(1)}, u32[]{:S(2)}, u32[]{:S(2)}) collective-permute-start(f32[1,64,1]{1,2,0:T(1,128)S(1)} %get-tuple-element.87), channel_id=1, source_target_pairs={{0,4},{4,8},{8,12},{12,16},{16,20},{20,24},{24,28},{28,0},{1,5},{5... | collective-permute-start | bytes 776 | tf_op jit(solution)/shard_map/ppermute | solution.py:23
  411.4 6.6 %collective-permute-start.78 = (f32[1,1,258]{1,2,0:T(8,128)S(1)}, f32[1,1,258]{1,2,0:T(8,128)S(1)}, u32[]{:S(2)}, u32[]{:S(2)}) collective-permute-start(f32[1,1,258]{1,2,0:T(8,128)S(1)} %get-tuple-element.75), channel_id=1, source_target_pairs={{0,1},{1,2},{2,3},{4,5},{5,6},{6,7},{8,9},{9,10},{10,11},{12,13},{... | collective-permute-start | bytes 3104 | tf_op jit(solution)/shard_map/ppermute | solution.py:23
  (64 other events, 296.4 us)
where the time goes:
time: 426 us; the launch traced here: 421 us
  starting transfers between devices  196 us (46%)
  blocking collectives  115 us (27%)
  waiting for transfers between devices  53.4 us (13%)
  local copies, waits for them, and re-layouts  25.3 us (6%)
  between operations  17.1 us (4%)
  other arithmetic  13.8 us (3%)
    ppermute x38, starting transfers between devices, with_halo(): lax.ppermute(lax.slice_in_dim(block, 0, width, axis=dim), axis, backward)  104 us
    ppermute x42, starting transfers between devices, with_halo(): lax.ppermute(lax.slice_in_dim(block, block.shape[dim] - width, None, axis...  91.4 us
    psum x11, blocking collectives, strip_total(): return lax.psum(value, 'lat')  80.7 us
    all_gather x1, blocking collectives, on_device(): gathered = lax.all_gather(stacked, 'lon', axis=2, tiled=True)  34.8 us
    ppermute x42, waiting for transfers between devices, with_halo(): lax.ppermute(lax.slice_in_dim(block, block.shape[dim] - width, None, axis...  27.2 us
    ppermute x38, waiting for transfers between devices, with_halo(): lax.ppermute(lax.slice_in_dim(block, 0, width, axis=dim), axis, backward)  26.2 us
  transfers between devices with their start and end apart: 80, of which 34 were waited for; matrix products, arithmetic and copies ran while one was open for 4% of the time, Pallas kernels for 0%

commit v1 on v0

v1 whole, which is shorter than its diff:
```python
import functools

import jax
import jax.numpy as jnp
from jax import lax
from jax.experimental import pallas as pl
from jax.experimental.pallas import tpu as pltpu
from jax.sharding import PartitionSpec as P

LEVELS = 3
SWEEPS = 2
BOTTOM_ITERS = 6

DAMPING = 0.8
ROW_STEP = 150.0 / 8640.0
BAND_SOUTH = -50.0

HALO = 32
LANES = 128
TILE = 8
FIELDS = 3
VMEM = pltpu.VMEM


def iota(shape, dim):
    return lax.broadcasted_iota(jnp.int32, shape, dim)


def lane_shift(field, count):
    width = field.shape[1]
    return pltpu.roll(field, (-count) % width, 1)


def row_shift(field, count):
    height = field.shape[0]
    return pltpu.roll(field, (-count) % height, 0)


def operator(field, east_face, north_face, diagonal, stride):
    side = east_face * lane_shift(field, stride) + lane_shift(east_face * field, -stride)
    ends = north_face * row_shift(field, 1) + row_shift(north_face * field, -1)
    return diagonal * field - (side + ends)


def level_diagonal(east_face, north_face, source_term, stride):
    total = source_term + (
        (east_face + lane_shift(east_face, -stride)) + (north_face + row_shift(north_face, -1))
    )
    return jnp.where(source_term > 0.0, total, 1.0)


def descend(where_ref, own_ref, lat_near_ref, lat_far_ref, lon_near_ref, lon_far_ref, scale_ref,
            pack_ref, *rest):
    level_refs = [rest[5 * i : 5 * i + 5] for i in range(LEVELS)]
    mask_ref, grid_ref, fold_ref = rest[5 * LEVELS :]
    lon_index = where_ref[0]
    lon_odd = lax.rem(lon_index, 2)
    lat_odd = lax.rem(where_ref[1], 2)
    rows, cols = own_ref.shape[1], own_ref.shape[2]
    height = rows + 2 * HALO
    width = cols + LANES
    near_row = rows + pl.multiple_of(lat_odd * HALO, HALO)
    far_row = rows + pl.multiple_of((1 - lat_odd) * HALO, HALO)
    lane = iota((TILE, LANES), 1)
    slot = lane // HALO
    for part, (rows_at, count, near, far, body) in enumerate((
        (0, rows, lon_near_ref, lon_far_ref, own_ref),
        (near_row, HALO, None, None, lat_near_ref),
        (far_row, HALO, None, None, lat_far_ref),
    )):
        for f in range(FIELDS):
            if part == 0:
                grid_ref[f, pl.ds(0, rows), pl.ds(0, cols)] = body[f]
            else:
                grid_ref[f, pl.ds(rows_at, count), pl.ds(0, cols)] = body[:, f * cols : (f + 1) * cols]
        if part == 0:
            near_val, far_val = near[...], far[...]
        else:
            near_val = body[:, FIELDS * cols : FIELDS * cols + LANES]
            far_val = body[:, FIELDS * cols + LANES :]
        odd = jnp.broadcast_to(lon_odd, near_val.shape) > 0
        east_val = jnp.where(odd, far_val, near_val)
        west_val = jnp.where(odd, near_val, far_val)
        slots = iota(near_val.shape, 1) // HALO
        for f in range(FIELDS):
            both = jnp.where(
                slots == f, east_val, jnp.where(slots == (f + 3) % 4, west_val, 0.0)
            )
            grid_ref[f, pl.ds(rows_at, count), pl.ds(cols, LANES)] = lane_shift(both, f * HALO)

    depth = grid_ref[0]
    inverse_center = jnp.concatenate([scale_ref[0]] * (width // LANES), axis=1)
    northern = jnp.concatenate([scale_ref[1]] * (width // LANES), axis=1)
    east_face = jnp.minimum(depth, lane_shift(depth, 1)) * inverse_center
    north_face = jnp.minimum(depth, row_shift(depth, 1)) * northern
    source_term = grid_ref[1]
    source = grid_ref[2]
    mask_ref[...] = jnp.where(source_term > 0.0, 1.0, 0.0)
    for level in range(LEVELS):
        stride = 1 << level
        diagonal = level_diagonal(east_face, north_face, source_term, stride)
        inverse = DAMPING / diagonal
        field = inverse * source
        for _ in range(SWEEPS - 1):
            field = field + inverse * (source - operator(field, east_face, north_face, diagonal, stride))
        image = source - operator(field, east_face, north_face, diagonal, stride)
        east_ref, north_ref, diagonal_ref, source_ref, field_ref = level_refs[level]
        east_ref[...] = east_face
        north_ref[...] = north_face
        diagonal_ref[...] = diagonal
        source_ref[...] = source
        field_ref[...] = field
        half = height >> (level + 1)
        even = pl.ds(0, half, stride=2)
        odd_rows = pl.ds(1, half, stride=2)

        def put(slot_index, value):
            for c in range(width // LANES):
                fold_ref[slot_index, c, pl.ds(0, 2 * half), :] = value[:, c * LANES : (c + 1) * LANES]

        def get(slot_index, which):
            return jnp.concatenate(
                [fold_ref[slot_index, c, which, :] for c in range(width // LANES)], axis=1
            )

        put(0, east_face)
        put(1, north_face)
        put(2, source_term)
        put(3, image)
        east_sum = get(0, even) + get(0, odd_rows)
        east_face = lane_shift(east_sum, stride)
        north_odd = get(1, odd_rows)
        north_face = north_odd + lane_shift(north_odd, stride)
        term_sum = get(2, even) + get(2, odd_rows)
        source_term = term_sum + lane_shift(term_sum, stride)
        image_sum = get(3, even) + get(3, odd_rows)
        source = image_sum + lane_shift(image_sum, stride)

    stride = 1 << LEVELS
    bottom_width = cols // stride
    per_column = LANES // stride
    cell = lane % bottom_width
    pick = (cell % per_column) * stride
    packed = jnp.zeros((TILE, LANES), jnp.float32)
    turn = lax.rem(lane // bottom_width + (LANES // bottom_width) - lax.rem(lon_index, LANES // bottom_width),
                   LANES // bottom_width)
    for f, value in enumerate((source, east_face, north_face, source_term)):
        flat = jnp.zeros((TILE, LANES), jnp.float32)
        for c in range(cols // LANES):
            taken = jnp.take_along_axis(value[:TILE, c * LANES : (c + 1) * LANES], pick, axis=1)
            flat = jnp.where(cell // per_column == c, taken, flat)
        packed = jnp.where(turn == f, flat, packed)
    pack_ref[...] = packed


def total(value):
    height, width = value.shape
    parts = [
        value[r : r + TILE, c : c + LANES]
        for r in range(0, height, TILE)
        for c in range(0, width, LANES)
    ]
    while len(parts) > 1:
        parts = [parts[i] + parts[i + 1] if i + 1 < len(parts) else parts[i] for i in range(0, len(parts), 2)]
    return jnp.sum(jnp.sum(parts[0], axis=0, keepdims=True), axis=1, keepdims=True)


def ascend(lat_count, lon_count, where_ref, blocks_ref, *rest):
    level_refs = [rest[5 * i : 5 * i + 5] for i in range(LEVELS)]
    mask_ref, solution_ref, residual_ref, window_ref, fold_ref = rest[5 * LEVELS :]
    lon_index = where_ref[0]
    lat_index = where_ref[1]
    rows, cols = solution_ref.shape
    height = rows + 2 * HALO
    width = cols + LANES
    stride = 1 << LEVELS
    bottom_rows = rows // stride
    bottom_width = cols // stride
    group = LANES // bottom_width
    slot = iota((bottom_rows, LANES), 1) // bottom_width
    fields = []
    for f in range(4):
        strips = []
        for a in range(lat_count):
            pieces = []
            for c in range(lon_count // group):
                merged = None
                for j in range(group):
                    block = blocks_ref[(c * group + j) * lat_count + a]
                    merged = block if merged is None else jnp.where(slot == (f + j) % group, block, merged)
                pieces.append(lane_shift(merged, f * bottom_width))
            strips.append(jnp.concatenate(pieces, axis=1))
        fields.append(jnp.concatenate(strips, axis=0))
    source, east_face, north_face, source_term = fields
    diagonal = level_diagonal(east_face, north_face, source_term, 1)

    iterate = jnp.zeros_like(source)
    remain = source
    direction = source
    norm_now = total(remain * remain)
    for _ in range(BOTTOM_ITERS):
        image = operator(direction, east_face, north_face, diagonal, 1)
        step_size = norm_now / total(direction * image)
        iterate = iterate + step_size * direction
        remain = remain - step_size * image
        norm_next = total(remain * remain)
        direction = remain + (norm_next / norm_now) * direction
        norm_now = norm_next

    bottom_height = lat_count * bottom_rows
    zero_tile = jnp.zeros((TILE, lon_count * bottom_width), jnp.float32)
    window_ref[pl.ds(0, TILE), :] = zero_tile
    window_ref[pl.ds(TILE, bottom_height), :] = iterate
    window_ref[pl.ds(TILE + bottom_height, TILE), :] = zero_tile
    start = pl.multiple_of(lat_index * bottom_rows, TILE)
    strip = window_ref[pl.ds(start, 3 * TILE), :]
    margin = LANES // 2 // stride
    whole_width = lon_count * bottom_width
    shift = lax.rem(margin - lon_index * bottom_width + whole_width, whole_width)
    strip = pltpu.roll(strip, shift, 1)[:, :LANES]
    south, own, north = strip[:TILE], strip[TILE : 2 * TILE], strip[2 * TILE :]
    halo_rows = HALO // stride
    row = iota((TILE, LANES), 0)
    lower = jnp.where(row < halo_rows, north, south)
    lane = iota((TILE, LANES), 1)
    parts = []
    for c in range(width // LANES):
        if c < cols // LANES:
            pick = margin + (c * LANES + lane) // stride
        else:
            pick = jnp.where(
                lane < LANES // 2, margin + bottom_width + lane // stride, (lane - LANES // 2) // stride
            )
        parts.append(jnp.concatenate(
            [jnp.take_along_axis(own, pick, axis=1), jnp.take_along_axis(lower, pick, axis=1)], axis=0
        ))
    correction = jnp.concatenate(parts, axis=1)

    for level in range(LEVELS - 1, -1, -1):
        stride = 1 << level
        east_ref, north_ref, diagonal_ref, source_ref, field_ref = level_refs[level]
        half = height >> (level + 1)
        for c in range(width // LANES):
            piece = correction[:, c * LANES : (c + 1) * LANES]
            fold_ref[c, pl.ds(0, half, stride=2), :] = piece
            fold_ref[c, pl.ds(1, half, stride=2), :] = piece
        spread = jnp.concatenate([fold_ref[c, pl.ds(0, 2 * half), :] for c in range(width // LANES)], axis=1)
        if level < LEVELS - 1:
            lanes = iota(spread.shape, 1)
            spread = jnp.where(lax.rem(lanes // stride, 2) == 0, spread, lane_shift(spread, -stride))
        east_face, north_face, diagonal = east_ref[...], north_ref[...], diagonal_ref[...]
        source = source_ref[...]
        field = field_ref[...]
        if level == 0:
            spread = mask_ref[...] * spread
        field = field + spread
        inverse = DAMPING / diagonal
        for _ in range(SWEEPS):
            field = field + inverse * (source - operator(field, east_face, north_face, diagonal, stride))
        correction = field
    solution_ref[...] = correction[:rows, :cols]
    final = source - operator(correction, east_face, north_face, diagonal, 1)
    residual_ref[...] = final[:rows, :cols]


def metric(first_row, row_count):
    row_index = first_row + jnp.arange(row_count, dtype=jnp.float32)[:, None]
    center = jnp.cos(jnp.deg2rad(BAND_SOUTH + ROW_STEP * (row_index + 0.5)))
    northern = jnp.cos(jnp.deg2rad(BAND_SOUTH + ROW_STEP * (row_index + 1.0)))
    return center, northern


def swap_pairs(count, first, periodic):
    pairs = []
    for i in range(first, count, 2):
        j = i + 1
        if j < count or periodic:
            pairs += [(i, j % count), (j % count, i)]
    return pairs


def on_device(lat_count, lon_count, forcing, surface_term, sea_cells, levels):
    rows, cols = forcing.shape
    height, width = rows + 2 * HALO, cols + LANES
    lon_index = lax.axis_index("lon").astype(jnp.int32)
    lat_index = lax.axis_index("lat").astype(jnp.int32)
    where = jnp.stack([lon_index, lat_index])
    lon_odd, lat_odd = lon_index % 2, lat_index % 2
    sea_mask = sea_cells.astype(jnp.float32)
    layers = levels.astype(jnp.float32)
    depth = sea_mask * ((layers + layers * (layers - 1.0) / 20.0) / 200.0)
    first_row = (lat_index * rows).astype(jnp.float32)
    center, _ = metric(first_row, rows)
    own = jnp.stack([depth, surface_term * center * sea_mask, forcing * sea_mask])

    edge = own[:, :, :HALO]
    blank = jnp.zeros((rows, HALO), jnp.float32)
    west_edge = jnp.concatenate([edge[0], edge[1], edge[2], blank], axis=1)
    edge = own[:, :, cols - HALO :]
    east_edge = jnp.concatenate([edge[1], edge[2], blank, edge[0]], axis=1)
    odd = lon_odd == 1
    lon_near = lax.ppermute(jnp.where(odd, west_edge, east_edge), "lon", swap_pairs(lon_count, 0, True))
    lon_far = lax.ppermute(jnp.where(odd, east_edge, west_edge), "lon", swap_pairs(lon_count, 1, True))

    wide = jnp.concatenate([own[0], own[1], own[2], lon_near, lon_far], axis=1)
    odd = lat_odd == 1
    south_edge, north_edge = wide[:HALO], wide[rows - HALO :]
    lat_near = lax.ppermute(jnp.where(odd, south_edge, north_edge), "lat", swap_pairs(lat_count, 0, False))
    lat_far = lax.ppermute(jnp.where(odd, north_edge, south_edge), "lat", swap_pairs(lat_count, 1, False))

    row = jnp.arange(height)
    row = jnp.where(row < rows + HALO, row, row - height).astype(jnp.float32)[:, None] + first_row
    wide_center = jnp.cos(jnp.deg2rad(BAND_SOUTH + ROW_STEP * (row + 0.5)))
    wide_northern = jnp.cos(jnp.deg2rad(BAND_SOUTH + ROW_STEP * (row + 1.0)))
    scale = jnp.broadcast_to(jnp.stack([1.0 / wide_center, wide_northern]), (2, height, LANES))

    smem = pl.BlockSpec(memory_space=pltpu.SMEM)
    vmem = pl.BlockSpec(memory_space=pltpu.VMEM)
    f32 = jnp.float32
    level_shapes = []
    for level in range(LEVELS):
        level_shapes += [jax.ShapeDtypeStruct((height >> level, width), f32)] * 5
    held = pl.pallas_call(
        descend,
        out_shape=[jax.ShapeDtypeStruct((TILE, LANES), f32)]
        + level_shapes
        + [jax.ShapeDtypeStruct((height, width), f32)],
        in_specs=[smem] + [vmem] * 6,
        out_specs=[vmem] * (2 + len(level_shapes)),
        scratch_shapes=[
            pltpu.VMEM((FIELDS, height, width), f32),
            pltpu.VMEM((4, width // LANES, height, LANES), f32),
        ],
        compiler_params=pltpu.CompilerParams(vmem_limit_bytes=40 * 1024 * 1024),
        name="descend",
    )(where, own, lat_near, lat_far, lon_near, lon_far, scale)
    packed, held = held[0], held[1:]

    count = lat_count * lon_count
    blocks = lax.all_to_all(
        jnp.broadcast_to(packed[None], (count, TILE, LANES)), ("lon", "lat"), 0, 0, tiled=True
    )

    return pl.pallas_call(
        functools.partial(ascend, lat_count, lon_count),
        out_shape=[jax.ShapeDtypeStruct((rows, cols), f32)] * 2,
        in_specs=[smem] + [vmem] * (1 + len(held)),
        out_specs=[vmem] * 2,
        scratch_shapes=[
            pltpu.VMEM((lat_count * (rows >> LEVELS) + 2 * TILE, lon_count * (cols >> LEVELS)), f32),
            pltpu.VMEM((width // LANES, height, LANES), f32),
        ],
        compiler_params=pltpu.CompilerParams(vmem_limit_bytes=40 * 1024 * 1024),
        name="ascend",
    )(where, blocks, *held)


def solution(mesh):
    body = functools.partial(on_device, mesh.shape["lat"], mesh.shape["lon"])
    return jax.shard_map(
        body,
        mesh=mesh,
        in_specs=(P("lat", "lon"),) * 4,
        out_specs=(P("lat", "lon"),) * 2,
        check_vma=False,
    )
```

time: 426 us -> 38.2 us (0.09); the launches traced: 421 us -> 38 us
  starting transfers between devices: 196 us -> 9.65 us
  blocking collectives: 115 us -> 13.7 us
  waiting for transfers between devices: 53.4 us -> 4.71 us
  local copies, waits for them, and re-layouts: 25.3 us -> 1.81 us
  between operations: 17.1 us -> 0.76 us
  other arithmetic: 13.8 us -> 1.34 us
  Pallas kernels: 0 us -> 5.96 us
    ppermute x80 -> x4, starting transfers between devices: 196 us -> 9.65 us  [the longest x1 6.07 us: on_device(): lax.ppermute(jnp.where(odd, east_edge, west_edge), 'lon', swap_pairs(lon_...]
    psum x11 -> x0, blocking collectives: 80.7 us -> none  [strip_total(): return lax.psum(value, 'lat')]
    ppermute x80 -> x4, waiting for transfers between devices: 53.4 us -> 4.71 us  [the longest x1 3.82 us: on_device(): lax.ppermute(jnp.where(odd, west_edge, east_edge), 'lon', swap_pairs(lon_...]
    all_gather x1 -> x0, blocking collectives: 34.8 us -> none  [on_device(): gathered = lax.all_gather(stacked, 'lon', axis=2, tiled=True)]
    slice x90 -> x0, local copies, waits for them, and re-layouts: 18.9 us -> none  [the longest x33 2.85 us: with_halo(): lax.slice_in_dim(block, block.shape[dim] - width, None, axis=dim)]
    all_to_all x0 -> x1, blocking collectives: none -> 13.7 us  [on_device(): lax.all_to_all(jnp.broadcast_to(packed[None], (count, TILE, LANES)), ('lo...]
    reduce_sum x11 -> x0, other arithmetic: 7.09 us -> none  [the longest x6 4.07 us: conjugate(): step_size = norm_now / total_fn(jnp.sum(direction * image))]
    pallas_call x0 -> x2, Pallas kernels: none -> 5.96 us  [the longest x1 3.99 us: on_device(): pl.pallas_call(functools.partial(ascend, lat_count, lon_count), out_shape...]
  transfers between devices with their start and end apart: 80 -> 4, of which waited for: 34 -> 2; matrix products, arithmetic and copies ran while one was open for 4% -> 0% of each run, Pallas kernels for 0% -> 0%
where the time goes in v1:
time: 38.2 us; the launch traced here: 38 us
  blocking collectives  13.7 us (36%)
  starting transfers between devices  9.65 us (25%)
  Pallas kernels  5.96 us (16%)
  waiting for transfers between devices  4.71 us (12%)
  local copies, waits for them, and re-layouts  1.81 us (5%)
  other arithmetic  1.34 us (4%)
  between operations  0.76 us (2%)
    all_to_all x1, blocking collectives, on_device(): lax.all_to_all(jnp.broadcast_to(packed[None], (count, TILE, LANES)), ('lo...  13.7 us
    ppermute x1, starting transfers between devices, on_device(): lax.ppermute(jnp.where(odd, east_edge, west_edge), 'lon', swap_pairs(lon_...  6.07 us
    pallas_call x1, Pallas kernels, on_device(): pl.pallas_call(functools.partial(ascend, lat_count, lon_count), out_shape...  3.99 us
    ppermute x1, waiting for transfers between devices, on_device(): lax.ppermute(jnp.where(odd, west_edge, east_edge), 'lon', swap_pairs(lon_...  3.82 us
    ppermute x1, starting transfers between devices, on_device(): lax.ppermute(jnp.where(odd, south_edge, north_edge), 'lat', swap_pairs(la...  2.91 us
    pallas_call x1, Pallas kernels, on_device(): pl.pallas_call(descend, out_shape=[jax.ShapeDtypeStruct((TILE, LANES), f3...  1.97 us
    unnamed x7, local copies, waits for them, and re-layouts  1.54 us
    unnamed x3, other arithmetic  0.99 us
  transfers between devices with their start and end apart: 4, of which 2 were waited for; matrix products, arithmetic and copies ran while one was open for 0% of the time, Pallas kernels for 0%

profile of v1, /device:TPU:0, one launch (start us, length us, event | category | flops | bytes accessed | tf_op | source)
XLA Modules:
  0.0 38.0 jit_solution(5741268744042117683)
XLA Ops:
  0.6 0.1 multiply_cosine_fusion.1
  0.7 0.9 %constant_dynamic-update-slice_fusion.3 = (f32[64,1024]{1,0:T(8,128)S(1)}, f32[1,64,256]{2,1,0:T(8,128)S(1)}) fusion(s32[64,256]{1,0:T(8,128)} %param.7, s32[64,256]{1,0:T(8,128)} %param.6), kind=kLoop, calls=%fused_computation.25 | loop fusion | flops 131071 | bytes 262144
  1.6 0.0 copy-start
  1.6 0.0 copy-start.1
  1.6 0.1 slice_bitcast_fusion.5
  1.7 0.7 %copy-done = s32[64,256]{1,0:T(8,128)S(1)} copy-done((s32[64,256]{1,0:T(8,128)S(1)}, s32[64,256]{1,0:T(8,128)}, u32[]{:S(2)}) %copy-start) | copy-done | bytes 65560
  2.4 0.0 copy-done.1
  2.5 0.1 constant_dynamic-update-slice_fusion.2
  2.6 0.8 %copy-done.2 = f32[64,256]{1,0:T(8,128)S(1)} copy-done((f32[64,256]{1,0:T(8,128)S(1)}, f32[64,256]{1,0:T(8,128)}, u32[]{:S(2)}) %copy-start.2) | copy-done | bytes 65560
  3.3 0.1 slice_bitcast_fusion.3
  3.4 0.1 broadcast_select_fusion
  3.5 6.1 %collective-permute-start.1 = (f32[64,128]{1,0:T(8,128)S(1)}, f32[64,128]{1,0:T(8,128)S(1)}, u32[]{:S(2)}, u32[]{:S(2)}) collective-permute-start(f32[64,128]{1,0:T(8,128)S(1)} %get-tuple-element.38), channel_id=1, source_target_pairs={{4,8},{8,4},{12,16},{16,12},{20,24},{24,20},{28,0},{0,28},{5,9},{9... | collective-permute-start | bytes 98312 | tf_op jit(solution)/shard_map/ppermute | solution.py:303
  9.6 0.0 collective-permute-start
  9.6 0.1 multiply_cosine_fusion
  9.7 3.8 %collective-permute-done.lon_near_ref = f32[64,128]{1,0:T(8,128)S(1)} collective-permute-done((f32[64,128]{1,0:T(8,128)S(1)}, f32[64,128]{1,0:T(8,128)S(1)}, u32[]{:S(2)}, u32[]{:S(2)}) %collective-permute-start) | collective-permute-done | bytes 32800 | tf_op jit(solution)/shard_map/ppermute | solution.py:302
  13.5 0.0 collective-permute-done.1.lon_far_ref
  13.6 0.7 %collective-permute-start.3 = (f32[32,1024]{1,0:T(8,128)S(1)}, f32[32,1024]{1,0:T(8,128)S(1)}, u32[]{:S(2)}, u32[]{:S(2)}) collective-permute-start(f32[32,1024]{1,0:T(8,128)S(1)} %get-tuple-element.36), channel_id=1, source_target_pairs={{1,2},{2,1},{5,6},{6,5},{9,10},{10,9},{13,14},{14,13},{17,18},{18,... | collective-permute-start | bytes 393224 | tf_op jit(solution)/shard_map/ppermute | solution.py:309
  14.3 2.9 %collective-permute-start.2 = (f32[32,1024]{1,0:T(8,128)S(1)}, f32[32,1024]{1,0:T(8,128)S(1)}, u32[]{:S(2)}, u32[]{:S(2)}) collective-permute-start(f32[32,1024]{1,0:T(8,128)S(1)} %get-tuple-element.37), channel_id=1, source_target_pairs={{0,1},{1,0},{2,3},{3,2},{4,5},{5,4},{6,7},{7,6},{8,9},{9,8},{10,11... | collective-permute-start | bytes 393224 | tf_op jit(solution)/shard_map/ppermute | solution.py:308
  17.2 0.1 pad_add_fusion.where_ref
  17.3 0.9 %collective-permute-done.2.lat_near_ref = f32[32,1024]{1,0:T(8,128)S(1)} collective-permute-done((f32[32,1024]{1,0:T(8,128)S(1)}, f32[32,1024]{1,0:T(8,128)S(1)}, u32[]{:S(2)}, u32[]{:S(2)}) %collective-permute-start.2) | collective-permute-done | bytes 131104 | tf_op jit(solution)/shard_map/ppermute | solution.py:308
  18.2 0.1 broadcast_in_dim.20.scale_ref
  18.2 2.0 %descend.1 = (f32[8,128]{1,0:T(8,128)S(1)}, f32[128,384]{1,0:T(8,128)S(1)}, f32[128,384]{1,0:T(8,128)S(1)}, f32[128,384]{1,0:T(8,128)S(1)}, f32[128,384]{1,0:T(8...) custom-call(s32[2]{0:T(128)S(1)} %pad_add_fusion.where_ref, ...), custom_call_target="tpu_custom_call" | custom-call | tf_op jit(solution)/shard_map/descend/pallas_call | solution.py:323
  20.2 13.7 %all_to_all.5.blocks_ref = f32[32,8,128]{2,1,0:T(8,128)S(1)} all-to-all(f32[32,8,128]{2,1,0:T(8,128)S(1)} %broadcast_in_dim.21), channel_id=1, replica_groups=mesh['lon'=8,'lat'=4] {'lon','lat'}, dimensions={0} | all-to-all | bytes 262144 | tf_op jit(solution)/shard_map/all_to_all | solution.py:340
  34.0 4.0 %ascend.1 = (f32[64,256]{1,0:T(8,128)}, f32[64,256]{1,0:T(8,128)}) custom-call(s32[2]{0:T(128)S(1)} %pad_add_fusion.where_ref, f32[32,8,128]{2,1,0:T(8,128)S(1)} %all_to_all.5.blocks_ref, f32[128,384]{1,0:T(8,128)S(1)} %get-tuple-element.20.rest_0_, f32[128,384]{1,0:T(8,128)S(1)} %get-tuple-element.21.rest_1_, f32[128,384]{1,0:T(8,128)S(1)} %get-tuple-element.22.rest_2_, ...), custom_call_target="tpu_custom_call" | custom-call | tf_op jit(solution)/shard_map/ascend/pallas_call | solution.py:344
  (10 shorter events, 0.1 us)
Async XLA Ops:
  1.6 0.8 %copy-start = (s32[64,256]{1,0:T(8,128)S(1)}, s32[64,256]{1,0:T(8,128)}, u32[]{:S(2)}) copy-start(s32[64,256]{1,0:T(8,128)} %param.6) | copy-start | bytes 196612
  1.6 0.9 %copy-start.1 = (f32[64,256]{1,0:T(8,128)S(1)}, f32[64,256]{1,0:T(8,128)}, u32[]{:S(2)}) copy-start(f32[64,256]{1,0:T(8,128)} %param.5) | copy-start | bytes 196612
  2.5 0.8 %copy-start.2 = (f32[64,256]{1,0:T(8,128)S(1)}, f32[64,256]{1,0:T(8,128)}, u32[]{:S(2)}) copy-start(f32[64,256]{1,0:T(8,128)} %param.4) | copy-start | bytes 196612
  3.5 10.0 %collective-permute-start.1 = (f32[64,128]{1,0:T(8,128)S(1)}, f32[64,128]{1,0:T(8,128)S(1)}, u32[]{:S(2)}, u32[]{:S(2)}) collective-permute-start(f32[64,128]{1,0:T(8,128)S(1)} %get-tuple-element.38), channel_id=1, source_target_pairs={{4,8},{8,4},{12,16},{16,12},{20,24},{24,20},{28,0},{0,28},{5,9},{9... | collective-permute-start | bytes 98312 | tf_op jit(solution)/shard_map/ppermute | solution.py:303
  9.6 3.9 %collective-permute-start = (f32[64,128]{1,0:T(8,128)S(1)}, f32[64,128]{1,0:T(8,128)S(1)}, u32[]{:S(2)}, u32[]{:S(2)}) collective-permute-start(f32[64,128]{1,0:T(8,128)S(1)} %get-tuple-element.39), channel_id=1, source_target_pairs={{0,4},{4,0},{8,12},{12,8},{16,20},{20,16},{24,28},{28,24},{1,5},{5... | collective-permute-start | bytes 98312 | tf_op jit(solution)/shard_map/ppermute | solution.py:302
  13.6 3.7 %collective-permute-start.3 = (f32[32,1024]{1,0:T(8,128)S(1)}, f32[32,1024]{1,0:T(8,128)S(1)}, u32[]{:S(2)}, u32[]{:S(2)}) collective-permute-start(f32[32,1024]{1,0:T(8,128)S(1)} %get-tuple-element.36), channel_id=1, source_target_pairs={{1,2},{2,1},{5,6},{6,5},{9,10},{10,9},{13,14},{14,13},{17,18},{18,... | collective-permute-start | bytes 393224 | tf_op jit(solution)/shard_map/ppermute | solution.py:309
  14.3 3.9 %collective-permute-start.2 = (f32[32,1024]{1,0:T(8,128)S(1)}, f32[32,1024]{1,0:T(8,128)S(1)}, u32[]{:S(2)}, u32[]{:S(2)}) collective-permute-start(f32[32,1024]{1,0:T(8,128)S(1)} %get-tuple-element.37), channel_id=1, source_target_pairs={{0,1},{1,0},{2,3},{3,2},{4,5},{5,4},{6,7},{7,6},{8,9},{9,8},{10,11... | collective-permute-start | bytes 393224 | tf_op jit(solution)/shard_map/ppermute | solution.py:308

commit v2 on v1

v2 whole, which is shorter than its diff:
```python
import functools

import jax
import jax.numpy as jnp
from jax import lax
from jax.experimental import pallas as pl
from jax.experimental.pallas import tpu as pltpu
from jax.sharding import PartitionSpec as P

LEVELS = 3
SWEEPS = 2
BOTTOM_ITERS = 6

DAMPING = 0.8
ROW_STEP = 150.0 / 8640.0
BAND_SOUTH = -50.0

HALO = 32
LANES = 128
TILE = 8
FIELDS = 3
VMEM_LIMIT = 40 * 1024 * 1024


def iota(shape, dim):
    return lax.broadcasted_iota(jnp.int32, shape, dim)


def lane_shift(field, count):
    return pltpu.roll(field, (-count) % field.shape[1], 1)


def north_of(tiles, t):
    if t + 1 < len(tiles):
        return tiles[t + 1]
    return pltpu.roll(tiles[0], TILE - 1, 0)


def south_of(tiles, t):
    if t > 0:
        return tiles[t - 1]
    return pltpu.roll(tiles[-1], 1, 0)


def neighbour_sum(field, east_face, north_face, stride):
    upward = [north_face[t] * field[t] for t in range(len(field))]
    return [
        (east_face[t] * lane_shift(field[t], stride) + lane_shift(east_face[t] * field[t], -stride))
        + (north_face[t] * north_of(field, t) + south_of(upward, t))
        for t in range(len(field))
    ]


def sweep(field, source, inverse, east_face, north_face, stride):
    around = neighbour_sum(field, east_face, north_face, stride)
    return [
        (1.0 - DAMPING) * field[t] + inverse[t] * (source[t] + around[t]) for t in range(len(field))
    ]


def remainder(field, source, diagonal, east_face, north_face, stride):
    around = neighbour_sum(field, east_face, north_face, stride)
    return [source[t] - diagonal[t] * field[t] + around[t] for t in range(len(field))]


def tiles_of(ref):
    return [ref[t] for t in range(ref.shape[0])]


def keep(ref, tiles):
    for t, value in enumerate(tiles):
        ref[t] = value


def prepare(where_ref, forcing_ref, surface_ref, sea_ref, levels_ref,
            own_ref, lon_near_ref, lon_far_ref, lat_near_ref, lat_far_ref, scale_ref,
            forcing_buf, surface_buf, sea_buf, levels_buf, sems):
    copies = [
        pltpu.make_async_copy(source, target, sems.at[i])
        for i, (source, target) in enumerate((
            (levels_ref, levels_buf), (sea_ref, sea_buf), (surface_ref, surface_buf), (forcing_ref, forcing_buf),
        ))
    ]
    for copy in copies:
        copy.start()
    rows, cols = forcing_buf.shape
    lon_odd = lax.rem(where_ref[0], 2)
    lat_odd = lax.rem(where_ref[1], 2)
    first_row = where_ref[1] * rows
    count = scale_ref.shape[1]
    height = count * TILE
    for t in range(count):
        row = iota((TILE, LANES), 0) * count + t
        row = jnp.where(row < rows + HALO, row, row - height) + first_row
        row = row.astype(jnp.float32)
        scale_ref[0, t] = 1.0 / jnp.cos(jnp.deg2rad(BAND_SOUTH + ROW_STEP * (row + 0.5)))
        scale_ref[1, t] = jnp.cos(jnp.deg2rad(BAND_SOUTH + ROW_STEP * (row + 1.0)))
    row = (iota((rows, LANES), 0) + first_row).astype(jnp.float32)
    center = jnp.cos(jnp.deg2rad(BAND_SOUTH + ROW_STEP * (row + 0.5)))
    center = jnp.concatenate([center] * (cols // LANES), axis=1)
    for copy in copies:
        copy.wait()
    sea_mask = sea_buf[...].astype(jnp.float32)
    layers = levels_buf[...].astype(jnp.float32)
    depth = sea_mask * ((layers + layers * (layers - 1.0) / 20.0) / 200.0)
    fields = (depth, surface_buf[...] * center * sea_mask, forcing_buf[...] * sea_mask)
    slot = iota((rows, LANES), 1) // HALO
    last = LANES // HALO - 1
    west_edge = jnp.zeros((rows, LANES), jnp.float32)
    east_edge = jnp.zeros((rows, LANES), jnp.float32)
    for f, value in enumerate(fields):
        own_ref[f] = value
        west_edge = jnp.where(slot == f, lane_shift(value[:, :LANES], -f * HALO), west_edge)
        east_edge = jnp.where(
            slot == (f + last) % (last + 1), lane_shift(value[:, cols - LANES :], -f * HALO), east_edge
        )
    odd = jnp.broadcast_to(lon_odd, (rows, LANES)) > 0
    lon_near_ref[...] = jnp.where(odd, west_edge, east_edge)
    lon_far_ref[...] = jnp.where(odd, east_edge, west_edge)
    odd = jnp.broadcast_to(lat_odd, (HALO, cols)) > 0
    for f, value in enumerate(fields):
        south_edge, north_edge = value[:HALO], value[rows - HALO :]
        part = slice(f * cols, (f + 1) * cols)
        lat_near_ref[:, part] = jnp.where(odd, south_edge, north_edge)
        lat_far_ref[:, part] = jnp.where(odd, north_edge, south_edge)


def descend(where_ref, own_ref, lon_near_ref, lon_far_ref, lat_near_ref, lat_far_ref,
            corner_near_ref, corner_far_ref, scale_ref, pack_ref, *rest):
    level_refs = [rest[5 * i : 5 * i + 5] for i in range(LEVELS)]
    diagonal_ref, grid_ref = rest[5 * LEVELS :]
    lon_index = where_ref[0]
    lon_odd = lax.rem(lon_index, 2)
    lat_odd = lax.rem(where_ref[1], 2)
    rows, cols = own_ref.shape[1], own_ref.shape[2]
    count, width = diagonal_ref.shape[0], diagonal_ref.shape[2]
    own_columns = cols // LANES
    columns = width // LANES
    near_row = rows + pl.multiple_of(lat_odd * HALO, HALO)
    far_row = rows + pl.multiple_of((1 - lat_odd) * HALO, HALO)
    last = LANES // HALO - 1
    parts = (
        (0, lon_near_ref[...], lon_far_ref[...], [own_ref.at[f] for f in range(FIELDS)]),
        (near_row, corner_near_ref[:, :LANES], corner_near_ref[:, LANES:],
         [lat_near_ref.at[:, pl.ds(f * cols, cols)] for f in range(FIELDS)]),
        (far_row, corner_far_ref[:, :LANES], corner_far_ref[:, LANES:],
         [lat_far_ref.at[:, pl.ds(f * cols, cols)] for f in range(FIELDS)]),
    )
    for first, near_val, far_val, bodies in parts:
        size = near_val.shape[0]
        odd = jnp.broadcast_to(lon_odd, near_val.shape) > 0
        east_val = jnp.where(odd, far_val, near_val)
        west_val = jnp.where(odd, near_val, far_val)
        slot = iota(near_val.shape, 1) // HALO
        for f, body in enumerate(bodies):
            both = jnp.where(
                slot == f, east_val, jnp.where(slot == (f + last) % (last + 1), west_val, 0.0)
            )
            for c in range(own_columns):
                grid_ref[f, c, pl.ds(first, size), :] = body[:, c * LANES : (c + 1) * LANES]
            grid_ref[f, own_columns, pl.ds(first, size), :] = lane_shift(both, f * HALO)

    def load(f):
        return [
            jnp.concatenate(
                [grid_ref[f, c, pl.ds(t, TILE, stride=count), :] for c in range(columns)], axis=1
            )
            for t in range(count)
        ]

    depth = load(0)
    source_term = load(1)
    source = load(2)
    across = [jnp.concatenate([scale_ref[0, t]] * columns, axis=1) for t in range(count)]
    along = [jnp.concatenate([scale_ref[1, t]] * columns, axis=1) for t in range(count)]
    east_face = [jnp.minimum(depth[t], lane_shift(depth[t], 1)) * across[t] for t in range(count)]
    north_face = [jnp.minimum(depth[t], north_of(depth, t)) * along[t] for t in range(count)]
    for level in range(LEVELS):
        stride = 1 << level
        inverse, diagonal = [], []
        for t in range(count >> level):
            total = source_term[t] + (
                (east_face[t] + lane_shift(east_face[t], -stride))
                + (north_face[t] + south_of(north_face, t))
            )
            diagonal.append(jnp.where(source_term[t] > 0.0, total, 1.0))
            inverse.append(DAMPING / diagonal[t])
        field = [inverse[t] * source[t] for t in range(count >> level)]
        for _ in range(SWEEPS - 1):
            field = sweep(field, source, inverse, east_face, north_face, stride)
        image = remainder(field, source, diagonal, east_face, north_face, stride)
        for ref, value in zip(level_refs[level], (east_face, north_face, inverse, source, field)):
            keep(ref, value)
        if level == 0:
            keep(diagonal_ref, diagonal)

        def coarse(tiles):
            sums = [tiles[t] + tiles[t + 1] for t in range(0, len(tiles), 2)]
            return [value + lane_shift(value, stride) for value in sums]

        east_face = [
            lane_shift(east_face[t] + east_face[t + 1], stride) for t in range(0, len(east_face), 2)
        ]
        north_face = [
            north_face[t] + lane_shift(north_face[t], stride) for t in range(1, len(north_face), 2)
        ]
        source_term = coarse(source_term)
        source = coarse(image)

    stride = 1 << LEVELS
    bottom_width = cols // stride
    group = LANES // bottom_width
    per_column = LANES // stride
    tiles = len(source)
    lane = iota((TILE, LANES), 1)
    cell = lane % bottom_width
    pick = (cell % per_column) * stride
    turn = lax.rem(lane // bottom_width + group - lax.rem(lon_index, group), group)
    for t in range(tiles):
        packed = jnp.zeros((TILE, LANES), jnp.float32)
        for f, value in enumerate((source[t], east_face[t], north_face[t], source_term[t])):
            flat = jnp.zeros((TILE, LANES), jnp.float32)
            for c in range(own_columns):
                taken = jnp.take_along_axis(value[:, c * LANES : (c + 1) * LANES], pick, axis=1)
                flat = jnp.where(cell // per_column == c, taken, flat)
            packed = jnp.where(turn == f, flat, packed)
        own_rows = pack_ref.shape[0] // tiles
        pack_ref[pl.ds(t, own_rows, stride=tiles), :] = packed[:own_rows]


def total_of(tiles):
    parts = list(tiles)
    while len(parts) > 1:
        parts = [
            parts[i] + parts[i + 1] if i + 1 < len(parts) else parts[i] for i in range(0, len(parts), 2)
        ]
    value = parts[0]
    value = sum(value[:, c : c + LANES] for c in range(0, value.shape[1], LANES))
    return jnp.sum(jnp.sum(value, axis=0, keepdims=True), axis=1, keepdims=True)


def conjugate(source, east_face, north_face, source_term):
    height = source.shape[0]

    def split(value):
        return [value[r : r + TILE] for r in range(0, height, TILE)]

    def up(value):
        return pltpu.roll(value, height - 1, 0)

    def down(value):
        return pltpu.roll(value, 1, 0)

    diagonal = source_term + (
        (east_face + lane_shift(east_face, -1)) + (north_face + down(north_face))
    )
    iterate = jnp.zeros_like(source)
    remain = source
    direction = source
    for _ in range(BOTTOM_ITERS):
        image = diagonal * direction - (
            (east_face * lane_shift(direction, 1) + lane_shift(east_face * direction, -1))
            + (north_face * up(direction) + down(north_face * direction))
        )
        norm = total_of(split(remain * remain))
        energy = total_of(split(direction * image))
        cross = total_of(split(remain * image))
        square = total_of(split(image * image))
        step_size = norm / energy
        iterate = iterate + step_size * direction
        remain = remain - step_size * image
        norm_next = norm - step_size * (2.0 * cross - step_size * square)
        direction = remain + (norm_next / norm) * direction
    return iterate


def ascend(lat_count, lon_count, where_ref, blocks_ref, *rest):
    level_refs = [rest[5 * i : 5 * i + 5] for i in range(LEVELS)]
    diagonal_ref, solution_ref, residual_ref, window_ref, turn_ref, order_ref = rest[5 * LEVELS :]
    lon_index = where_ref[0]
    lat_index = where_ref[1]
    rows, cols = solution_ref.shape
    count, width = diagonal_ref.shape[0], diagonal_ref.shape[2]
    own_columns = cols // LANES
    columns = width // LANES
    stride = 1 << LEVELS
    bottom_rows = rows // stride
    bottom_width = cols // stride
    group = LANES // bottom_width
    slot = iota((bottom_rows, LANES), 1) // bottom_width
    fields = []
    for f in range(4):
        strips = []
        for a in range(lat_count):
            pieces = []
            for c in range(lon_count // group):
                merged = None
                for j in range(group):
                    block = blocks_ref[(c * group + j) * lat_count + a]
                    merged = block if merged is None else jnp.where(slot == (f + j) % group, block, merged)
                pieces.append(lane_shift(merged, f * bottom_width))
            strips.append(jnp.concatenate(pieces, axis=1))
        fields.append(jnp.concatenate(strips, axis=0))
    iterate = conjugate(*fields)

    bottom_height = lat_count * bottom_rows
    whole_width = lon_count * bottom_width
    pad = 2 * TILE
    window_ref[pl.ds(0, pad), :] = jnp.zeros((pad, LANES), jnp.float32)
    window_ref[pl.ds(pad + bottom_height, pad), :] = jnp.zeros((pad, LANES), jnp.float32)
    margin = LANES // 2 // stride
    shift = lax.rem(margin - lon_index * bottom_width + whole_width, whole_width)
    window_ref[pl.ds(pad, bottom_height), :] = pltpu.roll(iterate, shift, 1)[:, :LANES]
    start = pl.multiple_of(lat_index * bottom_rows, TILE)
    strip = window_ref[pl.ds(start, 5 * TILE), :]
    turn_ref[...] = strip
    tiles = count >> LEVELS
    sublane = iota((TILE, LANES), 0)
    ahead = (rows + HALO) // stride // tiles
    lane = iota((TILE, LANES), 1)
    correction = []
    for t in range(tiles):
        upper = turn_ref[pl.ds(pad + t, TILE, stride=tiles), :]
        lower = turn_ref[pl.ds(pad + t - tiles * TILE, TILE, stride=tiles), :]
        value = jnp.where(sublane < ahead, upper, lower)
        parts = []
        for c in range(columns):
            if c < own_columns:
                pick = margin + (c * LANES + lane) // stride
            else:
                pick = jnp.where(
                    lane < LANES // 2, margin + bottom_width + lane // stride, (lane - LANES // 2) // stride
                )
            parts.append(jnp.take_along_axis(value, pick, axis=1))
        correction.append(jnp.concatenate(parts, axis=1))

    lane = iota((TILE, width), 1)
    for level in range(LEVELS - 1, -1, -1):
        stride = 1 << level
        east_face, north_face, inverse, source, field = map(tiles_of, level_refs[level])
        if level < LEVELS - 1:
            first = lax.rem(lane // stride, 2) == 0
            correction = [jnp.where(first, value, lane_shift(value, -stride)) for value in correction]
        spread = [correction[t // 2] for t in range(count >> level)]
        if level == 0:
            sea = [east_face[t] + north_face[t] > 0.0 for t in range(count)]
            spread = [jnp.where(sea[t], spread[t], 0.0) for t in range(count)]
        field = [field[t] + spread[t] for t in range(count >> level)]
        for _ in range(SWEEPS):
            field = sweep(field, source, inverse, east_face, north_face, stride)
        correction = field
    final = remainder(correction, source, tiles_of(diagonal_ref), east_face, north_face, 1)
    own_sublanes = rows // count
    for k, (ref, value) in enumerate(((solution_ref, correction), (residual_ref, final))):
        for c in range(own_columns):
            part = slice(c * LANES, (c + 1) * LANES)
            for t in range(count):
                order_ref[k, c, pl.ds(t, own_sublanes, stride=count), :] = value[t][:own_sublanes, part]
            ref[:, part] = order_ref[k, c]


def swap_pairs(count, first, periodic):
    pairs = []
    for i in range(first, count, 2):
        j = i + 1
        if j < count or periodic:
            pairs += [(i, j % count), (j % count, i)]
    return pairs


def on_device(lat_count, lon_count, forcing, surface_term, sea_cells, levels):
    rows, cols = forcing.shape
    height, width = rows + 2 * HALO, cols + LANES
    count = height // TILE
    f32 = jnp.float32
    smem = pl.BlockSpec(memory_space=pltpu.SMEM)
    vmem = pl.BlockSpec(memory_space=pltpu.VMEM)
    hbm = pl.BlockSpec(memory_space=pltpu.HBM)
    params = pltpu.CompilerParams(vmem_limit_bytes=VMEM_LIMIT)
    lon_index = lax.axis_index("lon").astype(jnp.int32)
    lat_index = lax.axis_index("lat").astype(jnp.int32)
    where = jnp.stack([lon_index, lat_index])

    own, lon_near, lon_far, lat_near, lat_far, scale = pl.pallas_call(
        prepare,
        out_shape=[
            jax.ShapeDtypeStruct((FIELDS, rows, cols), f32),
            jax.ShapeDtypeStruct((rows, LANES), f32),
            jax.ShapeDtypeStruct((rows, LANES), f32),
            jax.ShapeDtypeStruct((HALO, FIELDS * cols), f32),
            jax.ShapeDtypeStruct((HALO, FIELDS * cols), f32),
            jax.ShapeDtypeStruct((2, count, TILE, LANES), f32),
        ],
        in_specs=[smem] + [hbm] * 4,
        out_specs=[vmem] * 6,
        scratch_shapes=[
            pltpu.VMEM((rows, cols), f32),
            pltpu.VMEM((rows, cols), f32),
            pltpu.VMEM((rows, cols), jnp.int32),
            pltpu.VMEM((rows, cols), jnp.int32),
            pltpu.SemaphoreType.DMA((4,)),
        ],
        compiler_params=params,
        name="prepare",
    )(where, *(pltpu.with_memory_space_constraint(x, pltpu.HBM) for x in (forcing, surface_term, sea_cells, levels)))

    far_pairs, near_pairs = swap_pairs(lon_count, 1, True), swap_pairs(lon_count, 0, True)
    north_pairs, south_pairs = swap_pairs(lat_count, 0, False), swap_pairs(lat_count, 1, False)
    lon_far = lax.ppermute(lon_far, "lon", far_pairs)
    lon_near = lax.ppermute(lon_near, "lon", near_pairs)
    lat_far = lax.ppermute(lat_far, "lat", south_pairs)
    lat_near = lax.ppermute(lat_near, "lat", north_pairs)
    sides = jnp.concatenate([lon_near, lon_far], axis=1)
    odd = lat_index % 2 == 1
    south_edge, north_edge = sides[:HALO], sides[rows - HALO :]
    corner_far = lax.ppermute(jnp.where(odd, north_edge, south_edge), "lat", south_pairs)
    corner_near = lax.ppermute(jnp.where(odd, south_edge, north_edge), "lat", north_pairs)

    level_shapes = []
    for level in range(LEVELS):
        level_shapes += [jax.ShapeDtypeStruct((count >> level, TILE, width), f32)] * 5
    held = pl.pallas_call(
        descend,
        out_shape=[jax.ShapeDtypeStruct((rows >> LEVELS, LANES), f32)]
        + level_shapes
        + [jax.ShapeDtypeStruct((count, TILE, width), f32)],
        in_specs=[smem] + [vmem] * 8,
        out_specs=[vmem] * (2 + len(level_shapes)),
        scratch_shapes=[pltpu.VMEM((FIELDS, width // LANES, height, LANES), f32)],
        compiler_params=params,
        name="descend",
    )(where, own, lon_near, lon_far, lat_near, lat_far, corner_near, corner_far, scale)
    packed, held = held[0], held[1:]

    blocks = lax.all_to_all(
        jnp.broadcast_to(packed[None], (lat_count * lon_count,) + packed.shape), ("lon", "lat"), 0, 0, tiled=True
    )

    return pl.pallas_call(
        functools.partial(ascend, lat_count, lon_count),
        out_shape=[jax.ShapeDtypeStruct((rows, cols), f32)] * 2,
        in_specs=[smem] + [vmem] * (1 + len(held)),
        out_specs=[vmem] * 2,
        scratch_shapes=[
            pltpu.VMEM((lat_count * (rows >> LEVELS) + 4 * TILE, LANES), f32),
            pltpu.VMEM((5 * TILE, LANES), f32),
            pltpu.VMEM((2, cols // LANES, rows, LANES), f32),
        ],
        compiler_params=params,
        name="ascend",
    )(where, blocks, *held)


def solution(mesh):
    body = functools.partial(on_device, mesh.shape["lat"], mesh.shape["lon"])
    return jax.shard_map(
        body,
        mesh=mesh,
        in_specs=(P("lat", "lon"),) * 4,
        out_specs=(P("lat", "lon"),) * 2,
        check_vma=False,
    )
```

time: 38.2 us -> 35.9 us (0.940)
  local copies, waits for them, and re-layouts: 1.81 us -> 0.02 us
  waiting for transfers between devices: 4.71 us -> 3.23 us
  other arithmetic: 1.34 us -> 0.09 us
  Pallas kernels: 5.96 us -> 7.14 us
  starting transfers between devices: 9.65 us -> 10.8 us
    pallas_call x1 -> x2, Pallas kernels: 1.97 us -> 3.52 us  [the longest x1 1.91 us: on_device(): pl.pallas_call(descend, out_shape=[jax.ShapeDtypeStruct((rows >> LEVELS,...]
    unnamed x7 -> x1, local copies, waits for them, and re-layouts: 1.54 us -> 0.01 us
    ppermute x4 -> x6, waiting for transfers between devices: 4.71 us -> 3.23 us  [the longest x1 2.37 us: on_device(): lon_far = lax.ppermute(lon_far, 'lon', far_pairs)]
    ppermute x4 -> x6, starting transfers between devices: 9.65 us -> 10.8 us  [the longest x1 3.54 us: on_device(): lon_far = lax.ppermute(lon_far, 'lon', far_pairs)]
    unnamed x3 -> x0, other arithmetic: 0.99 us -> none
  transfers between devices with their start and end apart: 4 -> 6, of which waited for: 2 -> 2; matrix products, arithmetic and copies ran while one was open for 0% -> 0% of each run, Pallas kernels for 0% -> 0%
where the time goes in v2:
time: 35.9 us; the launch traced here: 35.7 us
  blocking collectives  13.7 us (38%)
  starting transfers between devices  10.8 us (30%)
  Pallas kernels  7.14 us (20%)
  waiting for transfers between devices  3.23 us (9%)
  between operations  0.7 us (2%)
    all_to_all x1, blocking collectives, on_device(): lax.all_to_all(jnp.broadcast_to(packed[None], (lat_count * lon_count,) +...  13.7 us
    pallas_call x1, Pallas kernels, on_device(): pl.pallas_call(functools.partial(ascend, lat_count, lon_count), out_shape...  3.62 us
    ppermute x1, starting transfers between devices, on_device(): lon_far = lax.ppermute(lon_far, 'lon', far_pairs)  3.54 us
    ppermute x1, starting transfers between devices, on_device(): lon_near = lax.ppermute(lon_near, 'lon', near_pairs)  3.03 us
    ppermute x1, starting transfers between devices, on_device(): lax.ppermute(jnp.where(odd, south_edge, north_edge), 'lat', north_pairs)  2.92 us
    ppermute x1, waiting for transfers between devices, on_device(): lon_far = lax.ppermute(lon_far, 'lon', far_pairs)  2.37 us
    pallas_call x1, Pallas kernels, on_device(): pl.pallas_call(descend, out_shape=[jax.ShapeDtypeStruct((rows >> LEVELS,...  1.91 us
    pallas_call x1, Pallas kernels, on_device(): pl.pallas_call(prepare, out_shape=[jax.ShapeDtypeStruct((FIELDS, rows, co...  1.61 us
  transfers between devices with their start and end apart: 6, of which 2 were waited for; matrix products, arithmetic and copies ran while one was open for 0% of the time, Pallas kernels for 0%

profile of v2, /device:TPU:0, one launch (start us, length us, event | category | flops | bytes accessed | tf_op | source)
XLA Modules:
  0.0 35.7 jit_solution(8788607254910723320)
XLA Ops:
  0.6 0.1 pad_add_fusion.where_ref
  0.7 1.6 %prepare.1 = (f32[3,64,256]{2,1,0:T(8,128)S(1)}, f32[64,128]{1,0:T(8,128)S(1)}, f32[64,128]{1,0:T(8,128)S(1)}, f32[32,768]{1,0:T(8,128)S(1)}, f32[32,768]{1,0:T(8,128)S(1)}, /*index=5*/f32[2,16,8,128]{3,2,1,0:T(8,128)S(1)}) custom-call(s32[2]{0:T(128)S(1)} %pad_add_fusion.where_ref, f32[64,256]{1,0:T(8,128)} %forcing_ref.1, f32[64,256]{1,0:T(8,128)} %surface_ref.1, ...), custom_call_target="tpu_custom_call" | custom-call | tf_op jit(solution)/shard_map/prepare/pallas_call | solution.py:384
  2.3 3.0 %collective-permute-start = (f32[64,128]{1,0:T(8,128)S(1)}, f32[64,128]{1,0:T(8,128)S(1)}, u32[]{:S(2)}, u32[]{:S(2)}) collective-permute-start(f32[64,128]{1,0:T(8,128)S(1)} %get-tuple-element.26), channel_id=1, source_target_pairs={{0,4},{4,0},{8,12},{12,8},{16,20},{20,16},{24,28},{28,24},{1,5},{5... | collective-permute-start | bytes 98312 | tf_op jit(solution)/shard_map/ppermute | solution.py:410
  5.4 3.5 %collective-permute-start.1 = (f32[64,128]{1,0:T(8,128)S(1)}, f32[64,128]{1,0:T(8,128)S(1)}, u32[]{:S(2)}, u32[]{:S(2)}) collective-permute-start(f32[64,128]{1,0:T(8,128)S(1)} %get-tuple-element.27), channel_id=1, source_target_pairs={{4,8},{8,4},{12,16},{16,12},{20,24},{24,20},{28,0},{0,28},{5,9},{9... | collective-permute-start | bytes 98312 | tf_op jit(solution)/shard_map/ppermute | solution.py:409
  8.9 0.0 collective-permute-start.2
  8.9 0.7 %collective-permute-start.3 = (f32[32,768]{1,0:T(8,128)S(1)}, f32[32,768]{1,0:T(8,128)S(1)}, u32[]{:S(2)}, u32[]{:S(2)}) collective-permute-start(f32[32,768]{1,0:T(8,128)S(1)} %get-tuple-element.29), channel_id=1, source_target_pairs={{1,2},{2,1},{5,6},{6,5},{9,10},{10,9},{13,14},{14,13},{17,18},{18,... | collective-permute-start | bytes 294920 | tf_op jit(solution)/shard_map/ppermute | solution.py:411
  9.6 0.0 collective-permute-done.lon_near_ref
  9.6 2.4 %collective-permute-done.1.lon_far_ref = f32[64,128]{1,0:T(8,128)S(1)} collective-permute-done((f32[64,128]{1,0:T(8,128)S(1)}, f32[64,128]{1,0:T(8,128)S(1)}, u32[]{:S(2)}, u32[]{:S(2)}) %collective-permute-start.1) | collective-permute-done | bytes 32800 | tf_op jit(solution)/shard_map/ppermute | solution.py:409
  12.0 0.7 %collective-permute-start.5 = (f32[32,256]{1,0:T(8,128)S(1)}, f32[32,256]{1,0:T(8,128)S(1)}, u32[]{:S(2)}, u32[]{:S(2)}) collective-permute-start(f32[32,256]{1,0:T(8,128)S(1)} %get-tuple-element.48), channel_id=1, source_target_pairs={{1,2},{2,1},{5,6},{6,5},{9,10},{10,9},{13,14},{14,13},{17,18},{18,... | collective-permute-start | bytes 98312 | tf_op jit(solution)/shard_map/ppermute | solution.py:416
  12.7 2.9 %collective-permute-start.4 = (f32[32,256]{1,0:T(8,128)S(1)}, f32[32,256]{1,0:T(8,128)S(1)}, u32[]{:S(2)}, u32[]{:S(2)}) collective-permute-start(f32[32,256]{1,0:T(8,128)S(1)} %get-tuple-element.49), channel_id=1, source_target_pairs={{0,1},{1,0},{2,3},{3,2},{4,5},{5,4},{6,7},{7,6},{8,9},{9,8},{10,11... | collective-permute-start | bytes 98312 | tf_op jit(solution)/shard_map/ppermute | solution.py:417
  15.6 0.0 collective-permute-done.5.corner_far_ref
  15.6 0.9 %collective-permute-done.4.corner_near_ref = f32[32,256]{1,0:T(8,128)S(1)} collective-permute-done((f32[32,256]{1,0:T(8,128)S(1)}, f32[32,256]{1,0:T(8,128)S(1)}, u32[]{:S(2)}, u32[]{:S(2)}) %collective-permute-start.4) | collective-permute-done | bytes 32800 | tf_op jit(solution)/shard_map/ppermute | solution.py:417
  16.4 0.0 collective-permute-done.2.lat_near_ref
  16.4 0.0 collective-permute-done.3.lat_far_ref
  16.4 1.9 %descend.1 = (f32[8,128]{1,0:T(8,128)S(1)}, f32[16,8,384]{2,1,0:T(8,128)S(1)}, f32[16,8,384]{2,1,0:T(8,128)S(1)}, f32[16,8,384]{2,1,0:T(8,128)S(1)}, f32[16,8,38...) custom-call(s32[2]{0:T(128)S(1)} %pad_add_fusion.where_ref, ...), custom_call_target="tpu_custom_call" | custom-call | tf_op jit(solution)/shard_map/descend/pallas_call | solution.py:422
  18.4 13.7 %all_to_all.5.blocks_ref = f32[32,8,128]{2,1,0:T(8,128)S(1)} all-to-all(f32[32,8,128]{2,1,0:T(8,128)S(1)} %broadcast_in_dim.2), channel_id=1, replica_groups=mesh['lon'=8,'lat'=4] {'lon','lat'}, dimensions={0} | all-to-all | bytes 262144 | tf_op jit(solution)/shard_map/all_to_all | solution.py:435
  32.1 3.6 %ascend.1 = (f32[64,256]{1,0:T(8,128)}, f32[64,256]{1,0:T(8,128)}) custom-call(s32[2]{0:T(128)S(1)} %pad_add_fusion.where_ref, f32[32,8,128]{2,1,0:T(8,128)S(1)} %all_to_all.5.blocks_ref, f32[16,8,384]{2,1,0:T(8,128)S(1)} %get-tuple-element.32.rest_0_, f32[16,8,384]{2,1,0:T(8,128)S(1)} %get-tuple-element.33.rest_1_, ...), custom_call_target="tpu_custom_call" | custom-call | tf_op jit(solution)/shard_map/ascend/pallas_call | solution.py:439
  (4 shorter events, 0.0 us)
Async XLA Ops:
  2.3 7.3 %collective-permute-start = (f32[64,128]{1,0:T(8,128)S(1)}, f32[64,128]{1,0:T(8,128)S(1)}, u32[]{:S(2)}, u32[]{:S(2)}) collective-permute-start(f32[64,128]{1,0:T(8,128)S(1)} %get-tuple-element.26), channel_id=1, source_target_pairs={{0,4},{4,0},{8,12},{12,8},{16,20},{20,16},{24,28},{28,24},{1,5},{5... | collective-permute-start | bytes 98312 | tf_op jit(solution)/shard_map/ppermute | solution.py:410
  5.4 6.6 %collective-permute-start.1 = (f32[64,128]{1,0:T(8,128)S(1)}, f32[64,128]{1,0:T(8,128)S(1)}, u32[]{:S(2)}, u32[]{:S(2)}) collective-permute-start(f32[64,128]{1,0:T(8,128)S(1)} %get-tuple-element.27), channel_id=1, source_target_pairs={{4,8},{8,4},{12,16},{16,12},{20,24},{24,20},{28,0},{0,28},{5,9},{9... | collective-permute-start | bytes 98312 | tf_op jit(solution)/shard_map/ppermute | solution.py:409
  8.9 7.5 %collective-permute-start.2 = (f32[32,768]{1,0:T(8,128)S(1)}, f32[32,768]{1,0:T(8,128)S(1)}, u32[]{:S(2)}, u32[]{:S(2)}) collective-permute-start(f32[32,768]{1,0:T(8,128)S(1)} %get-tuple-element.28), channel_id=1, source_target_pairs={{0,1},{1,0},{2,3},{3,2},{4,5},{5,4},{6,7},{7,6},{8,9},{9,8},{10,11... | collective-permute-start | bytes 294920 | tf_op jit(solution)/shard_map/ppermute | solution.py:412
  8.9 7.5 %collective-permute-start.3 = (f32[32,768]{1,0:T(8,128)S(1)}, f32[32,768]{1,0:T(8,128)S(1)}, u32[]{:S(2)}, u32[]{:S(2)}) collective-permute-start(f32[32,768]{1,0:T(8,128)S(1)} %get-tuple-element.29), channel_id=1, source_target_pairs={{1,2},{2,1},{5,6},{6,5},{9,10},{10,9},{13,14},{14,13},{17,18},{18,... | collective-permute-start | bytes 294920 | tf_op jit(solution)/shard_map/ppermute | solution.py:411
  12.0 3.6 %collective-permute-start.5 = (f32[32,256]{1,0:T(8,128)S(1)}, f32[32,256]{1,0:T(8,128)S(1)}, u32[]{:S(2)}, u32[]{:S(2)}) collective-permute-start(f32[32,256]{1,0:T(8,128)S(1)} %get-tuple-element.48), channel_id=1, source_target_pairs={{1,2},{2,1},{5,6},{6,5},{9,10},{10,9},{13,14},{14,13},{17,18},{18,... | collective-permute-start | bytes 98312 | tf_op jit(solution)/shard_map/ppermute | solution.py:416
  12.7 3.8 %collective-permute-start.4 = (f32[32,256]{1,0:T(8,128)S(1)}, f32[32,256]{1,0:T(8,128)S(1)}, u32[]{:S(2)}, u32[]{:S(2)}) collective-permute-start(f32[32,256]{1,0:T(8,128)S(1)} %get-tuple-element.49), channel_id=1, source_target_pairs={{0,1},{1,0},{2,3},{3,2},{4,5},{5,4},{6,7},{7,6},{8,9},{9,8},{10,11... | collective-permute-start | bytes 98312 | tf_op jit(solution)/shard_map/ppermute | solution.py:417

commit v3 on v2

--- a/solution.py
+++ b/solution.py
@@ -19,7 +19,8 @@
 LANES = 128
 TILE = 8
 FIELDS = 3
-VMEM_LIMIT = 40 * 1024 * 1024
+SHIFT = 2
+VMEM_LIMIT = 8 * 1024 * 1024
 
 
 def iota(shape, dim):
@@ -72,8 +73,14 @@
         ref[t] = value
 
 
+def metric(row):
+    center = jnp.cos(jnp.deg2rad(BAND_SOUTH + ROW_STEP * (row + 0.5)))
+    northern = jnp.cos(jnp.deg2rad(BAND_SOUTH + ROW_STEP * (row + 1.0)))
+    return center, northern
+
+
 def prepare(where_ref, forcing_ref, surface_ref, sea_ref, levels_ref,
-            own_ref, lon_near_ref, lon_far_ref, lat_near_ref, lat_far_ref, scale_ref,
+            own_ref, east_edge_ref, west_edge_ref, lat_near_ref, lat_far_ref, diagonal_edge_ref,
             forcing_buf, surface_buf, sea_buf, levels_buf, sems):
     copies = [
         pltpu.make_async_copy(source, target, sems.at[i])
@@ -84,17 +91,8 @@
     for copy in copies:
         copy.start()
     rows, cols = forcing_buf.shape
-    lon_odd = lax.rem(where_ref[0], 2)
     lat_odd = lax.rem(where_ref[1], 2)
     first_row = where_ref[1] * rows
-    count = scale_ref.shape[1]
-    height = count * TILE
-    for t in range(count):
-        row = iota((TILE, LANES), 0) * count + t
-        row = jnp.where(row < rows + HALO, row, row - height) + first_row
-        row = row.astype(jnp.float32)
-        scale_ref[0, t] = 1.0 / jnp.cos(jnp.deg2rad(BAND_SOUTH + ROW_STEP * (row + 0.5)))
-        scale_ref[1, t] = jnp.cos(jnp.deg2rad(BAND_SOUTH + ROW_STEP * (row + 1.0)))
     row = (iota((rows, LANES), 0) + first_row).astype(jnp.float32)
     center = jnp.cos(jnp.deg2rad(BAND_SOUTH + ROW_STEP * (row + 0.5)))
     center = jnp.concatenate([center] * (cols // LANES), axis=1)
@@ -105,60 +103,96 @@
     depth = sea_mask * ((layers + layers * (layers - 1.0) / 20.0) / 200.0)
     fields = (depth, surface_buf[...] * center * sea_mask, forcing_buf[...] * sea_mask)
     slot = iota((rows, LANES), 1) // HALO
-    last = LANES // HALO - 1
+    slots = LANES // HALO
     west_edge = jnp.zeros((rows, LANES), jnp.float32)
     east_edge = jnp.zeros((rows, LANES), jnp.float32)
     for f, value in enumerate(fields):
         own_ref[f] = value
         west_edge = jnp.where(slot == f, lane_shift(value[:, :LANES], -f * HALO), west_edge)
         east_edge = jnp.where(
-            slot == (f + last) % (last + 1), lane_shift(value[:, cols - LANES :], -f * HALO), east_edge
+            slot == (f + slots - 1) % slots, lane_shift(value[:, cols - LANES :], -f * HALO), east_edge
         )
-    odd = jnp.broadcast_to(lon_odd, (rows, LANES)) > 0
-    lon_near_ref[...] = jnp.where(odd, west_edge, east_edge)
-    lon_far_ref[...] = jnp.where(odd, east_edge, west_edge)
+    east_edge_ref[...] = east_edge
+    west_edge_ref[...] = west_edge
     odd = jnp.broadcast_to(lat_odd, (HALO, cols)) > 0
     for f, value in enumerate(fields):
         south_edge, north_edge = value[:HALO], value[rows - HALO :]
         part = slice(f * cols, (f + 1) * cols)
         lat_near_ref[:, part] = jnp.where(odd, south_edge, north_edge)
         lat_far_ref[:, part] = jnp.where(odd, north_edge, south_edge)
-
-
-def descend(where_ref, own_ref, lon_near_ref, lon_far_ref, lat_near_ref, lat_far_ref,
-            corner_near_ref, corner_far_ref, scale_ref, pack_ref, *rest):
-    level_refs = [rest[5 * i : 5 * i + 5] for i in range(LEVELS)]
-    diagonal_ref, grid_ref = rest[5 * LEVELS :]
-    lon_index = where_ref[0]
-    lon_odd = lax.rem(lon_index, 2)
+    odd = odd[:, :LANES]
+    part = slice(FIELDS * cols, FIELDS * cols + LANES)
+    lat_near_ref[:, part] = jnp.where(odd, west_edge[:HALO], west_edge[rows - HALO :])
+    lat_far_ref[:, part] = jnp.where(odd, west_edge[rows - HALO :], west_edge[:HALO])
+    diagonal_edge_ref[...] = jnp.where(odd, east_edge[rows - HALO :], east_edge[:HALO])
+
+
+def faces(depth, across, along):
+    count = len(depth)
+    east_face = [jnp.minimum(depth[t], lane_shift(depth[t], 1)) * across[t] for t in range(count)]
+    north_face = [jnp.minimum(depth[t], north_of(depth, t)) * along[t] for t in range(count)]
+    return east_face, north_face
+
+
+def level_down(level, east_face, north_face, source_term, source):
+    stride = 1 << level
+    count = len(source)
+    inverse, diagonal = [], []
+    for t in range(count):
+        total = source_term[t] + (
+            (east_face[t] + lane_shift(east_face[t], -stride))
+            + (north_face[t] + south_of(north_face, t))
+        )
+        diagonal.append(jnp.where(source_term[t] > 0.0, total, 1.0))
+        inverse.append(DAMPING / diagonal[t])
+    field = [inverse[t] * source[t] for t in range(count)]
+    for _ in range(SWEEPS - 1):
+        field = sweep(field, source, inverse, east_face, north_face, stride)
+    image = remainder(field, source, diagonal, east_face, north_face, stride)
+    kept = (east_face, north_face, inverse, source, field, diagonal)
+
+    def coarse(tiles):
+        sums = [tiles[t] + tiles[t + 1] for t in range(0, count, 2)]
+        return [value + lane_shift(value, stride) for value in sums]
+
+    east_next = [lane_shift(east_face[t] + east_face[t + 1], stride) for t in range(0, count, 2)]
+    north_next = [north_face[t] + lane_shift(north_face[t], stride) for t in range(1, count, 2)]
+    return kept, (east_next, north_next, coarse(source_term), coarse(image))
+
+
+def lay_out(lat_count, where_ref, own_ref, lat_near_ref, lat_far_ref, west_ref, west_far_ref, east_ref, scale_ref, grid_ref):
+    rows, cols = own_ref.shape[1], own_ref.shape[2]
+    columns, height = grid_ref.shape[1], grid_ref.shape[2]
+    count = height // TILE
+    own_columns = cols // LANES
     lat_odd = lax.rem(where_ref[1], 2)
-    rows, cols = own_ref.shape[1], own_ref.shape[2]
-    count, width = diagonal_ref.shape[0], diagonal_ref.shape[2]
-    own_columns = cols // LANES
-    columns = width // LANES
     near_row = rows + pl.multiple_of(lat_odd * HALO, HALO)
     far_row = rows + pl.multiple_of((1 - lat_odd) * HALO, HALO)
+    edge = FIELDS * cols + LANES
+    parts = (
+        (0, 0, west_ref, [own_ref.at[f] for f in range(FIELDS)]),
+        (near_row, rows, lat_near_ref.at[:, pl.ds(edge, LANES)],
+         [lat_near_ref.at[:, pl.ds(f * cols, cols)] for f in range(FIELDS)]),
+        (far_row, rows + HALO, west_far_ref, [lat_far_ref.at[:, pl.ds(f * cols, cols)] for f in range(FIELDS)]),
+    )
     last = LANES // HALO - 1
-    parts = (
-        (0, lon_near_ref[...], lon_far_ref[...], [own_ref.at[f] for f in range(FIELDS)]),
-        (near_row, corner_near_ref[:, :LANES], corner_near_ref[:, LANES:],
-         [lat_near_ref.at[:, pl.ds(f * cols, cols)] for f in range(FIELDS)]),
-        (far_row, corner_far_ref[:, :LANES], corner_far_ref[:, LANES:],
-         [lat_far_ref.at[:, pl.ds(f * cols, cols)] for f in range(FIELDS)]),
-    )
-    for first, near_val, far_val, bodies in parts:
-        size = near_val.shape[0]
-        odd = jnp.broadcast_to(lon_odd, near_val.shape) > 0
-        east_val = jnp.where(odd, far_val, near_val)
-        west_val = jnp.where(odd, near_val, far_val)
-        slot = iota(near_val.shape, 1) // HALO
+    for first, at, side_ref, bodies in parts:
+        west = side_ref[...]
+        slot = iota(west.shape, 1) // HALO
+        lat_index = where_ref[1]
+        outside = jnp.broadcast_to((lat_index == 0) | (lat_index == lat_count - 1), west.shape)
         for f, body in enumerate(bodies):
-            both = jnp.where(
-                slot == f, east_val, jnp.where(slot == (f + last) % (last + 1), west_val, 0.0)
-            )
             for c in range(own_columns):
-                grid_ref[f, c, pl.ds(first, size), :] = body[:, c * LANES : (c + 1) * LANES]
-            grid_ref[f, own_columns, pl.ds(first, size), :] = lane_shift(both, f * HALO)
+                value = body[:, c * LANES : (c + 1) * LANES]
+                if first is far_row:
+                    value = jnp.where(outside, 0.0, value)
+                grid_ref[f, c, pl.ds(first, west.shape[0]), :] = value
+            side = jnp.where(slot == (f + last) % (last + 1), west, 0.0)
+            if east_ref is not None:
+                side = jnp.where(slot == f, east_ref[pl.ds(at, west.shape[0]), :], side)
+            if first is far_row:
+                side = jnp.where(outside, 0.0, side)
+            grid_ref[f, own_columns, pl.ds(first, west.shape[0]), :] = lane_shift(side, f * HALO)
 
     def load(f):
         return [
@@ -168,64 +202,57 @@
             for t in range(count)
         ]
 
-    depth = load(0)
-    source_term = load(1)
-    source = load(2)
+    depth, source_term, source = load(0), load(1), load(2)
     across = [jnp.concatenate([scale_ref[0, t]] * columns, axis=1) for t in range(count)]
     along = [jnp.concatenate([scale_ref[1, t]] * columns, axis=1) for t in range(count)]
-    east_face = [jnp.minimum(depth[t], lane_shift(depth[t], 1)) * across[t] for t in range(count)]
-    north_face = [jnp.minimum(depth[t], north_of(depth, t)) * along[t] for t in range(count)]
+    return faces(depth, across, along) + (source_term, source)
+
+
+def hold(lat_count, where_ref, own_ref, lat_near_ref, lat_far_ref, west_ref, west_far_ref, east_ref, scale_ref, *rest):
+    level_refs = [rest[5 * i : 5 * i + 5] for i in range(LEVELS)]
+    diagonal_ref, grid_ref = rest[5 * LEVELS :]
+    state = lay_out(lat_count, where_ref, own_ref, lat_near_ref, lat_far_ref, west_ref, west_far_ref, east_ref, scale_ref,
+                    grid_ref)
     for level in range(LEVELS):
-        stride = 1 << level
-        inverse, diagonal = [], []
-        for t in range(count >> level):
-            total = source_term[t] + (
-                (east_face[t] + lane_shift(east_face[t], -stride))
-                + (north_face[t] + south_of(north_face, t))
-            )
-            diagonal.append(jnp.where(source_term[t] > 0.0, total, 1.0))
-            inverse.append(DAMPING / diagonal[t])
-        field = [inverse[t] * source[t] for t in range(count >> level)]
-        for _ in range(SWEEPS - 1):
-            field = sweep(field, source, inverse, east_face, north_face, stride)
-        image = remainder(field, source, diagonal, east_face, north_face, stride)
-        for ref, value in zip(level_refs[level], (east_face, north_face, inverse, source, field)):
-            keep(ref, value)
+        kept, state = level_down(level, *state)
+        for ref, tiles in zip(level_refs[level], kept):
+            keep(ref, tiles)
         if level == 0:
-            keep(diagonal_ref, diagonal)
-
-        def coarse(tiles):
-            sums = [tiles[t] + tiles[t + 1] for t in range(0, len(tiles), 2)]
-            return [value + lane_shift(value, stride) for value in sums]
-
-        east_face = [
-            lane_shift(east_face[t] + east_face[t + 1], stride) for t in range(0, len(east_face), 2)
-        ]
-        north_face = [
-            north_face[t] + lane_shift(north_face[t], stride) for t in range(1, len(north_face), 2)
-        ]
-        source_term = coarse(source_term)
-        source = coarse(image)
-
+            keep(diagonal_ref, kept[-1])
+
+
+def descend(lat_count, where_ref, own_ref, lat_near_ref, lat_far_ref, west_ref, west_far_ref, scale_ref, pack_ref, grid_ref):
+    lon_index = where_ref[0]
+    cols = own_ref.shape[2]
+    own_columns = cols // LANES
+    columns = grid_ref.shape[1]
+    state = lay_out(lat_count, where_ref, own_ref, lat_near_ref, lat_far_ref, west_ref, west_far_ref, None, scale_ref,
+                    grid_ref)
+    for level in range(LEVELS):
+        _, state = level_down(level, *state)
+
+    east_face, north_face, source_term, source = state
     stride = 1 << LEVELS
     bottom_width = cols // stride
     group = LANES // bottom_width
     per_column = LANES // stride
     tiles = len(source)
     lane = iota((TILE, LANES), 1)
-    cell = lane % bottom_width
-    pick = (cell % per_column) * stride
+    cell = lane % bottom_width - SHIFT
+    column = jnp.where(cell < 0, own_columns, cell // per_column)
+    pick = jnp.where(cell < 0, LANES + cell * stride, (cell % per_column) * stride)
     turn = lax.rem(lane // bottom_width + group - lax.rem(lon_index, group), group)
+    own_rows = pack_ref.shape[1] // tiles
     for t in range(tiles):
         packed = jnp.zeros((TILE, LANES), jnp.float32)
         for f, value in enumerate((source[t], east_face[t], north_face[t], source_term[t])):
             flat = jnp.zeros((TILE, LANES), jnp.float32)
-            for c in range(own_columns):
+            for c in range(columns):
                 taken = jnp.take_along_axis(value[:, c * LANES : (c + 1) * LANES], pick, axis=1)
-                flat = jnp.where(cell // per_column == c, taken, flat)
+                flat = jnp.where(column == c, taken, flat)
             packed = jnp.where(turn == f, flat, packed)
-        own_rows = pack_ref.shape[0] // tiles
-        pack_ref[pl.ds(t, own_rows, stride=tiles), :] = packed[:own_rows]
+        for k in range(pack_ref.shape[0]):
+            pack_ref[k, pl.ds(t, own_rows, stride=tiles), :] = packed[:own_rows]
 
 
 def total_of(tiles):
@@ -308,16 +335,16 @@
     pad = 2 * TILE
     window_ref[pl.ds(0, pad), :] = jnp.zeros((pad, LANES), jnp.float32)
     window_ref[pl.ds(pad + bottom_height, pad), :] = jnp.zeros((pad, LANES), jnp.float32)
-    margin = LANES // 2 // stride
-    shift = lax.rem(margin - lon_index * bottom_width + whole_width, whole_width)
+    half = LANES // 2
+    margin = half // stride
+    shift = lax.rem(margin - SHIFT - lon_index * bottom_width + whole_width, whole_width)
     window_ref[pl.ds(pad, bottom_height), :] = pltpu.roll(iterate, shift, 1)[:, :LANES]
     start = pl.multiple_of(lat_index * bottom_rows, TILE)
-    strip = window_ref[pl.ds(start, 5 * TILE), :]
-    turn_ref[...] = strip
+    turn_ref[...] = window_ref[pl.ds(start, 5 * TILE), :]
     tiles = count >> LEVELS
+    lane = iota((TILE, LANES), 1)
+    ahead = (rows + HALO) // stride // tiles
     sublane = iota((TILE, LANES), 0)
-    ahead = (rows + HALO) // stride // tiles
-    lane = iota((TILE, LANES), 1)
     correction = []
     for t in range(tiles):
         upper = turn_ref[pl.ds(pad + t, TILE, stride=tiles), :]
@@ -328,9 +355,7 @@
             if c < own_columns:
                 pick = margin + (c * LANES + lane) // stride
             else:
-                pick = jnp.where(
-                    lane < LANES // 2, margin + bottom_width + lane // stride, (lane - LANES // 2) // stride
-                )
+                pick = jnp.where(lane < half, margin + bottom_width + lane // stride, (lane - half) // stride)
             parts.append(jnp.take_along_axis(value, pick, axis=1))
         correction.append(jnp.concatenate(parts, axis=1))
 
@@ -359,12 +384,11 @@
             ref[:, part] = order_ref[k, c]
 
 
-def swap_pairs(count, first, periodic):
+def swap_pairs(count, first):
     pairs = []
     for i in range(first, count, 2):
-        j = i + 1
-        if j < count or periodic:
-            pairs += [(i, j % count), (j % count, i)]
+        j = (i + 1) % count
+        pairs += [(i, j), (j, i)]
     return pairs
 
 
@@ -380,16 +404,18 @@
     lon_index = lax.axis_index("lon").astype(jnp.int32)
     lat_index = lax.axis_index("lat").astype(jnp.int32)
     where = jnp.stack([lon_index, lat_index])
-
-    own, lon_near, lon_far, lat_near, lat_far, scale = pl.pallas_call(
+    inputs = [
+        pltpu.with_memory_space_constraint(x, pltpu.HBM) for x in (forcing, surface_term, sea_cells, levels)
+    ]
+    own, east_edge, west_edge, lat_near, lat_far, diagonal_edge = pl.pallas_call(
         prepare,
         out_shape=[
             jax.ShapeDtypeStruct((FIELDS, rows, cols), f32),
             jax.ShapeDtypeStruct((rows, LANES), f32),
             jax.ShapeDtypeStruct((rows, LANES), f32),
-            jax.ShapeDtypeStruct((HALO, FIELDS * cols), f32),
-            jax.ShapeDtypeStruct((HALO, FIELDS * cols), f32),
-            jax.ShapeDtypeStruct((2, count, TILE, LANES), f32),
+            jax.ShapeDtypeStruct((HALO, FIELDS * cols + LANES), f32),
+            jax.ShapeDtypeStruct((HALO, FIELDS * cols + LANES), f32),
+            jax.ShapeDtypeStruct((HALO, LANES), f32),
         ],
         in_specs=[smem] + [hbm] * 4,
         out_specs=[vmem] * 6,
@@ -402,39 +428,61 @@
         ],
         compiler_params=params,
         name="prepare",
-    )(where, *(pltpu.with_memory_space_constraint(x, pltpu.HBM) for x in (forcing, surface_term, sea_cells, levels)))
-
-    far_pairs, near_pairs = swap_pairs(lon_count, 1, True), swap_pairs(lon_count, 0, True)
-    north_pairs, south_pairs = swap_pairs(lat_count, 0, False), swap_pairs(lat_count, 1, False)
-    lon_far = lax.ppermute(lon_far, "lon", far_pairs)
-    lon_near = lax.ppermute(lon_near, "lon", near_pairs)
-    lat_far = lax.ppermute(lat_far, "lat", south_pairs)
-    lat_near = lax.ppermute(lat_near, "lat", north_pairs)
-    sides = jnp.concatenate([lon_near, lon_far], axis=1)
+    )(where, *inputs)
+
+    eastward = [(i, (i + 1) % lon_count) for i in range(lon_count)]
+    westward = [(target, source) for source, target in eastward]
+    near_pairs, far_pairs = swap_pairs(lat_count, 0), swap_pairs(lat_count, 1)
+    across_pairs = [
+        (i * lat_count + a, (i + 1) % lon_count * lat_count + b) for i in range(lon_count) for a, b in far_pairs
+    ]
+    west_halo = lax.ppermute(east_edge, "lon", eastward)
+    lat_far = lax.ppermute(lat_far, "lat", far_pairs)
+    west_far = lax.ppermute(diagonal_edge, ("lon", "lat"), across_pairs)
     odd = lat_index % 2 == 1
-    south_edge, north_edge = sides[:HALO], sides[rows - HALO :]
-    corner_far = lax.ppermute(jnp.where(odd, north_edge, south_edge), "lat", south_pairs)
-    corner_near = lax.ppermute(jnp.where(odd, south_edge, north_edge), "lat", north_pairs)
+    lat_near = lax.ppermute(
+        jnp.concatenate([lat_near, jnp.where(odd, west_halo[:HALO], west_halo[rows - HALO :])], axis=1),
+        "lat",
+        near_pairs,
+    )
+    edge = FIELDS * cols
+    east_halo = lax.ppermute(
+        jnp.concatenate([west_edge, lat_near[:, edge : edge + LANES], lat_far[:, edge : edge + LANES]], axis=0),
+        "lon",
+        westward,
+    )
+
+    row = jnp.arange(TILE)[None, :] * count + jnp.arange(count)[:, None]
+    row = jnp.where(row < rows + HALO, row, row - height).astype(f32) + (lat_index * rows).astype(f32)
+    center, northern = metric(row)
+    scale = jnp.broadcast_to(jnp.stack([1.0 / center, northern])[..., None], (2, count, TILE, LANES))
+
+    devices = lat_count * lon_count
+    grid = pltpu.VMEM((FIELDS, width // LANES, height, LANES), f32)
+    packed = pl.pallas_call(
+        functools.partial(descend, lat_count),
+        out_shape=jax.ShapeDtypeStruct((devices, rows >> LEVELS, LANES), f32),
+        in_specs=[smem] + [vmem] * 6,
+        out_specs=vmem,
+        scratch_shapes=[grid],
+        compiler_params=params,
+        name="descend",
+    )(where, own, lat_near, lat_far, west_halo, west_far, scale)
+    blocks = lax.all_to_all(packed, ("lon", "lat"), 0, 0, tiled=True)
 
     level_shapes = []
     for level in range(LEVELS):
         level_shapes += [jax.ShapeDtypeStruct((count >> level, TILE, width), f32)] * 5
     held = pl.pallas_call(
-        descend,
-        out_shape=[jax.ShapeDtypeStruct((rows >> LEVELS, LANES), f32)]
-        + level_shapes
-        + [jax.ShapeDtypeStruct((count, TILE, width), f32)],
-        in_specs=[smem] + [vmem] * 8,
-        out_specs=[vmem] * (2 + len(level_shapes)),
-        scratch_shapes=[pltpu.VMEM((FIELDS, width // LANES, height, LANES), f32)],
+        functools.partial(hold, lat_count),
+        out_shape=level_shapes + [jax.ShapeDtypeStruct((count, TILE, width), f32)],
+        in_specs=[smem] + [vmem] * 7,
+        out_specs=[vmem] * (1 + len(level_shapes)),
+        scratch_shapes=[grid],
         compiler_params=params,
-        name="descend",
-    )(where, own, lon_near, lon_far, lat_near, lat_far, corner_near, corner_far, scale)
-    packed, held = held[0], held[1:]
-
-    blocks = lax.all_to_all(
-        jnp.broadcast_to(packed[None], (lat_count * lon_count,) + packed.shape), ("lon", "lat"), 0, 0, tiled=True
-    )
+        cost_estimate=pl.CostEstimate(flops=0, bytes_accessed=60 * 1024 * 1024, transcendentals=0),
+        name="hold",
+    )(where, own, lat_near, lat_far, west_halo, west_far, east_halo, scale)
 
     return pl.pallas_call(
         functools.partial(ascend, lat_count, lon_count),

time: 35.9 us -> 32 us (0.89)
  blocking collectives: 13.7 us -> 0 us
  starting transfers between devices: 10.8 us -> 14.3 us
  waiting for transfers between devices: 3.23 us -> 6.3 us
  Pallas kernels: 7.14 us -> 9.32 us
  local copies, waits for them, and re-layouts: 0.02 us -> 0.86 us
    all_to_all x1 -> x0, blocking collectives: 13.7 us -> none  [on_device(): lax.all_to_all(jnp.broadcast_to(packed[None], (lat_count * lon_count,) +...]
    all_to_all x0 -> x1, starting transfers between devices: none -> 3.91 us  [on_device(): blocks = lax.all_to_all(packed, ('lon', 'lat'), 0, 0, tiled=True)]
    ppermute x6 -> x5, waiting for transfers between devices: 3.23 us -> 6.3 us  [the longest x1 2.23 us: on_device(): west_halo = lax.ppermute(east_edge, 'lon', eastward)]
    pallas_call x1 -> x2, Pallas kernels: 1.91 us -> 4.14 us  [the longest x1 2.52 us: on_device(): pl.pallas_call(functools.partial(descend, lat_count), out_shape=jax.Shape...]
    slice x0 -> x3, local copies, waits for them, and re-layouts: none -> 0.69 us  [the longest x2 0.69 us: on_device(): lat_far[:, edge:edge + LANES]]
    ppermute x6 -> x5, starting transfers between devices: 10.8 us -> 10.3 us  [the longest x1 4.55 us: on_device(): lax.ppermute(jnp.concatenate([west_edge, lat_near[:, edge:edge + LANES],...]
  transfers between devices with their start and end apart: 6 -> 6, of which waited for: 2 -> 3; matrix products, arithmetic and copies ran while one was open for 0% -> 1% of each run, Pallas kernels for 0% -> 5%
where the time goes in v3:
time: 32 us; the launch traced here: 31.7 us
  starting transfers between devices  14.3 us (45%)
  Pallas kernels  9.32 us (29%)
  waiting for transfers between devices  6.3 us (20%)
  local copies, waits for them, and re-layouts  0.86 us (3%)
  between operations  0.74 us (2%)
    ppermute x1, starting transfers between devices, on_device(): lax.ppermute(jnp.concatenate([west_edge, lat_near[:, edge:edge + LANES],...  4.55 us
    all_to_all x1, starting transfers between devices, on_device(): blocks = lax.all_to_all(packed, ('lon', 'lat'), 0, 0, tiled=True)  3.91 us
    pallas_call x1, Pallas kernels, on_device(): pl.pallas_call(functools.partial(ascend, lat_count, lon_count), out_shape...  3.57 us
    ppermute x1, starting transfers between devices, on_device(): west_halo = lax.ppermute(east_edge, 'lon', eastward)  3.02 us
    pallas_call x1, Pallas kernels, on_device(): pl.pallas_call(functools.partial(descend, lat_count), out_shape=jax.Shape...  2.52 us
    ppermute x1, waiting for transfers between devices, on_device(): west_halo = lax.ppermute(east_edge, 'lon', eastward)  2.23 us
    ppermute x1, waiting for transfers between devices, on_device(): west_far = lax.ppermute(diagonal_edge, ('lon', 'lat'), across_pairs)  2.16 us
    ppermute x1, starting transfers between devices, on_device(): west_far = lax.ppermute(diagonal_edge, ('lon', 'lat'), across_pairs)  2.05 us
  transfers between devices with their start and end apart: 6, of which 3 were waited for; matrix products, arithmetic and copies ran while one was open for 1% of the time, Pallas kernels for 5%

profile of v3, /device:TPU:0, one launch (start us, length us, event | category | flops | bytes accessed | tf_op | source)
XLA Modules:
  0.0 31.7 jit_solution(2040314761469478078)
XLA Ops:
  0.6 0.1 pad_add_fusion.where_ref
  0.7 1.6 %prepare.1 = (f32[3,64,256]{2,1,0:T(8,128)S(1)}, f32[64,128]{1,0:T(8,128)S(1)}, f32[64,128]{1,0:T(8,128)S(1)}, f32[32,896]{1,0:T(8,128)S(1)}, f32[32,896]{1,0:T(8,128)S(1)}, /*index=5*/f32[32,128]{1,0:T(8,128)S(1)}) custom-call(s32[2]{0:T(128)S(1)} %pad_add_fusion.where_ref, f32[64,256]{1,0:T(8,128)} %forcing_ref.1, f32[64,256]{1,0:T(8,128)} %surface_ref.1, ...), custom_call_target="tpu_custom_call" | custom-call | tf_op jit(solution)/shard_map/prepare/pallas_call | solution.py:410
  2.3 3.0 %collective-permute-start = (f32[64,128]{1,0:T(8,128)S(1)}, f32[64,128]{1,0:T(8,128)S(1)}, u32[]{:S(2)}, u32[]{:S(2)}) collective-permute-start(f32[64,128]{1,0:T(8,128)S(1)} %get-tuple-element.26), channel_id=1, source_target_pairs={{0,4},{4,8},{8,12},{12,16},{16,20},{20,24},{24,28},{28,0},{1,5},{5... | collective-permute-start | bytes 98312 | tf_op jit(solution)/shard_map/ppermute | solution.py:439
  5.4 0.7 %collective-permute-start.2 = (f32[32,896]{1,0:T(8,128)S(1)}, f32[32,896]{1,0:T(8,128)S(1)}, u32[]{:S(2)}, u32[]{:S(2)}) collective-permute-start(f32[32,896]{1,0:T(8,128)S(1)} %get-tuple-element.27), channel_id=1, source_target_pairs={{1,2},{2,1},{3,0},{0,3},{5,6},{6,5},{7,4},{4,7},{9,10},{10,9},{11,... | collective-permute-start | bytes 344072 | tf_op jit(solution)/shard_map/ppermute | solution.py:440
  6.0 2.1 %collective-permute-start.3 = (f32[32,128]{1,0:T(8,128)S(1)}, f32[32,128]{1,0:T(8,128)S(1)}, u32[]{:S(2)}, u32[]{:S(2)}) collective-permute-start(f32[32,128]{1,0:T(8,128)S(1)} %get-tuple-element.28), channel_id=1, source_target_pairs={{1,6},{2,5},{3,4},{0,7},{5,10},{6,9},{7,8},{4,11},{9,14},{10,13},{... | collective-permute-start | bytes 49160 | tf_op jit(solution)/shard_map/ppermute | solution.py:441
  8.1 2.2 %collective-permute-done.west_ref = f32[64,128]{1,0:T(8,128)S(1)} collective-permute-done((f32[64,128]{1,0:T(8,128)S(1)}, f32[64,128]{1,0:T(8,128)S(1)}, u32[]{:S(2)}, u32[]{:S(2)}) %collective-permute-start) | collective-permute-done | bytes 32800 | tf_op jit(solution)/shard_map/ppermute | solution.py:439
  10.3 0.1 collective-permute-start.1
  10.4 0.1 cosine_divide_fusion
  10.5 0.1 copy.6
  10.6 2.2 %collective-permute-done.3.west_far_ref = f32[32,128]{1,0:T(8,128)S(1)} collective-permute-done((f32[32,128]{1,0:T(8,128)S(1)}, f32[32,128]{1,0:T(8,128)S(1)}, u32[]{:S(2)}, u32[]{:S(2)}) %collective-permute-start.3) | collective-permute-done | bytes 16416 | tf_op jit(solution)/shard_map/ppermute | solution.py:441
  12.8 0.0 collective-permute-done.2.lat_far_ref
  12.8 0.0 collective-permute-done.1.lat_near_ref
  12.8 0.1 broadcast_in_dim.2.scale_ref
  12.9 2.5 %descend.1 = f32[32,8,128]{2,1,0:T(8,128)} custom-call(s32[2]{0:T(128)S(1)} %pad_add_fusion.where_ref, f32[3,64,256]{2,1,0:T(8,128)S(1)} %get-tuple-element.24.own_ref, f32[32,1024]{1,0:T(8,128)S(1)} %collective-permute-done.1.lat_near_ref, f32[32,896]{1,0:T(8,128)S(1)} %collective-permute-done.2.lat_far_ref, f32[64,128]{1,0:T(8,128)S(1)} %collective-permute-done.west_ref, ...), custom_call_target="tpu_custom_call" | custom-call | tf_op jit(solution)/shard_map/descend/pallas_call | solution.py:462
  15.4 3.9 %all-to-all-start = ((f32[32,8,128]{2,1,0:T(8,128)}), f32[32,8,128]{2,1,0:T(8,128)S(1)}, u32[]{:S(2)}, u32[]{:S(2)}) async-start(f32[32,8,128]{2,1,0:T(8,128)} %descend.1), calls=%async_computation | async-start | bytes 262144 | tf_op jit(solution)/shard_map/all_to_all | solution.py:471
  19.3 0.0 copy-done
  19.3 0.0 slice-start
  19.3 0.0 copy-start.1
  19.3 0.7 %slice-done = f32[32,128]{1,0:T(8,128)S(1)} async-done(((f32[32,896]{1,0:T(8,128)}), f32[32,128]{1,0:T(8,128)S(1)}, s32[]{:S(2)}) %slice-start) | async-done | bytes 16408 | tf_op jit(solution)/shard_map/slice | solution.py:450
  20.0 4.6 %collective-permute-start.4 = (f32[128,128]{1,0:T(8,128)S(1)}, f32[128,128]{1,0:T(8,128)S(1)}, u32[]{:S(2)}, u32[]{:S(2)}) collective-permute-start(f32[128,128]{1,0:T(8,128)S(1)} %pad_maximum_fusion.1), channel_id=1, source_target_pairs={{4,0},{8,4},{12,8},{16,12},{20,16},{24,20},{28,24},{0,28},{5,1},{9... | collective-permute-start | bytes 196616 | tf_op jit(solution)/shard_map/ppermute | solution.py:449
  24.6 1.9 %collective-permute-done.4.east_ref = f32[128,128]{1,0:T(8,128)S(1)} collective-permute-done((f32[128,128]{1,0:T(8,128)S(1)}, f32[128,128]{1,0:T(8,128)S(1)}, u32[]{:S(2)}, u32[]{:S(2)}) %collective-permute-start.4) | collective-permute-done | bytes 65568 | tf_op jit(solution)/shard_map/ppermute | solution.py:449
  26.5 1.6 %hold.1 = (f32[16,8,384]{2,1,0:T(8,128)S(1)}, f32[16,8,384]{2,1,0:T(8,128)S(1)}, f32[16,8,384]{2,1,0:T(8,128)S(1)}, f32[16,8,384]{2,1,0:T(8,128)S(1)}, f32[16,8,...) custom-call(s32[2]{0:T(128)S(1)} %pad_add_fusion.where_ref, ...), custom_call_target="tpu_custom_call" | custom-call | bytes 62914560 | tf_op jit(solution)/shard_map/hold/pallas_call | solution.py:476
  28.1 0.0 all-to-all-done.blocks_ref
  28.1 3.6 %ascend.1 = (f32[64,256]{1,0:T(8,128)}, f32[64,256]{1,0:T(8,128)}) custom-call(s32[2]{0:T(128)S(1)} %pad_add_fusion.where_ref, f32[32,8,128]{2,1,0:T(8,128)S(1)} %all-to-all-done.blocks_ref, f32[16,8,384]{2,1,0:T(8,128)S(1)} %get-tuple-element.30.rest_0_, f32[16,8,384]{2,1,0:T(8,128)S(1)} %get-tuple-element.31.rest_1_, ...), custom_call_target="tpu_custom_call" | custom-call | tf_op jit(solution)/shard_map/ascend/pallas_call | solution.py:487
  (8 shorter events, 0.0 us)
Async XLA Ops:
  2.3 8.0 %collective-permute-start = (f32[64,128]{1,0:T(8,128)S(1)}, f32[64,128]{1,0:T(8,128)S(1)}, u32[]{:S(2)}, u32[]{:S(2)}) collective-permute-start(f32[64,128]{1,0:T(8,128)S(1)} %get-tuple-element.26), channel_id=1, source_target_pairs={{0,4},{4,8},{8,12},{12,16},{16,20},{20,24},{24,28},{28,0},{1,5},{5... | collective-permute-start | bytes 98312 | tf_op jit(solution)/shard_map/ppermute | solution.py:439
  5.4 7.4 %collective-permute-start.2 = (f32[32,896]{1,0:T(8,128)S(1)}, f32[32,896]{1,0:T(8,128)S(1)}, u32[]{:S(2)}, u32[]{:S(2)}) collective-permute-start(f32[32,896]{1,0:T(8,128)S(1)} %get-tuple-element.27), channel_id=1, source_target_pairs={{1,2},{2,1},{3,0},{0,3},{5,6},{6,5},{7,4},{4,7},{9,10},{10,9},{11,... | collective-permute-start | bytes 344072 | tf_op jit(solution)/shard_map/ppermute | solution.py:440
  6.0 6.8 %collective-permute-start.3 = (f32[32,128]{1,0:T(8,128)S(1)}, f32[32,128]{1,0:T(8,128)S(1)}, u32[]{:S(2)}, u32[]{:S(2)}) collective-permute-start(f32[32,128]{1,0:T(8,128)S(1)} %get-tuple-element.28), channel_id=1, source_target_pairs={{1,6},{2,5},{3,4},{0,7},{5,10},{6,9},{7,8},{4,11},{9,14},{10,13},{... | collective-permute-start | bytes 49160 | tf_op jit(solution)/shard_map/ppermute | solution.py:441
  10.3 2.5 %collective-permute-start.1 = (f32[32,1024]{1,0:T(8,128)S(1)}, f32[32,1024]{1,0:T(8,128)S(1)}, u32[]{:S(2)}, u32[]{:S(2)}) collective-permute-start(f32[32,1024]{1,0:T(8,128)S(1)} %pad_maximum_fusion), channel_id=1, source_target_pairs={{0,1},{1,0},{2,3},{3,2},{4,5},{5,4},{6,7},{7,6},{8,9},{9,8},{10,11... | collective-permute-start | bytes 393224 | tf_op jit(solution)/shard_map/ppermute | solution.py:443
  12.8 6.5 %copy-start = (f32[32,896]{1,0:T(8,128)}, f32[32,896]{1,0:T(8,128)S(1)}, u32[]{:S(2)}) copy-start(f32[32,896]{1,0:T(8,128)S(1)} %collective-permute-done.2.lat_far_ref) | copy-start | bytes 344068
  15.4 12.8 %all-to-all-start = ((f32[32,8,128]{2,1,0:T(8,128)}), f32[32,8,128]{2,1,0:T(8,128)S(1)}, u32[]{:S(2)}, u32[]{:S(2)}) async-start(f32[32,8,128]{2,1,0:T(8,128)} %descend.1), calls=%async_computation | async-start | bytes 262144 | tf_op jit(solution)/shard_map/all_to_all | solution.py:471
  19.3 0.7 %slice-start = ((f32[32,896]{1,0:T(8,128)}), f32[32,128]{1,0:T(8,128)S(1)}, s32[]{:S(2)}) async-start(f32[32,896]{1,0:T(8,128)} %copy-done), calls=%async_computation.1 | async-start | bytes 32768 | tf_op jit(solution)/shard_map/slice | solution.py:450
  19.3 7.2 %copy-start.1 = (f32[32,896]{1,0:T(8,128)S(1)}, f32[32,896]{1,0:T(8,128)}, u32[]{:S(2)}) copy-start(f32[32,896]{1,0:T(8,128)} %copy-done) | copy-start | bytes 344068
  20.0 6.5 %collective-permute-start.4 = (f32[128,128]{1,0:T(8,128)S(1)}, f32[128,128]{1,0:T(8,128)S(1)}, u32[]{:S(2)}, u32[]{:S(2)}) collective-permute-start(f32[128,128]{1,0:T(8,128)S(1)} %pad_maximum_fusion.1), channel_id=1, source_target_pairs={{4,0},{8,4},{12,8},{16,12},{20,16},{24,20},{28,24},{0,28},{5,1},{9... | collective-permute-start | bytes 196616 | tf_op jit(solution)/shard_map/ppermute | solution.py:449

commit v4 on v3

--- a/solution.py
+++ b/solution.py
@@ -79,8 +79,8 @@
     return center, northern
 
 
-def prepare(where_ref, forcing_ref, surface_ref, sea_ref, levels_ref,
-            own_ref, east_edge_ref, west_edge_ref, lat_near_ref, lat_far_ref, diagonal_edge_ref,
+def prepare(forcing_ref, surface_ref, sea_ref, levels_ref,
+            own_ref, east_edge_ref, west_edge_ref,
             forcing_buf, surface_buf, sea_buf, levels_buf, sems):
     copies = [
         pltpu.make_async_copy(source, target, sems.at[i])
@@ -91,8 +91,7 @@
     for copy in copies:
         copy.start()
     rows, cols = forcing_buf.shape
-    lat_odd = lax.rem(where_ref[1], 2)
-    first_row = where_ref[1] * rows
+    first_row = lax.axis_index("lat") * rows
     row = (iota((rows, LANES), 0) + first_row).astype(jnp.float32)
     center = jnp.cos(jnp.deg2rad(BAND_SOUTH + ROW_STEP * (row + 0.5)))
     center = jnp.concatenate([center] * (cols // LANES), axis=1)
@@ -114,17 +113,28 @@
         )
     east_edge_ref[...] = east_edge
     west_edge_ref[...] = west_edge
-    odd = jnp.broadcast_to(lat_odd, (HALO, cols)) > 0
-    for f, value in enumerate(fields):
-        south_edge, north_edge = value[:HALO], value[rows - HALO :]
+
+
+def prepare_corner(east_edge_ref, diagonal_edge_ref):
+    rows = east_edge_ref.shape[0]
+    odd = jnp.broadcast_to(lax.rem(lax.axis_index("lat"), 2), diagonal_edge_ref.shape) > 0
+    diagonal_edge_ref[...] = jnp.where(odd, east_edge_ref[pl.ds(rows - HALO, HALO), :], east_edge_ref[pl.ds(0, HALO), :])
+
+
+def prepare_rows(own_ref, west_edge_ref, lat_near_ref, lat_far_ref):
+    rows, cols = own_ref.shape[1:]
+    south, north = pl.ds(0, HALO), pl.ds(rows - HALO, HALO)
+    odd = jnp.broadcast_to(lax.rem(lax.axis_index("lat"), 2), (HALO, cols)) > 0
+    for f in range(FIELDS):
+        south_edge, north_edge = own_ref[f, south, :], own_ref[f, north, :]
         part = slice(f * cols, (f + 1) * cols)
         lat_near_ref[:, part] = jnp.where(odd, south_edge, north_edge)
         lat_far_ref[:, part] = jnp.where(odd, north_edge, south_edge)
     odd = odd[:, :LANES]
+    south_edge, north_edge = west_edge_ref[south, :], west_edge_ref[north, :]
     part = slice(FIELDS * cols, FIELDS * cols + LANES)
-    lat_near_ref[:, part] = jnp.where(odd, west_edge[:HALO], west_edge[rows - HALO :])
-    lat_far_ref[:, part] = jnp.where(odd, west_edge[rows - HALO :], west_edge[:HALO])
-    diagonal_edge_ref[...] = jnp.where(odd, east_edge[rows - HALO :], east_edge[:HALO])
+    lat_near_ref[:, part] = jnp.where(odd, south_edge, north_edge)
+    lat_far_ref[:, part] = jnp.where(odd, north_edge, south_edge)
 
 
 def faces(depth, across, along):
@@ -160,12 +170,12 @@
     return kept, (east_next, north_next, coarse(source_term), coarse(image))
 
 
-def lay_out(lat_count, where_ref, own_ref, lat_near_ref, lat_far_ref, west_ref, west_far_ref, east_ref, scale_ref, grid_ref):
+def lay_out(lat_count, own_ref, lat_near_ref, lat_far_ref, west_ref, west_far_ref, east_ref, scale_ref, grid_ref):
     rows, cols = own_ref.shape[1], own_ref.shape[2]
     columns, height = grid_ref.shape[1], grid_ref.shape[2]
     count = height // TILE
     own_columns = cols // LANES
-    lat_odd = lax.rem(where_ref[1], 2)
+    lat_odd = lax.rem(lax.axis_index("lat"), 2)
     near_row = rows + pl.multiple_of(lat_odd * HALO, HALO)
     far_row = rows + pl.multiple_of((1 - lat_odd) * HALO, HALO)
     edge = FIELDS * cols + LANES
@@ -179,7 +189,7 @@
     for first, at, side_ref, bodies in parts:
         west = side_ref[...]
         slot = iota(west.shape, 1) // HALO
-        lat_index = where_ref[1]
+        lat_index = lax.axis_index("lat")
         outside = jnp.broadcast_to((lat_index == 0) | (lat_index == lat_count - 1), west.shape)
         for f, body in enumerate(bodies):
             for c in range(own_columns):
@@ -208,10 +218,10 @@
     return faces(depth, across, along) + (source_term, source)
 
 
-def hold(lat_count, where_ref, own_ref, lat_near_ref, lat_far_ref, west_ref, west_far_ref, east_ref, scale_ref, *rest):
+def hold(lat_count, own_ref, lat_near_ref, lat_far_ref, west_ref, west_far_ref, east_ref, scale_ref, *rest):
     level_refs = [rest[5 * i : 5 * i + 5] for i in range(LEVELS)]
     diagonal_ref, grid_ref = rest[5 * LEVELS :]
-    state = lay_out(lat_count, where_ref, own_ref, lat_near_ref, lat_far_ref, west_ref, west_far_ref, east_ref, scale_ref,
+    state = lay_out(lat_count, own_ref, lat_near_ref, lat_far_ref, west_ref, west_far_ref, east_ref, scale_ref,
                     grid_ref)
     for level in range(LEVELS):
         kept, state = level_down(level, *state)
@@ -221,12 +231,18 @@
             keep(diagonal_ref, kept[-1])
 
 
-def descend(lat_count, where_ref, own_ref, lat_near_ref, lat_far_ref, west_ref, west_far_ref, scale_ref, pack_ref, grid_ref):
-    lon_index = where_ref[0]
+def descend(lat_count, own_ref, lat_near_ref, lat_far_ref, west_ref, west_far_ref, west_edge_ref, scale_ref,
+            pack_ref, edge_ref, grid_ref):
+    rows = own_ref.shape[1]
+    edge = slice(FIELDS * own_ref.shape[2], FIELDS * own_ref.shape[2] + LANES)
+    edge_ref[pl.ds(0, rows), :] = west_edge_ref[...]
+    edge_ref[pl.ds(rows, HALO), :] = lat_near_ref[:, edge]
+    edge_ref[pl.ds(rows + HALO, HALO), :] = lat_far_ref[:, edge]
+    lon_index = lax.axis_index("lon")
     cols = own_ref.shape[2]
     own_columns = cols // LANES
     columns = grid_ref.shape[1]
-    state = lay_out(lat_count, where_ref, own_ref, lat_near_ref, lat_far_ref, west_ref, west_far_ref, None, scale_ref,
+    state = lay_out(lat_count, own_ref, lat_near_ref, lat_far_ref, west_ref, west_far_ref, None, scale_ref,
                     grid_ref)
     for level in range(LEVELS):
         _, state = level_down(level, *state)
@@ -301,11 +317,11 @@
     return iterate
 
 
-def ascend(lat_count, lon_count, where_ref, blocks_ref, *rest):
+def ascend(lat_count, lon_count, blocks_ref, *rest):
     level_refs = [rest[5 * i : 5 * i + 5] for i in range(LEVELS)]
-    diagonal_ref, solution_ref, residual_ref, window_ref, turn_ref, order_ref = rest[5 * LEVELS :]
-    lon_index = where_ref[0]
-    lat_index = where_ref[1]
+    diagonal_ref, solution_ref, residual_ref, window_ref, turn_ref, order_ref, sems = rest[5 * LEVELS :]
+    lon_index = lax.axis_index("lon")
+    lat_index = lax.axis_index("lat")
     rows, cols = solution_ref.shape
     count, width = diagonal_ref.shape[0], diagonal_ref.shape[2]
     own_columns = cols // LANES
@@ -374,14 +390,23 @@
         for _ in range(SWEEPS):
             field = sweep(field, source, inverse, east_face, north_face, stride)
         correction = field
-    final = remainder(correction, source, tiles_of(diagonal_ref), east_face, north_face, 1)
     own_sublanes = rows // count
-    for k, (ref, value) in enumerate(((solution_ref, correction), (residual_ref, final))):
+
+    def send_out(k, ref, tiles):
+        copies = []
         for c in range(own_columns):
             part = slice(c * LANES, (c + 1) * LANES)
             for t in range(count):
-                order_ref[k, c, pl.ds(t, own_sublanes, stride=count), :] = value[t][:own_sublanes, part]
-            ref[:, part] = order_ref[k, c]
+                order_ref[k, c, pl.ds(t, own_sublanes, stride=count), :] = tiles[t][:own_sublanes, part]
+            copies.append(pltpu.make_async_copy(order_ref.at[k, c], ref.at[:, part], sems.at[k, c]))
+            copies[-1].start()
+        return copies
+
+    copies = send_out(0, solution_ref, correction)
+    final = remainder(correction, source, tiles_of(diagonal_ref), east_face, north_face, 1)
+    copies += send_out(1, residual_ref, final)
+    for copy in copies:
+        copy.wait()
 
 
 def swap_pairs(count, first):
@@ -397,28 +422,22 @@
     height, width = rows + 2 * HALO, cols + LANES
     count = height // TILE
     f32 = jnp.float32
-    smem = pl.BlockSpec(memory_space=pltpu.SMEM)
     vmem = pl.BlockSpec(memory_space=pltpu.VMEM)
     hbm = pl.BlockSpec(memory_space=pltpu.HBM)
     params = pltpu.CompilerParams(vmem_limit_bytes=VMEM_LIMIT)
-    lon_index = lax.axis_index("lon").astype(jnp.int32)
     lat_index = lax.axis_index("lat").astype(jnp.int32)
-    where = jnp.stack([lon_index, lat_index])
     inputs = [
         pltpu.with_memory_space_constraint(x, pltpu.HBM) for x in (forcing, surface_term, sea_cells, levels)
     ]
-    own, east_edge, west_edge, lat_near, lat_far, diagonal_edge = pl.pallas_call(
+    own, east_edge, west_edge = pl.pallas_call(
         prepare,
         out_shape=[
             jax.ShapeDtypeStruct((FIELDS, rows, cols), f32),
             jax.ShapeDtypeStruct((rows, LANES), f32),
             jax.ShapeDtypeStruct((rows, LANES), f32),
-            jax.ShapeDtypeStruct((HALO, FIELDS * cols + LANES), f32),
-            jax.ShapeDtypeStruct((HALO, FIELDS * cols + LANES), f32),
-            jax.ShapeDtypeStruct((HALO, LANES), f32),
         ],
-        in_specs=[smem] + [hbm] * 4,
-        out_specs=[vmem] * 6,
+        in_specs=[hbm] * 4,
+        out_specs=[vmem] * 3,
         scratch_shapes=[
             pltpu.VMEM((rows, cols), f32),
             pltpu.VMEM((rows, cols), f32),
@@ -428,7 +447,24 @@
         ],
         compiler_params=params,
         name="prepare",
-    )(where, *inputs)
+    )(*inputs)
+
+    diagonal_edge = pl.pallas_call(
+        prepare_corner,
+        out_shape=jax.ShapeDtypeStruct((HALO, LANES), f32),
+        in_specs=[vmem],
+        out_specs=vmem,
+        compiler_params=params,
+        name="prepare_corner",
+    )(east_edge)
+    lat_near, lat_far = pl.pallas_call(
+        prepare_rows,
+        out_shape=[jax.ShapeDtypeStruct((HALO, FIELDS * cols + LANES), f32)] * 2,
+        in_specs=[vmem] * 2,
+        out_specs=[vmem] * 2,
+        compiler_params=params,
+        name="prepare_rows",
+    )(own, west_edge)
 
     eastward = [(i, (i + 1) % lon_count) for i in range(lon_count)]
     westward = [(target, source) for source, target in eastward]
@@ -445,12 +481,6 @@
         "lat",
         near_pairs,
     )
-    edge = FIELDS * cols
-    east_halo = lax.ppermute(
-        jnp.concatenate([west_edge, lat_near[:, edge : edge + LANES], lat_far[:, edge : edge + LANES]], axis=0),
-        "lon",
-        westward,
-    )
 
     row = jnp.arange(TILE)[None, :] * count + jnp.arange(count)[:, None]
     row = jnp.where(row < rows + HALO, row, row - height).astype(f32) + (lat_index * rows).astype(f32)
@@ -459,15 +489,19 @@
 
     devices = lat_count * lon_count
     grid = pltpu.VMEM((FIELDS, width // LANES, height, LANES), f32)
-    packed = pl.pallas_call(
+    packed, edges = pl.pallas_call(
         functools.partial(descend, lat_count),
-        out_shape=jax.ShapeDtypeStruct((devices, rows >> LEVELS, LANES), f32),
-        in_specs=[smem] + [vmem] * 6,
-        out_specs=vmem,
+        out_shape=[
+            jax.ShapeDtypeStruct((devices, rows >> LEVELS, LANES), f32),
+            jax.ShapeDtypeStruct((height, LANES), f32),
+        ],
+        in_specs=[vmem] * 7,
+        out_specs=[vmem] * 2,
         scratch_shapes=[grid],
         compiler_params=params,
         name="descend",
-    )(where, own, lat_near, lat_far, west_halo, west_far, scale)
+    )(own, lat_near, lat_far, west_halo, west_far, west_edge, scale)
+    east_halo = lax.ppermute(edges, "lon", westward)
     blocks = lax.all_to_all(packed, ("lon", "lat"), 0, 0, tiled=True)
 
     level_shapes = []
@@ -476,27 +510,28 @@
     held = pl.pallas_call(
         functools.partial(hold, lat_count),
         out_shape=level_shapes + [jax.ShapeDtypeStruct((count, TILE, width), f32)],
-        in_specs=[smem] + [vmem] * 7,
+        in_specs=[vmem] * 7,
         out_specs=[vmem] * (1 + len(level_shapes)),
         scratch_shapes=[grid],
         compiler_params=params,
         cost_estimate=pl.CostEstimate(flops=0, bytes_accessed=60 * 1024 * 1024, transcendentals=0),
         name="hold",
-    )(where, own, lat_near, lat_far, west_halo, west_far, east_halo, scale)
+    )(own, lat_near, lat_far, west_halo, west_far, east_halo, scale)
 
     return pl.pallas_call(
         functools.partial(ascend, lat_count, lon_count),
         out_shape=[jax.ShapeDtypeStruct((rows, cols), f32)] * 2,
-        in_specs=[smem] + [vmem] * (1 + len(held)),
-        out_specs=[vmem] * 2,
+        in_specs=[vmem] * (1 + len(held)),
+        out_specs=[hbm] * 2,
         scratch_shapes=[
             pltpu.VMEM((lat_count * (rows >> LEVELS) + 4 * TILE, LANES), f32),
             pltpu.VMEM((5 * TILE, LANES), f32),
             pltpu.VMEM((2, cols // LANES, rows, LANES), f32),
+            pltpu.SemaphoreType.DMA((2, cols // LANES)),
         ],
         compiler_params=params,
         name="ascend",
-    )(where, blocks, *held)
+    )(blocks, *held)
 
 
 def solution(mesh):

time: 32 us -> 29 us (0.906)
  Pallas kernels: 9.32 us -> 7.16 us
  local copies, waits for them, and re-layouts: 0.86 us -> 0.16 us
    slice x3 -> x0, local copies, waits for them, and re-layouts: 0.69 us -> none  [the longest x2 0.69 us: on_device(): lat_far[:, edge:edge + LANES]]
    all_to_all x1, waiting for transfers between devices: 0.01 us -> 0.63 us  [on_device(): blocks = lax.all_to_all(packed, ('lon', 'lat'), 0, 0, tiled=True)]
    ppermute x1, waiting for transfers between devices: 2.16 us -> 1.55 us  [on_device(): west_far = lax.ppermute(diagonal_edge, ('lon', 'lat'), across_pairs)]
    pallas_call x1, Pallas kernels: 1.63 us -> 1.08 us  [on_device(): pl.pallas_call(functools.partial(hold, lat_count), out_shape=level_shapes...]
    pallas_call x1 -> x3, Pallas kernels: 2.52 us -> 1.97 us  [the longest x1 1.94 us: on_device(): pl.pallas_call(functools.partial(descend, lat_count), out_shape=[jax.Shap...]
    pallas_call x1, Pallas kernels: 1.61 us -> 1.07 us  [on_device(): pl.pallas_call(prepare, out_shape=[jax.ShapeDtypeStruct((FIELDS, rows, co...]
    pallas_call x1, Pallas kernels: 3.57 us -> 3.03 us  [on_device(): pl.pallas_call(functools.partial(ascend, lat_count, lon_count), out_shape...]
    ppermute x1, starting transfers between devices: 0.65 us -> 1.16 us  [on_device(): lat_far = lax.ppermute(lat_far, 'lat', far_pairs)]
  transfers between devices with their start and end apart: 6 -> 6, of which waited for: 3 -> 4; matrix products, arithmetic and copies ran while one was open for 1% -> 1% of each run, Pallas kernels for 5% -> 4%
where the time goes in v4:
time: 29 us; the launch traced here: 28.8 us
  starting transfers between devices  14.4 us (50%)
  Pallas kernels  7.16 us (25%)
  waiting for transfers between devices  6.22 us (21%)
  between operations  0.69 us (2%)
    ppermute x1, starting transfers between devices, on_device(): east_halo = lax.ppermute(edges, 'lon', westward)  4.6 us
    all_to_all x1, starting transfers between devices, on_device(): blocks = lax.all_to_all(packed, ('lon', 'lat'), 0, 0, tiled=True)  3.98 us
    pallas_call x1, Pallas kernels, on_device(): pl.pallas_call(functools.partial(ascend, lat_count, lon_count), out_shape...  3.03 us
    ppermute x1, starting transfers between devices, on_device(): west_halo = lax.ppermute(east_edge, 'lon', eastward)  3.02 us
    ppermute x1, waiting for transfers between devices, on_device(): west_halo = lax.ppermute(east_edge, 'lon', eastward)  2.13 us
    pallas_call x1, Pallas kernels, on_device(): pl.pallas_call(functools.partial(descend, lat_count), out_shape=[jax.Shap...  1.94 us
    ppermute x1, waiting for transfers between devices, on_device(): east_halo = lax.ppermute(edges, 'lon', westward)  1.91 us
    ppermute x1, starting transfers between devices, on_device(): west_far = lax.ppermute(diagonal_edge, ('lon', 'lat'), across_pairs)  1.61 us
  transfers between devices with their start and end apart: 6, of which 4 were waited for; matrix products, arithmetic and copies ran while one was open for 1% of the time, Pallas kernels for 4%

profile of v4, /device:TPU:0, one launch (start us, length us, event | category | flops | bytes accessed | tf_op | source)
XLA Modules:
  0.0 28.8 jit_solution(7555040072662541341)
XLA Ops:
  0.6 1.1 %prepare.1 = (f32[3,64,256]{2,1,0:T(8,128)S(1)}, f32[64,128]{1,0:T(8,128)S(1)}, f32[64,128]{1,0:T(8,128)S(1)}) custom-call(f32[64,256]{1,0:T(8,128)} %forcing_ref.1, f32[64,256]{1,0:T(8,128)} %surface_ref.1, s32[64,256]{1,0:T(8,128)} %sea_ref.1, s32[64,256]{1,0:T(8,128)} %levels_ref.1), custom_call_target="tpu_custom_call" | custom-call | tf_op jit(solution)/shard_map/prepare/pallas_call | solution.py:432
  1.7 3.0 %collective-permute-start = (f32[64,128]{1,0:T(8,128)S(1)}, f32[64,128]{1,0:T(8,128)S(1)}, u32[]{:S(2)}, u32[]{:S(2)}) collective-permute-start(f32[64,128]{1,0:T(8,128)S(1)} %get-tuple-element.28.east_edge_ref), channel_id=1, source_target_pairs={{0,4},{4,8},{8,12},{12,16},{16,20},{20,24},{24,28},{28,0},{1,5},{5... | collective-permute-start | bytes 98312 | tf_op jit(solution)/shard_map/ppermute | solution.py:475
  4.7 1.6 %collective-permute-start.3 = (f32[32,128]{1,0:T(8,128)S(1)}, f32[32,128]{1,0:T(8,128)S(1)}, u32[]{:S(2)}, u32[]{:S(2)}) collective-permute-start(f32[32,128]{1,0:T(8,128)S(1)} %prepare_corner.1), channel_id=1, source_target_pairs={{1,6},{2,5},{3,4},{0,7},{5,10},{6,9},{7,8},{4,11},{9,14},{10,13},{... | collective-permute-start | bytes 49160 | tf_op jit(solution)/shard_map/ppermute | solution.py:477
  6.4 1.2 %collective-permute-start.2 = (f32[32,896]{1,0:T(8,128)S(1)}, f32[32,896]{1,0:T(8,128)S(1)}, u32[]{:S(2)}, u32[]{:S(2)}) collective-permute-start(f32[32,896]{1,0:T(8,128)S(1)} %get-tuple-element.29), channel_id=1, source_target_pairs={{1,2},{2,1},{3,0},{0,3},{5,6},{6,5},{7,4},{4,7},{9,10},{10,9},{11,... | collective-permute-start | bytes 344072 | tf_op jit(solution)/shard_map/ppermute | solution.py:476
  7.5 2.1 %collective-permute-done.west_ref = f32[64,128]{1,0:T(8,128)S(1)} collective-permute-done((f32[64,128]{1,0:T(8,128)S(1)}, f32[64,128]{1,0:T(8,128)S(1)}, u32[]{:S(2)}, u32[]{:S(2)}) %collective-permute-start) | collective-permute-done | bytes 32800 | tf_op jit(solution)/shard_map/ppermute | solution.py:475
  9.7 0.1 collective-permute-start.1
  9.8 0.1 cosine_divide_fusion
  9.9 0.1 copy.6
  10.0 1.6 %collective-permute-done.3.west_far_ref = f32[32,128]{1,0:T(8,128)S(1)} collective-permute-done((f32[32,128]{1,0:T(8,128)S(1)}, f32[32,128]{1,0:T(8,128)S(1)}, u32[]{:S(2)}, u32[]{:S(2)}) %collective-permute-start.3) | collective-permute-done | bytes 16416 | tf_op jit(solution)/shard_map/ppermute | solution.py:477
  11.5 0.0 collective-permute-done.2.lat_far_ref
  11.5 0.0 collective-permute-done.1.lat_near_ref
  11.5 0.1 broadcast_in_dim.2.scale_ref
  11.6 1.9 %descend.1 = (f32[32,8,128]{2,1,0:T(8,128)}, f32[128,128]{1,0:T(8,128)S(1)}) custom-call(f32[3,64,256]{2,1,0:T(8,128)S(1)} %get-tuple-element.25.own_ref, f32[32,1024]{1,0:T(8,128)S(1)} %collective-permute-done.1.lat_near_ref, f32[32,896]{1,0:T(8,128)S(1)} %collective-permute-done.2.lat_far_ref, f32[64,128]{1,0:T(8,128)S(1)} %collective-permute-done.west_ref, ...), custom_call_target="tpu_custom_call" | custom-call | tf_op jit(solution)/shard_map/descend/pallas_call | solution.py:492
  13.6 4.0 %all-to-all-start = ((f32[32,8,128]{2,1,0:T(8,128)}), f32[32,8,128]{2,1,0:T(8,128)S(1)}, u32[]{:S(2)}, u32[]{:S(2)}) async-start(f32[32,8,128]{2,1,0:T(8,128)} %get-tuple-element.30), calls=%async_computation | async-start | bytes 262144 | tf_op jit(solution)/shard_map/all_to_all | solution.py:505
  17.6 4.6 %collective-permute-start.4 = (f32[128,128]{1,0:T(8,128)S(1)}, f32[128,128]{1,0:T(8,128)S(1)}, u32[]{:S(2)}, u32[]{:S(2)}) collective-permute-start(f32[128,128]{1,0:T(8,128)S(1)} %get-tuple-element.31), channel_id=1, source_target_pairs={{4,0},{8,4},{12,8},{16,12},{20,16},{24,20},{28,24},{0,28},{5,1},{9... | collective-permute-start | bytes 196616 | tf_op jit(solution)/shard_map/ppermute | solution.py:504
  22.2 1.9 %collective-permute-done.4.east_ref = f32[128,128]{1,0:T(8,128)S(1)} collective-permute-done((f32[128,128]{1,0:T(8,128)S(1)}, f32[128,128]{1,0:T(8,128)S(1)}, u32[]{:S(2)}, u32[]{:S(2)}) %collective-permute-start.4) | collective-permute-done | bytes 65568 | tf_op jit(solution)/shard_map/ppermute | solution.py:504
  24.1 1.1 %hold.1 = (f32[16,8,384]{2,1,0:T(8,128)S(1)}, f32[16,8,384]{2,1,0:T(8,128)S(1)}, f32[16,8,384]{2,1,0:T(8,128)S(1)}, f32[16,8,384]{2,1,0:T(8,128)S(1)}, f32[16,8,...) custom-call(f32[3,64,256]{2,1,0:T(8,128)S(1)} %get-tuple-element.25., ...), custom_call_target="tpu_custom_call" | custom-call | bytes 62914560 | tf_op jit(solution)/shard_map/hold/pallas_call | solution.py:510
  25.2 0.6 %all-to-all-done.blocks_ref = f32[32,8,128]{2,1,0:T(8,128)S(1)} async-done(((f32[32,8,128]{2,1,0:T(8,128)}), f32[32,8,128]{2,1,0:T(8,128)S(1)}, u32[]{:S(2)}, u32[]{:S(2)}) %all-to-all-start) | async-done | bytes 131104 | tf_op jit(solution)/shard_map/all_to_all | solution.py:505
  25.8 3.0 %ascend.1 = (f32[64,256]{1,0:T(8,128)}, f32[64,256]{1,0:T(8,128)}) custom-call(f32[32,8,128]{2,1,0:T(8,128)S(1)} %all-to-all-done.blocks_ref, f32[16,8,384]{2,1,0:T(8,128)S(1)} %get-tuple-element.32.rest_0_, f32[16,8,384]{2,1,0:T(8,128)S(1)} %get-tuple-element.33.rest_1_, f32[16,8,384]{2,1,0:T(8,128)S(1)} %get-tuple-element.34.rest_2_, ...), custom_call_target="tpu_custom_call" | custom-call | tf_op jit(solution)/shard_map/ascend/pallas_call | solution.py:521
  (6 shorter events, 0.1 us)
Async XLA Ops:
  1.7 8.0 %collective-permute-start = (f32[64,128]{1,0:T(8,128)S(1)}, f32[64,128]{1,0:T(8,128)S(1)}, u32[]{:S(2)}, u32[]{:S(2)}) collective-permute-start(f32[64,128]{1,0:T(8,128)S(1)} %get-tuple-element.28.east_edge_ref), channel_id=1, source_target_pairs={{0,4},{4,8},{8,12},{12,16},{16,20},{20,24},{24,28},{28,0},{1,5},{5... | collective-permute-start | bytes 98312 | tf_op jit(solution)/shard_map/ppermute | solution.py:475
  4.7 6.8 %collective-permute-start.3 = (f32[32,128]{1,0:T(8,128)S(1)}, f32[32,128]{1,0:T(8,128)S(1)}, u32[]{:S(2)}, u32[]{:S(2)}) collective-permute-start(f32[32,128]{1,0:T(8,128)S(1)} %prepare_corner.1), channel_id=1, source_target_pairs={{1,6},{2,5},{3,4},{0,7},{5,10},{6,9},{7,8},{4,11},{9,14},{10,13},{... | collective-permute-start | bytes 49160 | tf_op jit(solution)/shard_map/ppermute | solution.py:477
  6.4 5.2 %collective-permute-start.2 = (f32[32,896]{1,0:T(8,128)S(1)}, f32[32,896]{1,0:T(8,128)S(1)}, u32[]{:S(2)}, u32[]{:S(2)}) collective-permute-start(f32[32,896]{1,0:T(8,128)S(1)} %get-tuple-element.29), channel_id=1, source_target_pairs={{1,2},{2,1},{3,0},{0,3},{5,6},{6,5},{7,4},{4,7},{9,10},{10,9},{11,... | collective-permute-start | bytes 344072 | tf_op jit(solution)/shard_map/ppermute | solution.py:476
  9.7 1.9 %collective-permute-start.1 = (f32[32,1024]{1,0:T(8,128)S(1)}, f32[32,1024]{1,0:T(8,128)S(1)}, u32[]{:S(2)}, u32[]{:S(2)}) collective-permute-start(f32[32,1024]{1,0:T(8,128)S(1)} %pad_maximum_fusion), channel_id=1, source_target_pairs={{0,1},{1,0},{2,3},{3,2},{4,5},{5,4},{6,7},{7,6},{8,9},{9,8},{10,11... | collective-permute-start | bytes 393224 | tf_op jit(solution)/shard_map/ppermute | solution.py:479
  13.6 12.2 %all-to-all-start = ((f32[32,8,128]{2,1,0:T(8,128)}), f32[32,8,128]{2,1,0:T(8,128)S(1)}, u32[]{:S(2)}, u32[]{:S(2)}) async-start(f32[32,8,128]{2,1,0:T(8,128)} %get-tuple-element.30), calls=%async_computation | async-start | bytes 262144 | tf_op jit(solution)/shard_map/all_to_all | solution.py:505
  17.6 6.5 %collective-permute-start.4 = (f32[128,128]{1,0:T(8,128)S(1)}, f32[128,128]{1,0:T(8,128)S(1)}, u32[]{:S(2)}, u32[]{:S(2)}) collective-permute-start(f32[128,128]{1,0:T(8,128)S(1)} %get-tuple-element.31), channel_id=1, source_target_pairs={{4,0},{8,4},{12,8},{16,12},{20,16},{24,20},{28,24},{0,28},{5,1},{9... | collective-permute-start | bytes 196616 | tf_op jit(solution)/shard_map/ppermute | solution.py:504

commit v5 on v4

--- a/solution.py
+++ b/solution.py
@@ -115,7 +115,7 @@
     west_edge_ref[...] = west_edge
 
 
-def prepare_corner(east_edge_ref, diagonal_edge_ref):
+def prepare_corner(east_edge_ref, rows_ref, diagonal_edge_ref):
     rows = east_edge_ref.shape[0]
     odd = jnp.broadcast_to(lax.rem(lax.axis_index("lat"), 2), diagonal_edge_ref.shape) > 0
     diagonal_edge_ref[...] = jnp.where(odd, east_edge_ref[pl.ds(rows - HALO, HALO), :], east_edge_ref[pl.ds(0, HALO), :])
@@ -294,32 +294,46 @@
     def down(value):
         return pltpu.roll(value, 1, 0)
 
-    diagonal = source_term + (
-        (east_face + lane_shift(east_face, -1)) + (north_face + down(north_face))
-    )
+    west_face = lane_shift(east_face, -1)
+    south_face = down(north_face)
+    diagonal = source_term + ((east_face + west_face) + (north_face + south_face))
+
+    def apply(value):
+        return diagonal * value - (
+            (east_face * lane_shift(value, 1) + west_face * lane_shift(value, -1))
+            + (north_face * up(value) + south_face * down(value))
+        )
+
     iterate = jnp.zeros_like(source)
     remain = source
-    direction = source
-    for _ in range(BOTTOM_ITERS):
-        image = diagonal * direction - (
-            (east_face * lane_shift(direction, 1) + lane_shift(east_face * direction, -1))
-            + (north_face * up(direction) + down(north_face * direction))
-        )
-        norm = total_of(split(remain * remain))
-        energy = total_of(split(direction * image))
-        cross = total_of(split(remain * image))
-        square = total_of(split(image * image))
-        step_size = norm / energy
+    image_r = apply(source)
+    direction = image_d = second = step_size = norm = None
+    for step in range(BOTTOM_ITERS):
+        norm_now = total_of(split(remain * remain))
+        energy = total_of(split(remain * image_r))
+        last = step == BOTTOM_ITERS - 1
+        ahead = None if last else apply(image_r)
+        if step == 0:
+            step_size = norm_now / energy
+            direction, image_d, second = remain, image_r, ahead
+        else:
+            ratio = norm_now / norm
+            step_size = norm_now / (energy - ratio * (norm_now / step_size))
+            direction = remain + ratio * direction
+            if not last:
+                image_d = image_r + ratio * image_d
+                second = ahead + ratio * second
+        norm = norm_now
         iterate = iterate + step_size * direction
-        remain = remain - step_size * image
-        norm_next = norm - step_size * (2.0 * cross - step_size * square)
-        direction = remain + (norm_next / norm) * direction
+        if not last:
+            remain = remain - step_size * image_d
+            image_r = image_r - step_size * second
     return iterate
 
 
 def ascend(lat_count, lon_count, blocks_ref, *rest):
     level_refs = [rest[5 * i : 5 * i + 5] for i in range(LEVELS)]
-    diagonal_ref, solution_ref, residual_ref, window_ref, turn_ref, order_ref, sems = rest[5 * LEVELS :]
+    diagonal_ref, solution_ref, residual_ref, window_ref, order_ref, sems = rest[5 * LEVELS :]
     lon_index = lax.axis_index("lon")
     lat_index = lax.axis_index("lat")
     rows, cols = solution_ref.shape
@@ -356,15 +370,14 @@
     shift = lax.rem(margin - SHIFT - lon_index * bottom_width + whole_width, whole_width)
     window_ref[pl.ds(pad, bottom_height), :] = pltpu.roll(iterate, shift, 1)[:, :LANES]
     start = pl.multiple_of(lat_index * bottom_rows, TILE)
-    turn_ref[...] = window_ref[pl.ds(start, 5 * TILE), :]
     tiles = count >> LEVELS
     lane = iota((TILE, LANES), 1)
     ahead = (rows + HALO) // stride // tiles
     sublane = iota((TILE, LANES), 0)
     correction = []
     for t in range(tiles):
-        upper = turn_ref[pl.ds(pad + t, TILE, stride=tiles), :]
-        lower = turn_ref[pl.ds(pad + t - tiles * TILE, TILE, stride=tiles), :]
+        upper = window_ref[pl.ds(start + pad + t, TILE, stride=tiles), :]
+        lower = window_ref[pl.ds(start + pad + t - tiles * TILE, TILE, stride=tiles), :]
         value = jnp.where(sublane < ahead, upper, lower)
         parts = []
         for c in range(columns):
@@ -409,11 +422,19 @@
         copy.wait()
 
 
-def swap_pairs(count, first):
+def near_pairs(lat_count):
+    return [(a, a ^ 1) for a in range(lat_count)]
+
+
+def far_pairs(lon_count, lat_count, east):
     pairs = []
-    for i in range(first, count, 2):
-        j = (i + 1) % count
-        pairs += [(i, j), (j, i)]
+    for i in range(lon_count):
+        for a in range(lat_count):
+            b = a + 1 if a % 2 else a - 1
+            j = (i + east) % lon_count
+            if b < 0 or b == lat_count:
+                b, j = a, i ^ 1
+            pairs.append((i * lat_count + a, j * lat_count + b))
     return pairs
 
 
@@ -449,14 +470,6 @@
         name="prepare",
     )(*inputs)
 
-    diagonal_edge = pl.pallas_call(
-        prepare_corner,
-        out_shape=jax.ShapeDtypeStruct((HALO, LANES), f32),
-        in_specs=[vmem],
-        out_specs=vmem,
-        compiler_params=params,
-        name="prepare_corner",
-    )(east_edge)
     lat_near, lat_far = pl.pallas_call(
         prepare_rows,
         out_shape=[jax.ShapeDtypeStruct((HALO, FIELDS * cols + LANES), f32)] * 2,
@@ -466,20 +479,24 @@
         name="prepare_rows",
     )(own, west_edge)
 
+    diagonal_edge = pl.pallas_call(
+        prepare_corner,
+        out_shape=jax.ShapeDtypeStruct((HALO, LANES), f32),
+        in_specs=[vmem] * 2,
+        out_specs=vmem,
+        compiler_params=params,
+        name="prepare_corner",
+    )(east_edge, lat_far)
     eastward = [(i, (i + 1) % lon_count) for i in range(lon_count)]
     westward = [(target, source) for source, target in eastward]
-    near_pairs, far_pairs = swap_pairs(lat_count, 0), swap_pairs(lat_count, 1)
-    across_pairs = [
-        (i * lat_count + a, (i + 1) % lon_count * lat_count + b) for i in range(lon_count) for a, b in far_pairs
-    ]
     west_halo = lax.ppermute(east_edge, "lon", eastward)
-    lat_far = lax.ppermute(lat_far, "lat", far_pairs)
-    west_far = lax.ppermute(diagonal_edge, ("lon", "lat"), across_pairs)
+    lat_far = lax.ppermute(lat_far, ("lon", "lat"), far_pairs(lon_count, lat_count, 0))
+    west_far = lax.ppermute(diagonal_edge, ("lon", "lat"), far_pairs(lon_count, lat_count, 1))
     odd = lat_index % 2 == 1
     lat_near = lax.ppermute(
         jnp.concatenate([lat_near, jnp.where(odd, west_halo[:HALO], west_halo[rows - HALO :])], axis=1),
         "lat",
-        near_pairs,
+        near_pairs(lat_count),
     )
 
     row = jnp.arange(TILE)[None, :] * count + jnp.arange(count)[:, None]
@@ -525,7 +542,6 @@
         out_specs=[hbm] * 2,
         scratch_shapes=[
             pltpu.VMEM((lat_count * (rows >> LEVELS) + 4 * TILE, LANES), f32),
-            pltpu.VMEM((5 * TILE, LANES), f32),
             pltpu.VMEM((2, cols // LANES, rows, LANES), f32),
             pltpu.SemaphoreType.DMA((2, cols // LANES)),
         ],

time: 29 us -> 28.2 us (0.972)
  starting transfers between devices: 14.4 us -> 13.7 us
  Pallas kernels: 7.16 us -> 6.79 us
    ppermute x2, waiting for transfers between devices: 1.55 us -> 0.48 us  [the longest x1 0.48 us: on_device(): lax.ppermute(diagonal_edge, ('lon', 'lat'), far_pairs(lon_count, lat_coun...]
    ppermute x1, waiting for transfers between devices: 2.13 us -> 2.84 us  [on_device(): west_halo = lax.ppermute(east_edge, 'lon', eastward)]
    ppermute x2, starting transfers between devices: 2.77 us -> 2.09 us  [the longest x1 1.58 us: on_device(): lax.ppermute(lat_far, ('lon', 'lat'), far_pairs(lon_count, lat_count, 0))]
    ppermute x1, waiting for transfers between devices: 0.01 us -> 0.64 us  [on_device(): lax.ppermute(jnp.concatenate([lat_near, jnp.where(odd, west_halo[:HALO],...]
    pallas_call x1, Pallas kernels: 3.03 us -> 2.66 us  [on_device(): pl.pallas_call(functools.partial(ascend, lat_count, lon_count), out_shape...]
  transfers between devices with their start and end apart: 6 -> 6, of which waited for: 4 -> 5; matrix products, arithmetic and copies ran while one was open for 1% -> 1% of each run, Pallas kernels for 4% -> 4%
where the time goes in v5:
time: 28.2 us; the launch traced here: 28 us
  starting transfers between devices  13.7 us (49%)
  Pallas kernels  6.79 us (24%)
  waiting for transfers between devices  6.49 us (23%)
  between operations  0.69 us (2%)
    ppermute x1, starting transfers between devices, on_device(): east_halo = lax.ppermute(edges, 'lon', westward)  4.6 us
    all_to_all x1, starting transfers between devices, on_device(): blocks = lax.all_to_all(packed, ('lon', 'lat'), 0, 0, tiled=True)  3.88 us
    ppermute x1, starting transfers between devices, on_device(): west_halo = lax.ppermute(east_edge, 'lon', eastward)  3.02 us
    ppermute x1, waiting for transfers between devices, on_device(): west_halo = lax.ppermute(east_edge, 'lon', eastward)  2.84 us
    pallas_call x1, Pallas kernels, on_device(): pl.pallas_call(functools.partial(ascend, lat_count, lon_count), out_shape...  2.66 us
    pallas_call x1, Pallas kernels, on_device(): pl.pallas_call(functools.partial(descend, lat_count), out_shape=[jax.Shap...  1.94 us
    ppermute x1, waiting for transfers between devices, on_device(): east_halo = lax.ppermute(edges, 'lon', westward)  1.91 us
    ppermute x1, starting transfers between devices, on_device(): lax.ppermute(lat_far, ('lon', 'lat'), far_pairs(lon_count, lat_count, 0))  1.58 us
  transfers between devices with their start and end apart: 6, of which 5 were waited for; matrix products, arithmetic and copies ran while one was open for 1% of the time, Pallas kernels for 4%

profile of v5, /device:TPU:0, one launch (start us, length us, event | category | flops | bytes accessed | tf_op | source)
XLA Modules:
  0.0 28.0 jit_solution(3967069345287815382)
XLA Ops:
  0.6 1.1 %prepare.1 = (f32[3,64,256]{2,1,0:T(8,128)S(1)}, f32[64,128]{1,0:T(8,128)S(1)}, f32[64,128]{1,0:T(8,128)S(1)}) custom-call(f32[64,256]{1,0:T(8,128)} %forcing_ref.1, f32[64,256]{1,0:T(8,128)} %surface_ref.1, s32[64,256]{1,0:T(8,128)} %sea_ref.1, s32[64,256]{1,0:T(8,128)} %levels_ref.1), custom_call_target="tpu_custom_call" | custom-call | tf_op jit(solution)/shard_map/prepare/pallas_call | solution.py:453
  1.7 3.0 %collective-permute-start = (f32[64,128]{1,0:T(8,128)S(1)}, f32[64,128]{1,0:T(8,128)S(1)}, u32[]{:S(2)}, u32[]{:S(2)}) collective-permute-start(f32[64,128]{1,0:T(8,128)S(1)} %get-tuple-element.28.east_edge_ref), channel_id=1, source_target_pairs={{0,4},{4,8},{8,12},{12,16},{16,20},{20,24},{24,28},{28,0},{1,5},{5... | collective-permute-start | bytes 98312 | tf_op jit(solution)/shard_map/ppermute | solution.py:492
  4.8 1.6 %collective-permute-start.2 = (f32[32,896]{1,0:T(8,128)S(1)}, f32[32,896]{1,0:T(8,128)S(1)}, u32[]{:S(2)}, u32[]{:S(2)}) collective-permute-start(f32[32,896]{1,0:T(8,128)S(1)} %get-tuple-element.29.rows_ref), channel_id=1, source_target_pairs={{0,4},{1,2},{2,1},{3,7},{4,0},{5,6},{6,5},{7,3},{8,12},{9,10},{10,... | collective-permute-start | bytes 344072 | tf_op jit(solution)/shard_map/ppermute | solution.py:493
  6.3 0.5 %collective-permute-start.3 = (f32[32,128]{1,0:T(8,128)S(1)}, f32[32,128]{1,0:T(8,128)S(1)}, u32[]{:S(2)}, u32[]{:S(2)}) collective-permute-start(f32[32,128]{1,0:T(8,128)S(1)} %prepare_corner.1), channel_id=1, source_target_pairs={{0,4},{1,6},{2,5},{3,7},{4,0},{5,10},{6,9},{7,3},{8,12},{9,14},{10... | collective-permute-start | bytes 49160 | tf_op jit(solution)/shard_map/ppermute | solution.py:494
  6.9 2.8 %collective-permute-done.west_ref = f32[64,128]{1,0:T(8,128)S(1)} collective-permute-done((f32[64,128]{1,0:T(8,128)S(1)}, f32[64,128]{1,0:T(8,128)S(1)}, u32[]{:S(2)}, u32[]{:S(2)}) %collective-permute-start) | collective-permute-done | bytes 32800 | tf_op jit(solution)/shard_map/ppermute | solution.py:492
  9.7 0.1 collective-permute-start.1
  9.8 0.1 cosine_divide_fusion
  9.9 0.1 copy.6
  10.0 0.5 %collective-permute-done.3.west_far_ref = f32[32,128]{1,0:T(8,128)S(1)} collective-permute-done((f32[32,128]{1,0:T(8,128)S(1)}, f32[32,128]{1,0:T(8,128)S(1)}, u32[]{:S(2)}, u32[]{:S(2)}) %collective-permute-start.3) | collective-permute-done | bytes 16416 | tf_op jit(solution)/shard_map/ppermute | solution.py:494
  10.5 0.0 collective-permute-done.2.lat_far_ref
  10.5 0.6 %collective-permute-done.1.lat_near_ref = f32[32,1024]{1,0:T(8,128)S(1)} collective-permute-done((f32[32,1024]{1,0:T(8,128)S(1)}, f32[32,1024]{1,0:T(8,128)S(1)}, u32[]{:S(2)}, u32[]{:S(2)}) %collective-permute-start.1) | collective-permute-done | bytes 131104 | tf_op jit(solution)/shard_map/ppermute | solution.py:496
  11.1 0.1 broadcast_in_dim.2.scale_ref
  11.2 1.9 %descend.1 = (f32[32,8,128]{2,1,0:T(8,128)}, f32[128,128]{1,0:T(8,128)S(1)}) custom-call(f32[3,64,256]{2,1,0:T(8,128)S(1)} %get-tuple-element.25.own_ref, f32[32,1024]{1,0:T(8,128)S(1)} %collective-permute-done.1.lat_near_ref, f32[32,896]{1,0:T(8,128)S(1)} %collective-permute-done.2.lat_far_ref, f32[64,128]{1,0:T(8,128)S(1)} %collective-permute-done.west_ref, ...), custom_call_target="tpu_custom_call" | custom-call | tf_op jit(solution)/shard_map/descend/pallas_call | solution.py:509
  13.2 3.9 %all-to-all-start = ((f32[32,8,128]{2,1,0:T(8,128)}), f32[32,8,128]{2,1,0:T(8,128)S(1)}, u32[]{:S(2)}, u32[]{:S(2)}) async-start(f32[32,8,128]{2,1,0:T(8,128)} %get-tuple-element.30), calls=%async_computation | async-start | bytes 262144 | tf_op jit(solution)/shard_map/all_to_all | solution.py:522
  17.1 4.6 %collective-permute-start.4 = (f32[128,128]{1,0:T(8,128)S(1)}, f32[128,128]{1,0:T(8,128)S(1)}, u32[]{:S(2)}, u32[]{:S(2)}) collective-permute-start(f32[128,128]{1,0:T(8,128)S(1)} %get-tuple-element.31), channel_id=1, source_target_pairs={{4,0},{8,4},{12,8},{16,12},{20,16},{24,20},{28,24},{0,28},{5,1},{9... | collective-permute-start | bytes 196616 | tf_op jit(solution)/shard_map/ppermute | solution.py:521
  21.7 1.9 %collective-permute-done.4.east_ref = f32[128,128]{1,0:T(8,128)S(1)} collective-permute-done((f32[128,128]{1,0:T(8,128)S(1)}, f32[128,128]{1,0:T(8,128)S(1)}, u32[]{:S(2)}, u32[]{:S(2)}) %collective-permute-start.4) | collective-permute-done | bytes 65568 | tf_op jit(solution)/shard_map/ppermute | solution.py:521
  23.6 1.1 %hold.1 = (f32[16,8,384]{2,1,0:T(8,128)S(1)}, f32[16,8,384]{2,1,0:T(8,128)S(1)}, f32[16,8,384]{2,1,0:T(8,128)S(1)}, f32[16,8,384]{2,1,0:T(8,128)S(1)}, f32[16,8,...) custom-call(f32[3,64,256]{2,1,0:T(8,128)S(1)} %get-tuple-element.25., ...), custom_call_target="tpu_custom_call" | custom-call | bytes 62914560 | tf_op jit(solution)/shard_map/hold/pallas_call | solution.py:527
  24.7 0.6 %all-to-all-done.blocks_ref = f32[32,8,128]{2,1,0:T(8,128)S(1)} async-done(((f32[32,8,128]{2,1,0:T(8,128)}), f32[32,8,128]{2,1,0:T(8,128)S(1)}, u32[]{:S(2)}, u32[]{:S(2)}) %all-to-all-start) | async-done | bytes 131104 | tf_op jit(solution)/shard_map/all_to_all | solution.py:522
  25.3 2.7 %ascend.1 = (f32[64,256]{1,0:T(8,128)}, f32[64,256]{1,0:T(8,128)}) custom-call(f32[32,8,128]{2,1,0:T(8,128)S(1)} %all-to-all-done.blocks_ref, f32[16,8,384]{2,1,0:T(8,128)S(1)} %get-tuple-element.32.rest_0_, f32[16,8,384]{2,1,0:T(8,128)S(1)} %get-tuple-element.33.rest_1_, f32[16,8,384]{2,1,0:T(8,128)S(1)} %get-tuple-element.34.rest_2_, ...), custom_call_target="tpu_custom_call" | custom-call | tf_op jit(solution)/shard_map/ascend/pallas_call | solution.py:538
  (6 shorter events, 0.1 us)
Async XLA Ops:
  1.7 8.0 %collective-permute-start = (f32[64,128]{1,0:T(8,128)S(1)}, f32[64,128]{1,0:T(8,128)S(1)}, u32[]{:S(2)}, u32[]{:S(2)}) collective-permute-start(f32[64,128]{1,0:T(8,128)S(1)} %get-tuple-element.28.east_edge_ref), channel_id=1, source_target_pairs={{0,4},{4,8},{8,12},{12,16},{16,20},{20,24},{24,28},{28,0},{1,5},{5... | collective-permute-start | bytes 98312 | tf_op jit(solution)/shard_map/ppermute | solution.py:492
  4.8 5.7 %collective-permute-start.2 = (f32[32,896]{1,0:T(8,128)S(1)}, f32[32,896]{1,0:T(8,128)S(1)}, u32[]{:S(2)}, u32[]{:S(2)}) collective-permute-start(f32[32,896]{1,0:T(8,128)S(1)} %get-tuple-element.29.rows_ref), channel_id=1, source_target_pairs={{0,4},{1,2},{2,1},{3,7},{4,0},{5,6},{6,5},{7,3},{8,12},{9,10},{10,... | collective-permute-start | bytes 344072 | tf_op jit(solution)/shard_map/ppermute | solution.py:493
  6.3 4.1 %collective-permute-start.3 = (f32[32,128]{1,0:T(8,128)S(1)}, f32[32,128]{1,0:T(8,128)S(1)}, u32[]{:S(2)}, u32[]{:S(2)}) collective-permute-start(f32[32,128]{1,0:T(8,128)S(1)} %prepare_corner.1), channel_id=1, source_target_pairs={{0,4},{1,6},{2,5},{3,7},{4,0},{5,10},{6,9},{7,3},{8,12},{9,14},{10... | collective-permute-start | bytes 49160 | tf_op jit(solution)/shard_map/ppermute | solution.py:494
  9.7 1.4 %collective-permute-start.1 = (f32[32,1024]{1,0:T(8,128)S(1)}, f32[32,1024]{1,0:T(8,128)S(1)}, u32[]{:S(2)}, u32[]{:S(2)}) collective-permute-start(f32[32,1024]{1,0:T(8,128)S(1)} %pad_maximum_fusion), channel_id=1, source_target_pairs={{0,1},{1,0},{2,3},{3,2},{4,5},{5,4},{6,7},{7,6},{8,9},{9,8},{10,11... | collective-permute-start | bytes 393224 | tf_op jit(solution)/shard_map/ppermute | solution.py:496
  13.2 12.1 %all-to-all-start = ((f32[32,8,128]{2,1,0:T(8,128)}), f32[32,8,128]{2,1,0:T(8,128)S(1)}, u32[]{:S(2)}, u32[]{:S(2)}) async-start(f32[32,8,128]{2,1,0:T(8,128)} %get-tuple-element.30), calls=%async_computation | async-start | bytes 262144 | tf_op jit(solution)/shard_map/all_to_all | solution.py:522
  17.1 6.5 %collective-permute-start.4 = (f32[128,128]{1,0:T(8,128)S(1)}, f32[128,128]{1,0:T(8,128)S(1)}, u32[]{:S(2)}, u32[]{:S(2)}) collective-permute-start(f32[128,128]{1,0:T(8,128)S(1)} %get-tuple-element.31), channel_id=1, source_target_pairs={{4,0},{8,4},{12,8},{16,12},{20,16},{24,20},{28,24},{0,28},{5,1},{9... | collective-permute-start | bytes 196616 | tf_op jit(solution)/shard_map/ppermute | solution.py:521

commit v6 on v5

--- a/solution.py
+++ b/solution.py
@@ -16,9 +16,11 @@
 BAND_SOUTH = -50.0
 
 HALO = 32
+REACH = 16
 LANES = 128
 TILE = 8
 FIELDS = 3
+KEPT = 6
 SHIFT = 2
 VMEM_LIMIT = 8 * 1024 * 1024
 
@@ -43,24 +45,25 @@
     return pltpu.roll(tiles[-1], 1, 0)
 
 
-def neighbour_sum(field, east_face, north_face, stride):
+def neighbour_sum(field, faces, stride):
+    east_face, west_face, north_face = faces
     upward = [north_face[t] * field[t] for t in range(len(field))]
     return [
-        (east_face[t] * lane_shift(field[t], stride) + lane_shift(east_face[t] * field[t], -stride))
+        (east_face[t] * lane_shift(field[t], stride) + west_face[t] * lane_shift(field[t], -stride))
         + (north_face[t] * north_of(field, t) + south_of(upward, t))
         for t in range(len(field))
     ]
 
 
-def sweep(field, source, inverse, east_face, north_face, stride):
-    around = neighbour_sum(field, east_face, north_face, stride)
+def sweep(field, source, inverse, faces, stride):
+    around = neighbour_sum(field, faces, stride)
     return [
         (1.0 - DAMPING) * field[t] + inverse[t] * (source[t] + around[t]) for t in range(len(field))
     ]
 
 
-def remainder(field, source, diagonal, east_face, north_face, stride):
-    around = neighbour_sum(field, east_face, north_face, stride)
+def remainder(field, source, diagonal, faces, stride):
+    around = neighbour_sum(field, faces, stride)
     return [source[t] - diagonal[t] * field[t] + around[t] for t in range(len(field))]
 
 
@@ -137,7 +140,7 @@
     lat_far_ref[:, part] = jnp.where(odd, north_edge, south_edge)
 
 
-def faces(depth, across, along):
+def fine_faces(depth, across, along):
     count = len(depth)
     east_face = [jnp.minimum(depth[t], lane_shift(depth[t], 1)) * across[t] for t in range(count)]
     north_face = [jnp.minimum(depth[t], north_of(depth, t)) * along[t] for t in range(count)]
@@ -147,27 +150,34 @@
 def level_down(level, east_face, north_face, source_term, source):
     stride = 1 << level
     count = len(source)
+    west_face = [lane_shift(value, -stride) for value in east_face]
+    faces = (east_face, west_face, north_face)
     inverse, diagonal = [], []
     for t in range(count):
-        total = source_term[t] + (
-            (east_face[t] + lane_shift(east_face[t], -stride))
-            + (north_face[t] + south_of(north_face, t))
-        )
+        total = source_term[t] + ((east_face[t] + west_face[t]) + (north_face[t] + south_of(north_face, t)))
         diagonal.append(jnp.where(source_term[t] > 0.0, total, 1.0))
         inverse.append(DAMPING / diagonal[t])
     field = [inverse[t] * source[t] for t in range(count)]
     for _ in range(SWEEPS - 1):
-        field = sweep(field, source, inverse, east_face, north_face, stride)
-    image = remainder(field, source, diagonal, east_face, north_face, stride)
-    kept = (east_face, north_face, inverse, source, field, diagonal)
+        field = sweep(field, source, inverse, faces, stride)
+    image = remainder(field, source, diagonal, faces, stride)
+    kept = (faces, inverse, source, field, diagonal)
+
+    return kept, image
+
+
+def level_next(level, faces, source_term, image):
+    stride = 1 << level
+    east_face, _, north_face = faces
+    firsts = range(0, len(image), 2)
 
     def coarse(tiles):
-        sums = [tiles[t] + tiles[t + 1] for t in range(0, count, 2)]
+        sums = [tiles[t] + tiles[t + 1] for t in firsts]
         return [value + lane_shift(value, stride) for value in sums]
 
-    east_next = [lane_shift(east_face[t] + east_face[t + 1], stride) for t in range(0, count, 2)]
-    north_next = [north_face[t] + lane_shift(north_face[t], stride) for t in range(1, count, 2)]
-    return kept, (east_next, north_next, coarse(source_term), coarse(image))
+    east_next = [lane_shift(east_face[t] + east_face[t + 1], stride) for t in firsts]
+    north_next = [north_face[t + 1] + lane_shift(north_face[t + 1], stride) for t in firsts]
+    return east_next, north_next, coarse(source_term), coarse(image)
 
 
 def lay_out(lat_count, own_ref, lat_near_ref, lat_far_ref, west_ref, west_far_ref, east_ref, scale_ref, grid_ref):
@@ -175,34 +185,40 @@
     columns, height = grid_ref.shape[1], grid_ref.shape[2]
     count = height // TILE
     own_columns = cols // LANES
-    lat_odd = lax.rem(lax.axis_index("lat"), 2)
-    near_row = rows + pl.multiple_of(lat_odd * HALO, HALO)
-    far_row = rows + pl.multiple_of((1 - lat_odd) * HALO, HALO)
+    halo = (height - rows) // 2
+    lat_index = lax.axis_index("lat")
+    lat_odd = lax.rem(lat_index, 2)
+    near_row = rows + pl.multiple_of(lat_odd * halo, TILE)
+    far_row = rows + pl.multiple_of((1 - lat_odd) * halo, TILE)
+    near_part = pl.ds(pl.multiple_of(lat_odd * (HALO - halo), TILE), halo)
+    far_part = pl.ds(pl.multiple_of((1 - lat_odd) * (HALO - halo), TILE), halo)
     edge = FIELDS * cols + LANES
+    last = LANES // HALO - 1
+    at_end = (lat_index == 0) | (lat_index == lat_count - 1)
+
+    def inside(value, far):
+        return jnp.where(jnp.broadcast_to(at_end, value.shape), 0.0, value) if far else value
+
     parts = (
-        (0, 0, west_ref, [own_ref.at[f] for f in range(FIELDS)]),
-        (near_row, rows, lat_near_ref.at[:, pl.ds(edge, LANES)],
-         [lat_near_ref.at[:, pl.ds(f * cols, cols)] for f in range(FIELDS)]),
-        (far_row, rows + HALO, west_far_ref, [lat_far_ref.at[:, pl.ds(f * cols, cols)] for f in range(FIELDS)]),
+        (0, rows, None, west_ref[...], None if east_ref is None else east_ref[pl.ds(0, rows), :], False),
+        (near_row, halo, lat_near_ref.at[near_part], lat_near_ref[near_part, edge : edge + LANES],
+         None if east_ref is None else east_ref[pl.ds(rows, HALO), :], False),
+        (far_row, halo, lat_far_ref.at[far_part], west_far_ref[far_part, :],
+         None if east_ref is None else east_ref[pl.ds(rows + HALO, HALO), :], True),
     )
-    last = LANES // HALO - 1
-    for first, at, side_ref, bodies in parts:
-        west = side_ref[...]
-        slot = iota(west.shape, 1) // HALO
-        lat_index = lax.axis_index("lat")
-        outside = jnp.broadcast_to((lat_index == 0) | (lat_index == lat_count - 1), west.shape)
-        for f, body in enumerate(bodies):
+    for first, size, body_ref, west, east, far in parts:
+        slot = iota((size, LANES), 1) // HALO
+        for f in range(FIELDS):
             for c in range(own_columns):
-                value = body[:, c * LANES : (c + 1) * LANES]
-                if first is far_row:
-                    value = jnp.where(outside, 0.0, value)
-                grid_ref[f, c, pl.ds(first, west.shape[0]), :] = value
+                if body_ref is None:
+                    value = own_ref[f, :, c * LANES : (c + 1) * LANES]
+                else:
+                    value = body_ref[:, f * cols + c * LANES : f * cols + (c + 1) * LANES]
+                grid_ref[f, c, pl.ds(first, size), :] = inside(value, far)
             side = jnp.where(slot == (f + last) % (last + 1), west, 0.0)
-            if east_ref is not None:
-                side = jnp.where(slot == f, east_ref[pl.ds(at, west.shape[0]), :], side)
-            if first is far_row:
-                side = jnp.where(outside, 0.0, side)
-            grid_ref[f, own_columns, pl.ds(first, west.shape[0]), :] = lane_shift(side, f * HALO)
+            if east is not None:
+                side = jnp.where(slot == f, east, side)
+            grid_ref[f, own_columns, pl.ds(first, size), :] = inside(lane_shift(side, f * HALO), far)
 
     def load(f):
         return [
@@ -215,24 +231,27 @@
     depth, source_term, source = load(0), load(1), load(2)
     across = [jnp.concatenate([scale_ref[0, t]] * columns, axis=1) for t in range(count)]
     along = [jnp.concatenate([scale_ref[1, t]] * columns, axis=1) for t in range(count)]
-    return faces(depth, across, along) + (source_term, source)
+    return fine_faces(depth, across, along) + (source_term, source)
 
 
 def hold(lat_count, own_ref, lat_near_ref, lat_far_ref, west_ref, west_far_ref, east_ref, scale_ref, *rest):
-    level_refs = [rest[5 * i : 5 * i + 5] for i in range(LEVELS)]
-    diagonal_ref, grid_ref = rest[5 * LEVELS :]
+    level_refs = [rest[KEPT * i : KEPT * i + KEPT] for i in range(LEVELS)]
+    diagonal_ref, grid_ref = rest[KEPT * LEVELS :]
     state = lay_out(lat_count, own_ref, lat_near_ref, lat_far_ref, west_ref, west_far_ref, east_ref, scale_ref,
                     grid_ref)
     for level in range(LEVELS):
-        kept, state = level_down(level, *state)
-        for ref, tiles in zip(level_refs[level], kept):
+        (faces, inverse, source, field, diagonal), image = level_down(level, *state)
+        swept = sweep(field, source, inverse, faces, 1 << level)
+        for ref, tiles in zip(level_refs[level], faces + (inverse, source, swept)):
             keep(ref, tiles)
         if level == 0:
-            keep(diagonal_ref, kept[-1])
+            keep(diagonal_ref, diagonal)
+        if level < LEVELS - 1:
+            state = level_next(level, faces, state[2], image)
 
 
 def descend(lat_count, own_ref, lat_near_ref, lat_far_ref, west_ref, west_far_ref, west_edge_ref, scale_ref,
-            pack_ref, edge_ref, grid_ref):
+            pack_ref, edge_ref, grid_ref, plain_ref):
     rows = own_ref.shape[1]
     edge = slice(FIELDS * own_ref.shape[2], FIELDS * own_ref.shape[2] + LANES)
     edge_ref[pl.ds(0, rows), :] = west_edge_ref[...]
@@ -245,30 +264,38 @@
     state = lay_out(lat_count, own_ref, lat_near_ref, lat_far_ref, west_ref, west_far_ref, None, scale_ref,
                     grid_ref)
     for level in range(LEVELS):
-        _, state = level_down(level, *state)
-
-    east_face, north_face, source_term, source = state
+        kept, image = level_down(level, *state)
+        if level < LEVELS - 1:
+            state = level_next(level, kept[0], state[2], image)
+
+    east_face, north_face, source_term, _ = state
+    for f, values in enumerate((image, east_face, north_face, source_term)):
+        for t, value in enumerate(values):
+            for c in range(columns):
+                plain_ref[f, c, pl.ds(t, TILE, stride=len(values)), :] = value[:, c * LANES : (c + 1) * LANES]
     stride = 1 << LEVELS
+    bottom_rows = rows // stride
     bottom_width = cols // stride
     group = LANES // bottom_width
     per_column = LANES // stride
-    tiles = len(source)
-    lane = iota((TILE, LANES), 1)
+    lane = iota((bottom_rows, LANES), 1)
     cell = lane % bottom_width - SHIFT
     column = jnp.where(cell < 0, own_columns, cell // per_column)
-    pick = jnp.where(cell < 0, LANES + cell * stride, (cell % per_column) * stride)
+    west_part = jnp.where(cell < 0, LANES + cell * stride, (cell % per_column) * stride)
+    east_part = west_part + stride // 2
     turn = lax.rem(lane // bottom_width + group - lax.rem(lon_index, group), group)
-    own_rows = pack_ref.shape[1] // tiles
-    for t in range(tiles):
-        packed = jnp.zeros((TILE, LANES), jnp.float32)
-        for f, value in enumerate((source[t], east_face[t], north_face[t], source_term[t])):
-            flat = jnp.zeros((TILE, LANES), jnp.float32)
-            for c in range(columns):
-                taken = jnp.take_along_axis(value[:, c * LANES : (c + 1) * LANES], pick, axis=1)
-                flat = jnp.where(column == c, taken, flat)
-            packed = jnp.where(turn == f, flat, packed)
-        for k in range(pack_ref.shape[0]):
-            pack_ref[k, pl.ds(t, own_rows, stride=tiles), :] = packed[:own_rows]
+    packed = jnp.zeros((bottom_rows, LANES), jnp.float32)
+    for f, picks in enumerate(((west_part, east_part), (east_part,), (west_part, east_part), (west_part, east_part))):
+        flat = jnp.zeros((bottom_rows, LANES), jnp.float32)
+        for c in range(columns):
+            value = plain_ref[f, c, pl.ds(1, bottom_rows, stride=2), :]
+            if f != 2:
+                value = value + plain_ref[f, c, pl.ds(0, bottom_rows, stride=2), :]
+            taken = sum(jnp.take_along_axis(value, pick, axis=1) for pick in picks)
+            flat = jnp.where(column == c, taken, flat)
+        packed = jnp.where(turn == f, flat, packed)
+    for k in range(pack_ref.shape[0]):
+        pack_ref[k] = packed
 
 
 def total_of(tiles):
@@ -332,8 +359,8 @@
 
 
 def ascend(lat_count, lon_count, blocks_ref, *rest):
-    level_refs = [rest[5 * i : 5 * i + 5] for i in range(LEVELS)]
-    diagonal_ref, solution_ref, residual_ref, window_ref, order_ref, sems = rest[5 * LEVELS :]
+    level_refs = [rest[KEPT * i : KEPT * i + KEPT] for i in range(LEVELS)]
+    diagonal_ref, solution_ref, residual_ref, window_ref, order_ref, sems = rest[KEPT * LEVELS :]
     lon_index = lax.axis_index("lon")
     lat_index = lax.axis_index("lat")
     rows, cols = solution_ref.shape
@@ -374,35 +401,49 @@
     lane = iota((TILE, LANES), 1)
     ahead = (rows + HALO) // stride // tiles
     sublane = iota((TILE, LANES), 0)
-    correction = []
+    step = 1 << (LEVELS - 1)
+    center, plus, minus = [], [], []
     for t in range(tiles):
         upper = window_ref[pl.ds(start + pad + t, TILE, stride=tiles), :]
         lower = window_ref[pl.ds(start + pad + t - tiles * TILE, TILE, stride=tiles), :]
         value = jnp.where(sublane < ahead, upper, lower)
-        parts = []
-        for c in range(columns):
-            if c < own_columns:
-                pick = margin + (c * LANES + lane) // stride
-            else:
-                pick = jnp.where(lane < half, margin + bottom_width + lane // stride, (lane - half) // stride)
-            parts.append(jnp.take_along_axis(value, pick, axis=1))
-        correction.append(jnp.concatenate(parts, axis=1))
+        for target, move in ((center, 0), (plus, step), (minus, -step)):
+            parts = []
+            for c in range(columns):
+                place = c * LANES + lane + (move + width)
+                place = jnp.where(place >= width, place - width, place)
+                place = jnp.where(place >= width, place - width, place)
+                pick = jnp.where(place < cols + half, margin + place // stride, (place - (cols + half)) // stride)
+                parts.append(jnp.take_along_axis(value, pick, axis=1))
+            target.append(jnp.concatenate(parts, axis=1))
 
     lane = iota((TILE, width), 1)
     for level in range(LEVELS - 1, -1, -1):
         stride = 1 << level
-        east_face, north_face, inverse, source, field = map(tiles_of, level_refs[level])
+        east_face, west_face, north_face, inverse, source, swept = map(tiles_of, level_refs[level])
+        faces = (east_face, west_face, north_face)
         if level < LEVELS - 1:
             first = lax.rem(lane // stride, 2) == 0
-            correction = [jnp.where(first, value, lane_shift(value, -stride)) for value in correction]
-        spread = [correction[t // 2] for t in range(count >> level)]
-        if level == 0:
-            sea = [east_face[t] + north_face[t] > 0.0 for t in range(count)]
-            spread = [jnp.where(sea[t], spread[t], 0.0) for t in range(count)]
-        field = [field[t] + spread[t] for t in range(count >> level)]
-        for _ in range(SWEEPS):
-            field = sweep(field, source, inverse, east_face, north_face, stride)
-        correction = field
+            east = [lane_shift(value, stride) for value in field]
+            west = [lane_shift(value, -stride) for value in field]
+            west_two = [lane_shift(value, -2 * stride) for value in field]
+            coarse = range(len(field))
+            center = [jnp.where(first, field[t], west[t]) for t in coarse]
+            plus = [jnp.where(first, field[t], east[t]) for t in coarse]
+            minus = [jnp.where(first, west_two[t], west[t]) for t in coarse]
+        spread = [center[t // 2] for t in range(count >> level)]
+        field = []
+        for t in range(count >> level):
+            around = (east_face[t] * plus[t // 2] + west_face[t] * minus[t // 2]) + (
+                north_face[t] * north_of(spread, t) + south_of(north_face, t) * south_of(spread, t)
+            )
+            here = spread[t]
+            if level == 0:
+                here = jnp.where(east_face[t] + north_face[t] > 0.0, here, 0.0)
+            field.append(swept[t] + ((1.0 - DAMPING) * here + inverse[t] * around))
+        for _ in range(SWEEPS - 1):
+            field = sweep(field, source, inverse, faces, stride)
+    correction = field
     own_sublanes = rows // count
 
     def send_out(k, ref, tiles):
@@ -416,7 +457,7 @@
         return copies
 
     copies = send_out(0, solution_ref, correction)
-    final = remainder(correction, source, tiles_of(diagonal_ref), east_face, north_face, 1)
+    final = remainder(correction, source, tiles_of(diagonal_ref), faces, 1)
     copies += send_out(1, residual_ref, final)
     for copy in copies:
         copy.wait()
@@ -499,10 +540,13 @@
         near_pairs(lat_count),
     )
 
-    row = jnp.arange(TILE)[None, :] * count + jnp.arange(count)[:, None]
-    row = jnp.where(row < rows + HALO, row, row - height).astype(f32) + (lat_index * rows).astype(f32)
-    center, northern = metric(row)
-    scale = jnp.broadcast_to(jnp.stack([1.0 / center, northern])[..., None], (2, count, TILE, LANES))
+    def scales(halo):
+        tall = rows + 2 * halo
+        tiles = tall // TILE
+        row = jnp.arange(TILE)[None, :] * tiles + jnp.arange(tiles)[:, None]
+        row = jnp.where(row < rows + halo, row, row - tall).astype(f32) + (lat_index * rows).astype(f32)
+        center, northern = metric(row)
+        return jnp.broadcast_to(jnp.stack([1.0 / center, northern])[..., None], (2, tiles, TILE, LANES))
 
     devices = lat_count * lon_count
     grid = pltpu.VMEM((FIELDS, width // LANES, height, LANES), f32)
@@ -514,16 +558,19 @@
         ],
         in_specs=[vmem] * 7,
         out_specs=[vmem] * 2,
-        scratch_shapes=[grid],
+        scratch_shapes=[
+            pltpu.VMEM((FIELDS, width // LANES, rows + 2 * REACH, LANES), f32),
+            pltpu.VMEM((4, width // LANES, (rows + 2 * REACH) >> (LEVELS - 1), LANES), f32),
+        ],
         compiler_params=params,
         name="descend",
-    )(own, lat_near, lat_far, west_halo, west_far, west_edge, scale)
+    )(own, lat_near, lat_far, west_halo, west_far, west_edge, scales(REACH))
     east_halo = lax.ppermute(edges, "lon", westward)
     blocks = lax.all_to_all(packed, ("lon", "lat"), 0, 0, tiled=True)
 
     level_shapes = []
     for level in range(LEVELS):
-        level_shapes += [jax.ShapeDtypeStruct((count >> level, TILE, width), f32)] * 5
+        level_shapes += [jax.ShapeDtypeStruct((count >> level, TILE, width), f32)] * KEPT
     held = pl.pallas_call(
         functools.partial(hold, lat_count),
         out_shape=level_shapes + [jax.ShapeDtypeStruct((count, TILE, width), f32)],
@@ -533,7 +580,7 @@
         compiler_params=params,
         cost_estimate=pl.CostEstimate(flops=0, bytes_accessed=60 * 1024 * 1024, transcendentals=0),
         name="hold",
-    )(own, lat_near, lat_far, west_halo, west_far, east_halo, scale)
+    )(own, lat_near, lat_far, west_halo, west_far, east_halo, scales(HALO))
 
     return pl.pallas_call(
         functools.partial(ascend, lat_count, lon_count),

time: 28.2 us -> 27.6 us (0.979)
  Pallas kernels: 6.79 us -> 6.32 us
  waiting for transfers between devices: 6.49 us -> 6.07 us
    all_to_all x1, waiting for transfers between devices: 0.63 us -> 0.32 us  [on_device(): blocks = lax.all_to_all(packed, ('lon', 'lat'), 0, 0, tiled=True)]
  transfers between devices with their start and end apart: 6 -> 6, of which waited for: 5 -> 5; matrix products, arithmetic and copies ran while one was open for 1% -> 2% of each run, Pallas kernels for 4% -> 4%
where the time goes in v6:
time: 27.6 us; the launch traced here: 27.4 us
  starting transfers between devices  13.7 us (50%)
  Pallas kernels  6.32 us (23%)
  waiting for transfers between devices  6.07 us (22%)
  between operations  0.72 us (3%)
  local copies, waits for them, and re-layouts  0.33 us (1%)
  other arithmetic  0.29 us (1%)
    ppermute x1, starting transfers between devices, on_device(): east_halo = lax.ppermute(edges, 'lon', westward)  4.6 us
    all_to_all x1, starting transfers between devices, on_device(): blocks = lax.all_to_all(packed, ('lon', 'lat'), 0, 0, tiled=True)  3.88 us
    ppermute x1, starting transfers between devices, on_device(): west_halo = lax.ppermute(east_edge, 'lon', eastward)  3.02 us
    ppermute x1, waiting for transfers between devices, on_device(): west_halo = lax.ppermute(east_edge, 'lon', eastward)  2.7 us
    pallas_call x1, Pallas kernels, on_device(): pl.pallas_call(functools.partial(ascend, lat_count, lon_count), out_shape...  2.38 us
    ppermute x1, waiting for transfers between devices, on_device(): east_halo = lax.ppermute(edges, 'lon', westward)  1.83 us
    pallas_call x1, Pallas kernels, on_device(): pl.pallas_call(functools.partial(descend, lat_count), out_shape=[jax.Shap...  1.67 us
    ppermute x1, starting transfers between devices, on_device(): lax.ppermute(lat_far, ('lon', 'lat'), far_pairs(lon_count, lat_count, 0))  1.58 us
  transfers between devices with their start and end apart: 6, of which 5 were waited for; matrix products, arithmetic and copies ran while one was open for 2% of the time, Pallas kernels for 4%

profile of v6, /device:TPU:0, one launch (start us, length us, event | category | flops | bytes accessed | tf_op | source)
XLA Modules:
  0.0 27.4 jit_solution(15449087058756443668)
XLA Ops:
  0.6 1.1 %prepare.1 = (f32[3,64,256]{2,1,0:T(8,128)S(1)}, f32[64,128]{1,0:T(8,128)S(1)}, f32[64,128]{1,0:T(8,128)S(1)}) custom-call(f32[64,256]{1,0:T(8,128)} %forcing_ref.1, f32[64,256]{1,0:T(8,128)} %surface_ref.1, s32[64,256]{1,0:T(8,128)} %sea_ref.1, s32[64,256]{1,0:T(8,128)} %levels_ref.1), custom_call_target="tpu_custom_call" | custom-call | tf_op jit(solution)/shard_map/prepare/pallas_call | solution.py:494
  1.7 3.0 %collective-permute-start = (f32[64,128]{1,0:T(8,128)S(1)}, f32[64,128]{1,0:T(8,128)S(1)}, u32[]{:S(2)}, u32[]{:S(2)}) collective-permute-start(f32[64,128]{1,0:T(8,128)S(1)} %get-tuple-element.31.east_edge_ref), channel_id=1, source_target_pairs={{0,4},{4,8},{8,12},{12,16},{16,20},{20,24},{24,28},{28,0},{1,5},{5... | collective-permute-start | bytes 98312 | tf_op jit(solution)/shard_map/ppermute | solution.py:533
  4.8 1.6 %collective-permute-start.2 = (f32[32,896]{1,0:T(8,128)S(1)}, f32[32,896]{1,0:T(8,128)S(1)}, u32[]{:S(2)}, u32[]{:S(2)}) collective-permute-start(f32[32,896]{1,0:T(8,128)S(1)} %get-tuple-element.32.rows_ref), channel_id=1, source_target_pairs={{0,4},{1,2},{2,1},{3,7},{4,0},{5,6},{6,5},{7,3},{8,12},{9,10},{10,... | collective-permute-start | bytes 344072 | tf_op jit(solution)/shard_map/ppermute | solution.py:534
  6.3 0.5 %collective-permute-start.3 = (f32[32,128]{1,0:T(8,128)S(1)}, f32[32,128]{1,0:T(8,128)S(1)}, u32[]{:S(2)}, u32[]{:S(2)}) collective-permute-start(f32[32,128]{1,0:T(8,128)S(1)} %prepare_corner.1), channel_id=1, source_target_pairs={{0,4},{1,6},{2,5},{3,7},{4,0},{5,10},{6,9},{7,3},{8,12},{9,14},{10... | collective-permute-start | bytes 49160 | tf_op jit(solution)/shard_map/ppermute | solution.py:535
  6.9 0.1 cosine_divide_fusion.1
  7.0 2.7 %collective-permute-done.west_ref = f32[64,128]{1,0:T(8,128)S(1)} collective-permute-done((f32[64,128]{1,0:T(8,128)S(1)}, f32[64,128]{1,0:T(8,128)S(1)}, u32[]{:S(2)}, u32[]{:S(2)}) %collective-permute-start) | collective-permute-done | bytes 32800 | tf_op jit(solution)/shard_map/ppermute | solution.py:533
  9.7 0.1 collective-permute-start.1
  9.8 0.1 copy.6
  9.9 0.6 %collective-permute-done.3.west_far_ref = f32[32,128]{1,0:T(8,128)S(1)} collective-permute-done((f32[32,128]{1,0:T(8,128)S(1)}, f32[32,128]{1,0:T(8,128)S(1)}, u32[]{:S(2)}, u32[]{:S(2)}) %collective-permute-start.3) | collective-permute-done | bytes 16416 | tf_op jit(solution)/shard_map/ppermute | solution.py:535
  10.5 0.0 collective-permute-done.2.lat_far_ref
  10.5 0.6 %collective-permute-done.1.lat_near_ref = f32[32,1024]{1,0:T(8,128)S(1)} collective-permute-done((f32[32,1024]{1,0:T(8,128)S(1)}, f32[32,1024]{1,0:T(8,128)S(1)}, u32[]{:S(2)}, u32[]{:S(2)}) %collective-permute-start.1) | collective-permute-done | bytes 131104 | tf_op jit(solution)/shard_map/ppermute | solution.py:537
  11.1 0.1 broadcast_in_dim.4.scale_ref
  11.2 1.7 %descend.1 = (f32[32,8,128]{2,1,0:T(8,128)}, f32[128,128]{1,0:T(8,128)S(1)}) custom-call(f32[3,64,256]{2,1,0:T(8,128)S(1)} %get-tuple-element.28.own_ref, f32[32,1024]{1,0:T(8,128)S(1)} %collective-permute-done.1.lat_near_ref, f32[32,896]{1,0:T(8,128)S(1)} %collective-permute-done.2.lat_far_ref, f32[64,128]{1,0:T(8,128)S(1)} %collective-permute-done.west_ref, ...), custom_call_target="tpu_custom_call" | custom-call | tf_op jit(solution)/shard_map/descend/pallas_call | solution.py:553
  12.9 3.9 %all-to-all-start = ((f32[32,8,128]{2,1,0:T(8,128)}), f32[32,8,128]{2,1,0:T(8,128)S(1)}, u32[]{:S(2)}, u32[]{:S(2)}) async-start(f32[32,8,128]{2,1,0:T(8,128)} %get-tuple-element.33), calls=%async_computation | async-start | bytes 262144 | tf_op jit(solution)/shard_map/all_to_all | solution.py:569
  16.8 0.1 cosine_divide_fusion
  16.9 4.6 %collective-permute-start.4 = (f32[128,128]{1,0:T(8,128)S(1)}, f32[128,128]{1,0:T(8,128)S(1)}, u32[]{:S(2)}, u32[]{:S(2)}) collective-permute-start(f32[128,128]{1,0:T(8,128)S(1)} %get-tuple-element.34), channel_id=1, source_target_pairs={{4,0},{8,4},{12,8},{16,12},{20,16},{24,20},{28,24},{0,28},{5,1},{9... | collective-permute-start | bytes 196616 | tf_op jit(solution)/shard_map/ppermute | solution.py:568
  21.5 0.1 copy.7
  21.6 1.8 %collective-permute-done.4.east_ref = f32[128,128]{1,0:T(8,128)S(1)} collective-permute-done((f32[128,128]{1,0:T(8,128)S(1)}, f32[128,128]{1,0:T(8,128)S(1)}, u32[]{:S(2)}, u32[]{:S(2)}) %collective-permute-start.4) | collective-permute-done | bytes 65568 | tf_op jit(solution)/shard_map/ppermute | solution.py:568
  23.4 0.1 broadcast_in_dim.5.scale_ref
  23.5 1.2 %hold.1 = (f32[16,8,384]{2,1,0:T(8,128)S(1)}, f32[16,8,384]{2,1,0:T(8,128)S(1)}, f32[16,8,384]{2,1,0:T(8,128)S(1)}, f32[16,8,384]{2,1,0:T(8,128)S(1)}, f32[16,8,...) custom-call(f32[3,64,256]{2,1,0:T(8,128)S(1)} %get-tuple-element.28., ...), custom_call_target="tpu_custom_call" | custom-call | bytes 62914560 | tf_op jit(solution)/shard_map/hold/pallas_call | solution.py:574
  24.7 0.3 %all-to-all-done.blocks_ref = f32[32,8,128]{2,1,0:T(8,128)S(1)} async-done(((f32[32,8,128]{2,1,0:T(8,128)}), f32[32,8,128]{2,1,0:T(8,128)S(1)}, u32[]{:S(2)}, u32[]{:S(2)}) %all-to-all-start) | async-done | bytes 131104 | tf_op jit(solution)/shard_map/all_to_all | solution.py:569
  25.0 2.4 %ascend.1 = (f32[64,256]{1,0:T(8,128)}, f32[64,256]{1,0:T(8,128)}) custom-call(f32[32,8,128]{2,1,0:T(8,128)S(1)} %all-to-all-done.blocks_ref, f32[16,8,384]{2,1,0:T(8,128)S(1)} %get-tuple-element.35.rest_0_, f32[16,8,384]{2,1,0:T(8,128)S(1)} %get-tuple-element.36.rest_1_, f32[16,8,384]{2,1,0:T(8,128)S(1)} %get-tuple-element.37.rest_2_, ...), custom_call_target="tpu_custom_call" | custom-call | tf_op jit(solution)/shard_map/ascend/pallas_call | solution.py:585
  (8 shorter events, 0.1 us)
Async XLA Ops:
  1.7 8.0 %collective-permute-start = (f32[64,128]{1,0:T(8,128)S(1)}, f32[64,128]{1,0:T(8,128)S(1)}, u32[]{:S(2)}, u32[]{:S(2)}) collective-permute-start(f32[64,128]{1,0:T(8,128)S(1)} %get-tuple-element.31.east_edge_ref), channel_id=1, source_target_pairs={{0,4},{4,8},{8,12},{12,16},{16,20},{20,24},{24,28},{28,0},{1,5},{5... | collective-permute-start | bytes 98312 | tf_op jit(solution)/shard_map/ppermute | solution.py:533
  4.8 5.7 %collective-permute-start.2 = (f32[32,896]{1,0:T(8,128)S(1)}, f32[32,896]{1,0:T(8,128)S(1)}, u32[]{:S(2)}, u32[]{:S(2)}) collective-permute-start(f32[32,896]{1,0:T(8,128)S(1)} %get-tuple-element.32.rows_ref), channel_id=1, source_target_pairs={{0,4},{1,2},{2,1},{3,7},{4,0},{5,6},{6,5},{7,3},{8,12},{9,10},{10,... | collective-permute-start | bytes 344072 | tf_op jit(solution)/shard_map/ppermute | solution.py:534
  6.3 4.1 %collective-permute-start.3 = (f32[32,128]{1,0:T(8,128)S(1)}, f32[32,128]{1,0:T(8,128)S(1)}, u32[]{:S(2)}, u32[]{:S(2)}) collective-permute-start(f32[32,128]{1,0:T(8,128)S(1)} %prepare_corner.1), channel_id=1, source_target_pairs={{0,4},{1,6},{2,5},{3,7},{4,0},{5,10},{6,9},{7,3},{8,12},{9,14},{10... | collective-permute-start | bytes 49160 | tf_op jit(solution)/shard_map/ppermute | solution.py:535
  9.7 1.4 %collective-permute-start.1 = (f32[32,1024]{1,0:T(8,128)S(1)}, f32[32,1024]{1,0:T(8,128)S(1)}, u32[]{:S(2)}, u32[]{:S(2)}) collective-permute-start(f32[32,1024]{1,0:T(8,128)S(1)} %pad_maximum_fusion), channel_id=1, source_target_pairs={{0,1},{1,0},{2,3},{3,2},{4,5},{5,4},{6,7},{7,6},{8,9},{9,8},{10,11... | collective-permute-start | bytes 393224 | tf_op jit(solution)/shard_map/ppermute | solution.py:537
  12.9 12.1 %all-to-all-start = ((f32[32,8,128]{2,1,0:T(8,128)}), f32[32,8,128]{2,1,0:T(8,128)S(1)}, u32[]{:S(2)}, u32[]{:S(2)}) async-start(f32[32,8,128]{2,1,0:T(8,128)} %get-tuple-element.33), calls=%async_computation | async-start | bytes 262144 | tf_op jit(solution)/shard_map/all_to_all | solution.py:569
  16.9 6.5 %collective-permute-start.4 = (f32[128,128]{1,0:T(8,128)S(1)}, f32[128,128]{1,0:T(8,128)S(1)}, u32[]{:S(2)}, u32[]{:S(2)}) collective-permute-start(f32[128,128]{1,0:T(8,128)S(1)} %get-tuple-element.34), channel_id=1, source_target_pairs={{4,0},{8,4},{12,8},{16,12},{20,16},{24,20},{28,24},{0,28},{5,1},{9... | collective-permute-start | bytes 196616 | tf_op jit(solution)/shard_map/ppermute | solution.py:568

commit v7 on v6

--- a/solution.py
+++ b/solution.py
@@ -102,7 +102,7 @@
         copy.wait()
     sea_mask = sea_buf[...].astype(jnp.float32)
     layers = levels_buf[...].astype(jnp.float32)
-    depth = sea_mask * ((layers + layers * (layers - 1.0) / 20.0) / 200.0)
+    depth = sea_mask * (layers * (0.00475 + 0.00025 * layers))
     fields = (depth, surface_buf[...] * center * sea_mask, forcing_buf[...] * sea_mask)
     slot = iota((rows, LANES), 1) // HALO
     slots = LANES // HALO
@@ -180,7 +180,7 @@
     return east_next, north_next, coarse(source_term), coarse(image)
 
 
-def lay_out(lat_count, own_ref, lat_near_ref, lat_far_ref, west_ref, west_far_ref, east_ref, scale_ref, grid_ref):
+def lay_out(lat_count, own_ref, lat_near_ref, lat_far_ref, west_ref, west_near_ref, west_far_ref, scale_ref, grid_ref):
     rows, cols = own_ref.shape[1], own_ref.shape[2]
     columns, height = grid_ref.shape[1], grid_ref.shape[2]
     count = height // TILE
@@ -192,7 +192,6 @@
     far_row = rows + pl.multiple_of((1 - lat_odd) * halo, TILE)
     near_part = pl.ds(pl.multiple_of(lat_odd * (HALO - halo), TILE), halo)
     far_part = pl.ds(pl.multiple_of((1 - lat_odd) * (HALO - halo), TILE), halo)
-    edge = FIELDS * cols + LANES
     last = LANES // HALO - 1
     at_end = (lat_index == 0) | (lat_index == lat_count - 1)
 
@@ -200,13 +199,11 @@
         return jnp.where(jnp.broadcast_to(at_end, value.shape), 0.0, value) if far else value
 
     parts = (
-        (0, rows, None, west_ref[...], None if east_ref is None else east_ref[pl.ds(0, rows), :], False),
-        (near_row, halo, lat_near_ref.at[near_part], lat_near_ref[near_part, edge : edge + LANES],
-         None if east_ref is None else east_ref[pl.ds(rows, HALO), :], False),
-        (far_row, halo, lat_far_ref.at[far_part], west_far_ref[far_part, :],
-         None if east_ref is None else east_ref[pl.ds(rows + HALO, HALO), :], True),
+        (0, rows, None, west_ref[...], False),
+        (near_row, halo, lat_near_ref.at[near_part], west_near_ref[near_part, :], False),
+        (far_row, halo, lat_far_ref.at[far_part], west_far_ref[far_part, :], True),
     )
-    for first, size, body_ref, west, east, far in parts:
+    for first, size, body_ref, west, far in parts:
         slot = iota((size, LANES), 1) // HALO
         for f in range(FIELDS):
             for c in range(own_columns):
@@ -216,8 +213,6 @@
                     value = body_ref[:, f * cols + c * LANES : f * cols + (c + 1) * LANES]
                 grid_ref[f, c, pl.ds(first, size), :] = inside(value, far)
             side = jnp.where(slot == (f + last) % (last + 1), west, 0.0)
-            if east is not None:
-                side = jnp.where(slot == f, east, side)
             grid_ref[f, own_columns, pl.ds(first, size), :] = inside(lane_shift(side, f * HALO), far)
 
     def load(f):
@@ -231,26 +226,79 @@
     depth, source_term, source = load(0), load(1), load(2)
     across = [jnp.concatenate([scale_ref[0, t]] * columns, axis=1) for t in range(count)]
     along = [jnp.concatenate([scale_ref[1, t]] * columns, axis=1) for t in range(count)]
-    return fine_faces(depth, across, along) + (source_term, source)
-
-
-def hold(lat_count, own_ref, lat_near_ref, lat_far_ref, west_ref, west_far_ref, east_ref, scale_ref, *rest):
-    level_refs = [rest[KEPT * i : KEPT * i + KEPT] for i in range(LEVELS)]
-    diagonal_ref, grid_ref = rest[KEPT * LEVELS :]
-    state = lay_out(lat_count, own_ref, lat_near_ref, lat_far_ref, west_ref, west_far_ref, east_ref, scale_ref,
-                    grid_ref)
+    return depth, source_term, source, across, along
+
+
+def way_down(depth, source_term, source, across, along, put):
+    state = fine_faces(depth, across, along) + (source_term, source)
     for level in range(LEVELS):
         (faces, inverse, source, field, diagonal), image = level_down(level, *state)
         swept = sweep(field, source, inverse, faces, 1 << level)
-        for ref, tiles in zip(level_refs[level], faces + (inverse, source, swept)):
-            keep(ref, tiles)
-        if level == 0:
-            keep(diagonal_ref, diagonal)
+        put(level, faces + (inverse, source, swept) + ((diagonal,) if level == 0 else ()))
         if level < LEVELS - 1:
             state = level_next(level, faces, state[2], image)
 
 
-def descend(lat_count, own_ref, lat_near_ref, lat_far_ref, west_ref, west_far_ref, west_edge_ref, scale_ref,
+def split_refs(rest):
+    level_refs = [list(rest[KEPT * i : KEPT * i + KEPT]) for i in range(LEVELS)]
+    level_refs[0].append(rest[KEPT * LEVELS])
+    return level_refs, rest[KEPT * LEVELS + 1 :]
+
+
+def hold(lat_count, own_ref, lat_near_ref, lat_far_ref, west_ref, west_near_ref, west_far_ref, scale_ref, *rest):
+    level_refs, (raw_ref, grid_ref) = split_refs(rest)
+    values = lay_out(lat_count, own_ref, lat_near_ref, lat_far_ref, west_ref, west_near_ref, west_far_ref, scale_ref, grid_ref)
+    cols = own_ref.shape[2]
+    for f in range(FIELDS):
+        for t, value in enumerate(values[f]):
+            raw_ref[f, t] = value[:, cols - LANES : cols]
+
+    def put(level, kept):
+        for ref, tiles in zip(level_refs[level], kept):
+            keep(ref, tiles)
+
+    way_down(*values, put)
+
+
+def patch(lat_count, raw_ref, east_ref, scale_ref, *rest):
+    half = len(rest) // 2
+    level_refs, (strip_ref,) = split_refs(rest[half:])
+    count = raw_ref.shape[1]
+    height = count * TILE
+    rows = height - 2 * HALO
+    lat_index = lax.axis_index("lat")
+    lat_odd = lax.rem(lat_index, 2)
+    near_row = rows + pl.multiple_of(lat_odd * HALO, HALO)
+    far_row = rows + pl.multiple_of((1 - lat_odd) * HALO, HALO)
+    at_end = (lat_index == 0) | (lat_index == lat_count - 1)
+    for first, at, size, far in ((0, 0, rows, False), (near_row, rows, HALO, False), (far_row, rows + HALO, HALO, True)):
+        side = east_ref[pl.ds(at, size), :]
+        if far:
+            side = jnp.where(jnp.broadcast_to(at_end, side.shape), 0.0, side)
+        for f in range(FIELDS):
+            strip_ref[f, pl.ds(first, size), :] = lane_shift(side, f * HALO)
+    lane = iota((TILE, LANES), 1)
+    own = lane >= LANES // 2
+    fields = [
+        [
+            jnp.where(own, raw_ref[f, t],
+                      jnp.where(lane < HALO, strip_ref[f, pl.ds(t, TILE, stride=count), :], 0.0))
+            for t in range(count)
+        ]
+        for f in range(FIELDS)
+    ]
+
+    def put(level, kept):
+        for ref, tiles in zip(level_refs[level], kept):
+            last = ref.shape[2] - LANES
+            for t, value in enumerate(tiles):
+                ref[t, :, last - LANES : last] = jnp.where(lane >= LANES - HALO, value, ref[t, :, last - LANES : last])
+                ref[t, :, last:] = jnp.where(own, ref[t, :, last:], value)
+
+    way_down(*fields, [scale_ref[0, t] for t in range(count)], [scale_ref[1, t] for t in range(count)], put)
+
+
+def descend(lat_count, own_ref, lat_near_ref, lat_far_ref, west_ref, west_near_ref, west_far_ref, west_edge_ref, scale_ref,
             pack_ref, edge_ref, grid_ref, plain_ref):
     rows = own_ref.shape[1]
     edge = slice(FIELDS * own_ref.shape[2], FIELDS * own_ref.shape[2] + LANES)
@@ -261,8 +309,10 @@
     cols = own_ref.shape[2]
     own_columns = cols // LANES
     columns = grid_ref.shape[1]
-    state = lay_out(lat_count, own_ref, lat_near_ref, lat_far_ref, west_ref, west_far_ref, None, scale_ref,
-                    grid_ref)
+    depth, source_term, source, across, along = lay_out(
+        lat_count, own_ref, lat_near_ref, lat_far_ref, west_ref, west_near_ref, west_far_ref, scale_ref, grid_ref
+    )
+    state = fine_faces(depth, across, along) + (source_term, source)
     for level in range(LEVELS):
         kept, image = level_down(level, *state)
         if level < LEVELS - 1:
@@ -334,23 +384,25 @@
     iterate = jnp.zeros_like(source)
     remain = source
     image_r = apply(source)
-    direction = image_d = second = step_size = norm = None
+    direction = image_d = second = None
+    over_norm = over_step = None
     for step in range(BOTTOM_ITERS):
-        norm_now = total_of(split(remain * remain))
+        norm = total_of(split(remain * remain))
         energy = total_of(split(remain * image_r))
         last = step == BOTTOM_ITERS - 1
         ahead = None if last else apply(image_r)
         if step == 0:
-            step_size = norm_now / energy
             direction, image_d, second = remain, image_r, ahead
         else:
-            ratio = norm_now / norm
-            step_size = norm_now / (energy - ratio * (norm_now / step_size))
+            ratio = norm * over_norm
+            energy = energy - ratio * (norm * over_step)
             direction = remain + ratio * direction
             if not last:
                 image_d = image_r + ratio * image_d
                 second = ahead + ratio * second
-        norm = norm_now
+        step_size = norm / energy
+        over_norm = 1.0 / norm
+        over_step = energy * over_norm
         iterate = iterate + step_size * direction
         if not last:
             remain = remain - step_size * image_d
@@ -380,7 +432,7 @@
             for c in range(lon_count // group):
                 merged = None
                 for j in range(group):
-                    block = blocks_ref[(c * group + j) * lat_count + a]
+                    block = blocks_ref[a * lon_count + c * group + j]
                     merged = block if merged is None else jnp.where(slot == (f + j) % group, block, merged)
                 pieces.append(lane_shift(merged, f * bottom_width))
             strips.append(jnp.concatenate(pieces, axis=1))
@@ -533,11 +585,10 @@
     west_halo = lax.ppermute(east_edge, "lon", eastward)
     lat_far = lax.ppermute(lat_far, ("lon", "lat"), far_pairs(lon_count, lat_count, 0))
     west_far = lax.ppermute(diagonal_edge, ("lon", "lat"), far_pairs(lon_count, lat_count, 1))
+    lat_near = lax.ppermute(lat_near, "lat", near_pairs(lat_count))
     odd = lat_index % 2 == 1
-    lat_near = lax.ppermute(
-        jnp.concatenate([lat_near, jnp.where(odd, west_halo[:HALO], west_halo[rows - HALO :])], axis=1),
-        "lat",
-        near_pairs(lat_count),
+    west_near = lax.ppermute(
+        jnp.where(odd, west_halo[:HALO], west_halo[rows - HALO :]), "lat", near_pairs(lat_count)
     )
 
     def scales(halo):
@@ -556,7 +607,7 @@
             jax.ShapeDtypeStruct((devices, rows >> LEVELS, LANES), f32),
             jax.ShapeDtypeStruct((height, LANES), f32),
         ],
-        in_specs=[vmem] * 7,
+        in_specs=[vmem] * 8,
         out_specs=[vmem] * 2,
         scratch_shapes=[
             pltpu.VMEM((FIELDS, width // LANES, rows + 2 * REACH, LANES), f32),
@@ -564,23 +615,36 @@
         ],
         compiler_params=params,
         name="descend",
-    )(own, lat_near, lat_far, west_halo, west_far, west_edge, scales(REACH))
+    )(own, lat_near, lat_far, west_halo, west_near, west_far, west_edge, scales(REACH))
     east_halo = lax.ppermute(edges, "lon", westward)
-    blocks = lax.all_to_all(packed, ("lon", "lat"), 0, 0, tiled=True)
+    blocks = lax.all_to_all(packed, ("lat", "lon"), 0, 0, tiled=True)
 
     level_shapes = []
     for level in range(LEVELS):
         level_shapes += [jax.ShapeDtypeStruct((count >> level, TILE, width), f32)] * KEPT
+    held_shapes = level_shapes + [jax.ShapeDtypeStruct((count, TILE, width), f32)]
+    fine_scale = scales(HALO)
     held = pl.pallas_call(
         functools.partial(hold, lat_count),
-        out_shape=level_shapes + [jax.ShapeDtypeStruct((count, TILE, width), f32)],
+        out_shape=held_shapes + [jax.ShapeDtypeStruct((FIELDS, count, TILE, LANES), f32)],
         in_specs=[vmem] * 7,
-        out_specs=[vmem] * (1 + len(level_shapes)),
+        out_specs=[vmem] * (1 + len(held_shapes)),
         scratch_shapes=[grid],
         compiler_params=params,
         cost_estimate=pl.CostEstimate(flops=0, bytes_accessed=60 * 1024 * 1024, transcendentals=0),
         name="hold",
-    )(own, lat_near, lat_far, west_halo, west_far, east_halo, scales(HALO))
+    )(own, lat_near, lat_far, west_halo, west_near, west_far, fine_scale)
+    held, raw = held[:-1], held[-1]
+    held = pl.pallas_call(
+        functools.partial(patch, lat_count),
+        out_shape=held_shapes,
+        in_specs=[vmem] * (3 + len(held_shapes)),
+        out_specs=[vmem] * len(held_shapes),
+        scratch_shapes=[pltpu.VMEM((FIELDS, height, LANES), f32)],
+        input_output_aliases={3 + i: i for i in range(len(held_shapes))},
+        compiler_params=params,
+        name="patch",
+    )(raw, east_halo, fine_scale, *held)
 
     return pl.pallas_call(
         functools.partial(ascend, lat_count, lon_count),

time: 27.6 us -> 27.1 us (0.982)
  waiting for transfers between devices: 6.07 us -> 3.91 us
  Pallas kernels: 6.32 us -> 7.21 us
  starting transfers between devices: 13.7 us -> 14.5 us
    ppermute x1, waiting for transfers between devices: 1.83 us -> 0.56 us  [on_device(): east_halo = lax.ppermute(edges, 'lon', westward)]
    pallas_call x1 -> x2, Pallas kernels: 1.16 us -> 2.05 us  [the longest x1 1.16 us: on_device(): pl.pallas_call(functools.partial(hold, lat_count), out_shape=held_shapes...]
    ppermute x1, waiting for transfers between devices: 2.7 us -> 2.07 us  [on_device(): west_halo = lax.ppermute(east_edge, 'lon', eastward)]
    ppermute x1 -> x2, starting transfers between devices: 0.07 us -> 0.62 us  [the longest x1 0.62 us: on_device(): lat_near = lax.ppermute(lat_near, 'lat', near_pairs(lat_count))]
    ppermute x1 -> x2, waiting for transfers between devices: 0.64 us -> 0.4 us  [the longest x1 0.4 us: on_device(): lax.ppermute(jnp.where(odd, west_halo[:HALO], west_halo[rows - HALO:]), '...]
  transfers between devices with their start and end apart: 6 -> 7, of which waited for: 5 -> 5; matrix products, arithmetic and copies ran while one was open for 2% -> 2% of each run, Pallas kernels for 4% -> 8%
where the time goes in v7:
time: 27.1 us; the launch traced here: 26.9 us
  starting transfers between devices  14.5 us (54%)
  Pallas kernels  7.21 us (27%)
  waiting for transfers between devices  3.91 us (14%)
  between operations  0.72 us (3%)
  local copies, waits for them, and re-layouts  0.33 us (1%)
  other arithmetic  0.28 us (1%)
    ppermute x1, starting transfers between devices, on_device(): east_halo = lax.ppermute(edges, 'lon', westward)  4.6 us
    all_to_all x1, starting transfers between devices, on_device(): blocks = lax.all_to_all(packed, ('lat', 'lon'), 0, 0, tiled=True)  4.12 us
    ppermute x1, starting transfers between devices, on_device(): west_halo = lax.ppermute(east_edge, 'lon', eastward)  3.02 us
    pallas_call x1, Pallas kernels, on_device(): pl.pallas_call(functools.partial(ascend, lat_count, lon_count), out_shape...  2.38 us
    ppermute x1, waiting for transfers between devices, on_device(): west_halo = lax.ppermute(east_edge, 'lon', eastward)  2.07 us
    pallas_call x1, Pallas kernels, on_device(): pl.pallas_call(functools.partial(descend, lat_count), out_shape=[jax.Shap...  1.68 us
    ppermute x1, starting transfers between devices, on_device(): lax.ppermute(lat_far, ('lon', 'lat'), far_pairs(lon_count, lat_count, 0))  1.58 us
    pallas_call x1, Pallas kernels, on_device(): pl.pallas_call(functools.partial(hold, lat_count), out_shape=held_shapes...  1.16 us
  transfers between devices with their start and end apart: 7, of which 5 were waited for; matrix products, arithmetic and copies ran while one was open for 2% of the time, Pallas kernels for 8%

profile of v7, /device:TPU:0, one launch (start us, length us, event | category | flops | bytes accessed | tf_op | source)
XLA Modules:
  0.0 26.9 jit_solution(1903439159552862291)
XLA Ops:
  0.6 1.1 %prepare.1 = (f32[3,64,256]{2,1,0:T(8,128)S(1)}, f32[64,128]{1,0:T(8,128)S(1)}, f32[64,128]{1,0:T(8,128)S(1)}) custom-call(f32[64,256]{1,0:T(8,128)} %forcing_ref.1, f32[64,256]{1,0:T(8,128)} %surface_ref.1, s32[64,256]{1,0:T(8,128)} %sea_ref.1, s32[64,256]{1,0:T(8,128)} %levels_ref.1), custom_call_target="tpu_custom_call" | custom-call | tf_op jit(solution)/shard_map/prepare/pallas_call | solution.py:546
  1.7 3.0 %collective-permute-start.2 = (f32[64,128]{1,0:T(8,128)S(1)}, f32[64,128]{1,0:T(8,128)S(1)}, u32[]{:S(2)}, u32[]{:S(2)}) collective-permute-start(f32[64,128]{1,0:T(8,128)S(1)} %get-tuple-element.52.east_edge_ref), channel_id=1, source_target_pairs={{0,4},{4,8},{8,12},{12,16},{16,20},{20,24},{24,28},{28,0},{1,5},{5... | collective-permute-start | bytes 98312 | tf_op jit(solution)/shard_map/ppermute | solution.py:585
  4.8 1.6 %collective-permute-start.1 = (f32[32,896]{1,0:T(8,128)S(1)}, f32[32,896]{1,0:T(8,128)S(1)}, u32[]{:S(2)}, u32[]{:S(2)}) collective-permute-start(f32[32,896]{1,0:T(8,128)S(1)} %get-tuple-element.51.rows_ref), channel_id=1, source_target_pairs={{0,4},{1,2},{2,1},{3,7},{4,0},{5,6},{6,5},{7,3},{8,12},{9,10},{10,... | collective-permute-start | bytes 344072 | tf_op jit(solution)/shard_map/ppermute | solution.py:586
  6.3 0.5 %collective-permute-start.4 = (f32[32,128]{1,0:T(8,128)S(1)}, f32[32,128]{1,0:T(8,128)S(1)}, u32[]{:S(2)}, u32[]{:S(2)}) collective-permute-start(f32[32,128]{1,0:T(8,128)S(1)} %prepare_corner.1), channel_id=1, source_target_pairs={{0,4},{1,6},{2,5},{3,7},{4,0},{5,10},{6,9},{7,3},{8,12},{9,14},{10... | collective-permute-start | bytes 49160 | tf_op jit(solution)/shard_map/ppermute | solution.py:587
  6.9 0.6 %collective-permute-start = (f32[32,896]{1,0:T(8,128)S(1)}, f32[32,896]{1,0:T(8,128)S(1)}, u32[]{:S(2)}, u32[]{:S(2)}) collective-permute-start(f32[32,896]{1,0:T(8,128)S(1)} %get-tuple-element.50), channel_id=1, source_target_pairs={{0,1},{1,0},{2,3},{3,2},{4,5},{5,4},{6,7},{7,6},{8,9},{9,8},{10,11... | collective-permute-start | bytes 344072 | tf_op jit(solution)/shard_map/ppermute | solution.py:588
  7.5 0.1 cosine_divide_fusion.1
  7.6 2.1 %collective-permute-done.2.west_ref = f32[64,128]{1,0:T(8,128)S(1)} collective-permute-done((f32[64,128]{1,0:T(8,128)S(1)}, f32[64,128]{1,0:T(8,128)S(1)}, u32[]{:S(2)}, u32[]{:S(2)}) %collective-permute-start.2) | collective-permute-done | bytes 32800 | tf_op jit(solution)/shard_map/ppermute | solution.py:585
  9.7 0.0 collective-permute-start.3
  9.7 0.1 copy.25
  9.8 0.7 %collective-permute-done.4.west_far_ref = f32[32,128]{1,0:T(8,128)S(1)} collective-permute-done((f32[32,128]{1,0:T(8,128)S(1)}, f32[32,128]{1,0:T(8,128)S(1)}, u32[]{:S(2)}, u32[]{:S(2)}) %collective-permute-start.4) | collective-permute-done | bytes 16416 | tf_op jit(solution)/shard_map/ppermute | solution.py:587
  10.5 0.4 %collective-permute-done.3.west_near_ref = f32[32,128]{1,0:T(8,128)S(1)} collective-permute-done((f32[32,128]{1,0:T(8,128)S(1)}, f32[32,128]{1,0:T(8,128)S(1)}, u32[]{:S(2)}, u32[]{:S(2)}) %collective-permute-start.3) | collective-permute-done | bytes 16416 | tf_op jit(solution)/shard_map/ppermute | solution.py:590
  10.9 0.0 collective-permute-done.lat_near_ref
  10.9 0.1 broadcast_in_dim.4.scale_ref
  11.0 1.7 %descend.1 = (f32[32,8,128]{2,1,0:T(8,128)}, f32[128,128]{1,0:T(8,128)S(1)}) custom-call(f32[3,64,256]{2,1,0:T(8,128)S(1)} %get-tuple-element.48.own_ref, f32[32,896]{1,0:T(8,128)S(1)} %collective-permute-done.lat_near_ref, f32[32,896]{1,0:T(8,128)S(1)} %collective-permute-done.1.lat_far_ref, f32[64,128]{1,0:T(8,128)S(1)} %collective-permute-done.2.west_ref, ...), custom_call_target="tpu_custom_call" | custom-call | tf_op jit(solution)/shard_map/descend/pallas_call | solution.py:604
  12.7 4.1 %all-to-all-start = ((f32[32,8,128]{2,1,0:T(8,128)}), f32[32,8,128]{2,1,0:T(8,128)S(1)}, u32[]{:S(2)}, u32[]{:S(2)}) async-start(f32[32,8,128]{2,1,0:T(8,128)} %get-tuple-element.53), calls=%async_computation | async-start | bytes 262144 | tf_op jit(solution)/shard_map/all_to_all | solution.py:620
  16.8 0.1 cosine_divide_fusion
  16.9 4.6 %collective-permute-start.5 = (f32[128,128]{1,0:T(8,128)S(1)}, f32[128,128]{1,0:T(8,128)S(1)}, u32[]{:S(2)}, u32[]{:S(2)}) collective-permute-start(f32[128,128]{1,0:T(8,128)S(1)} %get-tuple-element.55), channel_id=1, source_target_pairs={{4,0},{8,4},{12,8},{16,12},{20,16},{24,20},{28,24},{0,28},{5,1},{9... | collective-permute-start | bytes 196616 | tf_op jit(solution)/shard_map/ppermute | solution.py:619
  21.5 0.1 copy.26
  21.6 0.1 broadcast_in_dim.5.scale_ref
  21.7 1.2 %hold.1 = (f32[16,8,384]{2,1,0:T(8,128)S(1)}, f32[16,8,384]{2,1,0:T(8,128)S(1)}, f32[16,8,384]{2,1,0:T(8,128)S(1)}, f32[16,8,384]{2,1,0:T(8,128)S(1)}, f32[16,8,...) custom-call(f32[3,64,256]{2,1,0:T(8,128)S(1)} %get-tuple-element.48., ...), custom_call_target="tpu_custom_call" | custom-call | bytes 62914560 | tf_op jit(solution)/shard_map/hold/pallas_call | solution.py:627
  22.9 0.6 %collective-permute-done.5.east_ref = f32[128,128]{1,0:T(8,128)S(1)} collective-permute-done((f32[128,128]{1,0:T(8,128)S(1)}, f32[128,128]{1,0:T(8,128)S(1)}, u32[]{:S(2)}, u32[]{:S(2)}) %collective-permute-start.5) | collective-permute-done | bytes 65568 | tf_op jit(solution)/shard_map/ppermute | solution.py:619
  23.4 0.9 %patch.1 = (f32[16,8,384]{2,1,0:T(8,128)S(1)}, f32[16,8,384]{2,1,0:T(8,128)S(1)}, f32[16,8,384]{2,1,0:T(8,128)S(1)}, f32[16,8,384]{2,1,0:T(8,128)S(1)}, f32[16,8...) custom-call(f32[3,16,8,128]{3,2,1,0:T(8,128)S(1)} %get-tuple-element, ...), custom_call_target="tpu_custom_call", output_to_operand_aliasing={{0}: (3, {}), {1}: (4, {}), {2}: (5, {}), {3}: (6, {}), {4}... | custom-call | tf_op jit(solution)/shard_map/patch/pallas_call | solution.py:638
  24.3 0.2 all-to-all-done.blocks_ref
  24.5 2.4 %ascend.1 = (f32[64,256]{1,0:T(8,128)}, f32[64,256]{1,0:T(8,128)}) custom-call(f32[32,8,128]{2,1,0:T(8,128)S(1)} %all-to-all-done.blocks_ref, f32[16,8,384]{2,1,0:T(8,128)S(1)} %get-tuple-element.75.rest_0_, f32[16,8,384]{2,1,0:T(8,128)S(1)} %get-tuple-element.76.rest_1_, f32[16,8,384]{2,1,0:T(8,128)S(1)} %get-tuple-element.77.rest_2_, ...), custom_call_target="tpu_custom_call" | custom-call | tf_op jit(solution)/shard_map/ascend/pallas_call | solution.py:649
  (8 shorter events, 0.1 us)
Async XLA Ops:
  1.7 8.0 %collective-permute-start.2 = (f32[64,128]{1,0:T(8,128)S(1)}, f32[64,128]{1,0:T(8,128)S(1)}, u32[]{:S(2)}, u32[]{:S(2)}) collective-permute-start(f32[64,128]{1,0:T(8,128)S(1)} %get-tuple-element.52.east_edge_ref), channel_id=1, source_target_pairs={{0,4},{4,8},{8,12},{12,16},{16,20},{20,24},{24,28},{28,0},{1,5},{5... | collective-permute-start | bytes 98312 | tf_op jit(solution)/shard_map/ppermute | solution.py:585
  4.8 6.1 %collective-permute-start.1 = (f32[32,896]{1,0:T(8,128)S(1)}, f32[32,896]{1,0:T(8,128)S(1)}, u32[]{:S(2)}, u32[]{:S(2)}) collective-permute-start(f32[32,896]{1,0:T(8,128)S(1)} %get-tuple-element.51.rows_ref), channel_id=1, source_target_pairs={{0,4},{1,2},{2,1},{3,7},{4,0},{5,6},{6,5},{7,3},{8,12},{9,10},{10,... | collective-permute-start | bytes 344072 | tf_op jit(solution)/shard_map/ppermute | solution.py:586
  6.3 4.1 %collective-permute-start.4 = (f32[32,128]{1,0:T(8,128)S(1)}, f32[32,128]{1,0:T(8,128)S(1)}, u32[]{:S(2)}, u32[]{:S(2)}) collective-permute-start(f32[32,128]{1,0:T(8,128)S(1)} %prepare_corner.1), channel_id=1, source_target_pairs={{0,4},{1,6},{2,5},{3,7},{4,0},{5,10},{6,9},{7,3},{8,12},{9,14},{10... | collective-permute-start | bytes 49160 | tf_op jit(solution)/shard_map/ppermute | solution.py:587
  6.9 4.0 %collective-permute-start = (f32[32,896]{1,0:T(8,128)S(1)}, f32[32,896]{1,0:T(8,128)S(1)}, u32[]{:S(2)}, u32[]{:S(2)}) collective-permute-start(f32[32,896]{1,0:T(8,128)S(1)} %get-tuple-element.50), channel_id=1, source_target_pairs={{0,1},{1,0},{2,3},{3,2},{4,5},{5,4},{6,7},{7,6},{8,9},{9,8},{10,11... | collective-permute-start | bytes 344072 | tf_op jit(solution)/shard_map/ppermute | solution.py:588
  9.7 1.2 %collective-permute-start.3 = (f32[32,128]{1,0:T(8,128)S(1)}, f32[32,128]{1,0:T(8,128)S(1)}, u32[]{:S(2)}, u32[]{:S(2)}) collective-permute-start(f32[32,128]{1,0:T(8,128)S(1)} %slice_select_fusion), channel_id=1, source_target_pairs={{0,1},{1,0},{2,3},{3,2},{4,5},{5,4},{6,7},{7,6},{8,9},{9,8},{10,11... | collective-permute-start | bytes 49160 | tf_op jit(solution)/shard_map/ppermute | solution.py:590
  12.7 11.9 %all-to-all-start = ((f32[32,8,128]{2,1,0:T(8,128)}), f32[32,8,128]{2,1,0:T(8,128)S(1)}, u32[]{:S(2)}, u32[]{:S(2)}) async-start(f32[32,8,128]{2,1,0:T(8,128)} %get-tuple-element.53), calls=%async_computation | async-start | bytes 262144 | tf_op jit(solution)/shard_map/all_to_all | solution.py:620
  16.9 6.5 %collective-permute-start.5 = (f32[128,128]{1,0:T(8,128)S(1)}, f32[128,128]{1,0:T(8,128)S(1)}, u32[]{:S(2)}, u32[]{:S(2)}) collective-permute-start(f32[128,128]{1,0:T(8,128)S(1)} %get-tuple-element.55), channel_id=1, source_target_pairs={{4,0},{8,4},{12,8},{16,12},{20,16},{24,20},{28,24},{0,28},{5,1},{9... | collective-permute-start | bytes 196616 | tf_op jit(solution)/shard_map/ppermute | solution.py:619

commit v8 on v7

--- a/solution.py
+++ b/solution.py
@@ -141,43 +141,76 @@
 
 
 def fine_faces(depth, across, along):
-    count = len(depth)
-    east_face = [jnp.minimum(depth[t], lane_shift(depth[t], 1)) * across[t] for t in range(count)]
-    north_face = [jnp.minimum(depth[t], north_of(depth, t)) * along[t] for t in range(count)]
-    return east_face, north_face
-
-
-def level_down(level, east_face, north_face, source_term, source):
+    tiles = range(len(depth))
+    east_face = [jnp.minimum(depth[t], lane_shift(depth[t], 1)) * across[t] for t in tiles]
+    west_face = [jnp.minimum(depth[t], lane_shift(depth[t], -1)) * across[t] for t in tiles]
+    north_face = [jnp.minimum(depth[t], north_of(depth, t)) * along[t] for t in tiles]
+    return east_face, west_face, north_face
+
+
+def coefficients(level, faces, source_term):
+    east_face, west_face, north_face = faces
+    diagonal = []
+    for t in range(len(source_term)):
+        total = source_term[t] + ((east_face[t] + west_face[t]) + (north_face[t] + south_of(north_face, t)))
+        diagonal.append(jnp.where(source_term[t] > 0.0, total, 1.0))
+    return faces, [DAMPING / value for value in diagonal], diagonal
+
+
+def next_coefficients(level, faces, source_term):
+    stride = 1 << level
+    east_face, _, north_face = faces
+    firsts = range(0, len(source_term), 2)
+    east_sums = [east_face[t] + east_face[t + 1] for t in firsts]
+    term_sums = [source_term[t] + source_term[t + 1] for t in firsts]
+    east_next = [lane_shift(value, stride) for value in east_sums]
+    west_next = [lane_shift(value, -stride) for value in east_sums]
+    north_next = [north_face[t + 1] + lane_shift(north_face[t + 1], stride) for t in firsts]
+    return (east_next, west_next, north_next), [value + lane_shift(value, stride) for value in term_sums]
+
+
+def all_coefficients(depth, source_term, across, along):
+    faces = fine_faces(depth, across, along)
+    levels = []
+    for level in range(LEVELS):
+        levels.append(coefficients(level, faces, source_term) + (source_term,))
+        if level < LEVELS - 1:
+            faces, source_term = next_coefficients(level, faces, source_term)
+    return levels
+
+
+def level_down(level, faces, inverse, diagonal, source, sides):
     stride = 1 << level
     count = len(source)
-    west_face = [lane_shift(value, -stride) for value in east_face]
-    faces = (east_face, west_face, north_face)
-    inverse, diagonal = [], []
-    for t in range(count):
-        total = source_term[t] + ((east_face[t] + west_face[t]) + (north_face[t] + south_of(north_face, t)))
-        diagonal.append(jnp.where(source_term[t] > 0.0, total, 1.0))
-        inverse.append(DAMPING / diagonal[t])
     field = [inverse[t] * source[t] for t in range(count)]
-    for _ in range(SWEEPS - 1):
-        field = sweep(field, source, inverse, faces, stride)
-    image = remainder(field, source, diagonal, faces, stride)
-    kept = (faces, inverse, source, field, diagonal)
-
-    return kept, image
-
-
-def level_next(level, faces, source_term, image):
+    for k in range(SWEEPS - 1):
+        if k == 0 and sides is not None:
+            east_face, west_face, north_face = faces
+            plus, minus = sides
+            upward = [north_face[t] * field[t] for t in range(count)]
+            around = [
+                (
+                    east_face[t] * (lane_shift(inverse[t], stride) * plus[t])
+                    + west_face[t] * (lane_shift(inverse[t], -stride) * minus[t])
+                )
+                + (north_face[t] * north_of(field, t) + south_of(upward, t))
+                for t in range(count)
+            ]
+            field = [(1.0 - DAMPING) * field[t] + inverse[t] * (source[t] + around[t]) for t in range(count)]
+        else:
+            field = sweep(field, source, inverse, faces, stride)
+    return field, remainder(field, source, diagonal, faces, stride)
+
+
+def level_next(level, image):
     stride = 1 << level
-    east_face, _, north_face = faces
-    firsts = range(0, len(image), 2)
-
-    def coarse(tiles):
-        sums = [tiles[t] + tiles[t + 1] for t in firsts]
-        return [value + lane_shift(value, stride) for value in sums]
-
-    east_next = [lane_shift(east_face[t] + east_face[t + 1], stride) for t in firsts]
-    north_next = [north_face[t + 1] + lane_shift(north_face[t + 1], stride) for t in firsts]
-    return east_next, north_next, coarse(source_term), coarse(image)
+    left = [image[t] + image[t + 1] for t in range(0, len(image), 2)]
+    source = [value + lane_shift(value, stride) for value in left]
+    if left[0].shape[1] > LANES:
+        return source, None
+    plus = [lane_shift(value, 2 * stride) + lane_shift(value, 3 * stride) for value in left]
+    minus = [lane_shift(value, -2 * stride) + lane_shift(value, -stride) for value in left]
+    return source, (plus, minus)
 
 
 def lay_out(lat_count, own_ref, lat_near_ref, lat_far_ref, west_ref, west_near_ref, west_far_ref, scale_ref, grid_ref):
@@ -230,13 +263,14 @@
 
 
 def way_down(depth, source_term, source, across, along, put):
-    state = fine_faces(depth, across, along) + (source_term, source)
-    for level in range(LEVELS):
-        (faces, inverse, source, field, diagonal), image = level_down(level, *state)
+    levels = all_coefficients(depth, source_term, across, along)
+    sides = None
+    for level, (faces, inverse, diagonal, _) in enumerate(levels):
+        field, image = level_down(level, faces, inverse, diagonal, source, sides)
         swept = sweep(field, source, inverse, faces, 1 << level)
         put(level, faces + (inverse, source, swept) + ((diagonal,) if level == 0 else ()))
         if level < LEVELS - 1:
-            state = level_next(level, faces, state[2], image)
+            source, sides = level_next(level, image)
 
 
 def split_refs(rest):
@@ -262,6 +296,7 @@
 
 def patch(lat_count, raw_ref, east_ref, scale_ref, *rest):
     half = len(rest) // 2
+    held_refs, _ = split_refs(rest[:half])
     level_refs, (strip_ref,) = split_refs(rest[half:])
     count = raw_ref.shape[1]
     height = count * TILE
@@ -289,11 +324,13 @@
     ]
 
     def put(level, kept):
-        for ref, tiles in zip(level_refs[level], kept):
+        for held_ref, ref, tiles in zip(held_refs[level], level_refs[level], kept):
             last = ref.shape[2] - LANES
             for t, value in enumerate(tiles):
-                ref[t, :, last - LANES : last] = jnp.where(lane >= LANES - HALO, value, ref[t, :, last - LANES : last])
-                ref[t, :, last:] = jnp.where(own, ref[t, :, last:], value)
+                held = held_ref[t]
+                edge = jnp.where(lane >= LANES - HALO, value, held[:, last - LANES : last])
+                halo = jnp.where(own, held[:, last:], value)
+                ref[t] = jnp.concatenate([held[:, : last - LANES], edge, halo], axis=1)
 
     way_down(*fields, [scale_ref[0, t] for t in range(count)], [scale_ref[1, t] for t in range(count)], put)
 
@@ -312,13 +349,14 @@
     depth, source_term, source, across, along = lay_out(
         lat_count, own_ref, lat_near_ref, lat_far_ref, west_ref, west_near_ref, west_far_ref, scale_ref, grid_ref
     )
-    state = fine_faces(depth, across, along) + (source_term, source)
-    for level in range(LEVELS):
-        kept, image = level_down(level, *state)
+    levels = all_coefficients(depth, source_term, across, along)
+    sides = None
+    for level, (faces, inverse, diagonal, source_term) in enumerate(levels):
+        _, image = level_down(level, faces, inverse, diagonal, source, sides)
         if level < LEVELS - 1:
-            state = level_next(level, kept[0], state[2], image)
-
-    east_face, north_face, source_term, _ = state
+            source, sides = level_next(level, image)
+
+    east_face, _, north_face = faces
     for f, values in enumerate((image, east_face, north_face, source_term)):
         for t, value in enumerate(values):
             for c in range(columns):
@@ -641,7 +679,6 @@
         in_specs=[vmem] * (3 + len(held_shapes)),
         out_specs=[vmem] * len(held_shapes),
         scratch_shapes=[pltpu.VMEM((FIELDS, height, LANES), f32)],
-        input_output_aliases={3 + i: i for i in range(len(held_shapes))},
         compiler_params=params,
         name="patch",
     )(raw, east_halo, fine_scale, *held)

time: 27.1 us -> 27.1 us (level)
  transfers between devices with their start and end apart: 7 -> 7, of which waited for: 5 -> 5; matrix products, arithmetic and copies ran while one was open for 2% -> 2% of each run, Pallas kernels for 8% -> 7%
where the time goes in v8:
time: 27.1 us; the launch traced here: 26.9 us
  starting transfers between devices  14.5 us (54%)
  Pallas kernels  7.11 us (26%)
  waiting for transfers between devices  4.02 us (15%)
  between operations  0.72 us (3%)
  local copies, waits for them, and re-layouts  0.33 us (1%)
  other arithmetic  0.28 us (1%)
    ppermute x1, starting transfers between devices, on_device(): east_halo = lax.ppermute(edges, 'lon', westward)  4.6 us
    all_to_all x1, starting transfers between devices, on_device(): blocks = lax.all_to_all(packed, ('lat', 'lon'), 0, 0, tiled=True)  4.12 us
    ppermute x1, starting transfers between devices, on_device(): west_halo = lax.ppermute(east_edge, 'lon', eastward)  3.02 us
    pallas_call x1, Pallas kernels, on_device(): pl.pallas_call(functools.partial(ascend, lat_count, lon_count), out_shape...  2.38 us
    ppermute x1, waiting for transfers between devices, on_device(): west_halo = lax.ppermute(east_edge, 'lon', eastward)  2.07 us
    pallas_call x1, Pallas kernels, on_device(): pl.pallas_call(functools.partial(descend, lat_count), out_shape=[jax.Shap...  1.67 us
    ppermute x1, starting transfers between devices, on_device(): lax.ppermute(lat_far, ('lon', 'lat'), far_pairs(lon_count, lat_count, 0))  1.58 us
    pallas_call x1, Pallas kernels, on_device(): pl.pallas_call(functools.partial(hold, lat_count), out_shape=held_shapes...  1.19 us
  transfers between devices with their start and end apart: 7, of which 5 were waited for; matrix products, arithmetic and copies ran while one was open for 2% of the time, Pallas kernels for 7%

profile of v8, /device:TPU:0, one launch (start us, length us, event | category | flops | bytes accessed | tf_op | source)
XLA Modules:
  0.0 26.9 jit_solution(8422706412472817478)
XLA Ops:
  0.6 1.1 %prepare.1 = (f32[3,64,256]{2,1,0:T(8,128)S(1)}, f32[64,128]{1,0:T(8,128)S(1)}, f32[64,128]{1,0:T(8,128)S(1)}) custom-call(f32[64,256]{1,0:T(8,128)} %forcing_ref.1, f32[64,256]{1,0:T(8,128)} %surface_ref.1, s32[64,256]{1,0:T(8,128)} %sea_ref.1, s32[64,256]{1,0:T(8,128)} %levels_ref.1), custom_call_target="tpu_custom_call" | custom-call | tf_op jit(solution)/shard_map/prepare/pallas_call | solution.py:584
  1.7 3.0 %collective-permute-start.2 = (f32[64,128]{1,0:T(8,128)S(1)}, f32[64,128]{1,0:T(8,128)S(1)}, u32[]{:S(2)}, u32[]{:S(2)}) collective-permute-start(f32[64,128]{1,0:T(8,128)S(1)} %get-tuple-element.52.east_edge_ref), channel_id=1, source_target_pairs={{0,4},{4,8},{8,12},{12,16},{16,20},{20,24},{24,28},{28,0},{1,5},{5... | collective-permute-start | bytes 98312 | tf_op jit(solution)/shard_map/ppermute | solution.py:623
  4.8 1.6 %collective-permute-start.1 = (f32[32,896]{1,0:T(8,128)S(1)}, f32[32,896]{1,0:T(8,128)S(1)}, u32[]{:S(2)}, u32[]{:S(2)}) collective-permute-start(f32[32,896]{1,0:T(8,128)S(1)} %get-tuple-element.51.rows_ref), channel_id=1, source_target_pairs={{0,4},{1,2},{2,1},{3,7},{4,0},{5,6},{6,5},{7,3},{8,12},{9,10},{10,... | collective-permute-start | bytes 344072 | tf_op jit(solution)/shard_map/ppermute | solution.py:624
  6.3 0.5 %collective-permute-start.4 = (f32[32,128]{1,0:T(8,128)S(1)}, f32[32,128]{1,0:T(8,128)S(1)}, u32[]{:S(2)}, u32[]{:S(2)}) collective-permute-start(f32[32,128]{1,0:T(8,128)S(1)} %prepare_corner.1), channel_id=1, source_target_pairs={{0,4},{1,6},{2,5},{3,7},{4,0},{5,10},{6,9},{7,3},{8,12},{9,14},{10... | collective-permute-start | bytes 49160 | tf_op jit(solution)/shard_map/ppermute | solution.py:625
  6.9 0.6 %collective-permute-start = (f32[32,896]{1,0:T(8,128)S(1)}, f32[32,896]{1,0:T(8,128)S(1)}, u32[]{:S(2)}, u32[]{:S(2)}) collective-permute-start(f32[32,896]{1,0:T(8,128)S(1)} %get-tuple-element.50), channel_id=1, source_target_pairs={{0,1},{1,0},{2,3},{3,2},{4,5},{5,4},{6,7},{7,6},{8,9},{9,8},{10,11... | collective-permute-start | bytes 344072 | tf_op jit(solution)/shard_map/ppermute | solution.py:626
  7.5 0.1 cosine_divide_fusion.1
  7.6 2.1 %collective-permute-done.2.west_ref = f32[64,128]{1,0:T(8,128)S(1)} collective-permute-done((f32[64,128]{1,0:T(8,128)S(1)}, f32[64,128]{1,0:T(8,128)S(1)}, u32[]{:S(2)}, u32[]{:S(2)}) %collective-permute-start.2) | collective-permute-done | bytes 32800 | tf_op jit(solution)/shard_map/ppermute | solution.py:623
  9.7 0.1 copy.6
  9.8 0.7 %collective-permute-done.4.west_far_ref = f32[32,128]{1,0:T(8,128)S(1)} collective-permute-done((f32[32,128]{1,0:T(8,128)S(1)}, f32[32,128]{1,0:T(8,128)S(1)}, u32[]{:S(2)}, u32[]{:S(2)}) %collective-permute-start.4) | collective-permute-done | bytes 16416 | tf_op jit(solution)/shard_map/ppermute | solution.py:625
  10.5 0.4 %collective-permute-done.3.west_near_ref = f32[32,128]{1,0:T(8,128)S(1)} collective-permute-done((f32[32,128]{1,0:T(8,128)S(1)}, f32[32,128]{1,0:T(8,128)S(1)}, u32[]{:S(2)}, u32[]{:S(2)}) %collective-permute-start.3) | collective-permute-done | bytes 16416 | tf_op jit(solution)/shard_map/ppermute | solution.py:628
  10.9 0.0 collective-permute-done.lat_near_ref
  10.9 0.0 collective-permute-done.1.lat_far_ref
  10.9 0.1 broadcast_in_dim.4.scale_ref
  11.0 1.7 %descend.1 = (f32[32,8,128]{2,1,0:T(8,128)}, f32[128,128]{1,0:T(8,128)S(1)}) custom-call(f32[3,64,256]{2,1,0:T(8,128)S(1)} %get-tuple-element.48.own_ref, f32[32,896]{1,0:T(8,128)S(1)} %collective-permute-done.lat_near_ref, f32[32,896]{1,0:T(8,128)S(1)} %collective-permute-done.1.lat_far_ref, f32[64,128]{1,0:T(8,128)S(1)} %collective-permute-done.2.west_ref, ...), custom_call_target="tpu_custom_call" | custom-call | tf_op jit(solution)/shard_map/descend/pallas_call | solution.py:642
  12.7 4.1 %all-to-all-start = ((f32[32,8,128]{2,1,0:T(8,128)}), f32[32,8,128]{2,1,0:T(8,128)S(1)}, u32[]{:S(2)}, u32[]{:S(2)}) async-start(f32[32,8,128]{2,1,0:T(8,128)} %get-tuple-element.53), calls=%async_computation | async-start | bytes 262144 | tf_op jit(solution)/shard_map/all_to_all | solution.py:658
  16.8 0.1 cosine_divide_fusion
  16.9 4.6 %collective-permute-start.5 = (f32[128,128]{1,0:T(8,128)S(1)}, f32[128,128]{1,0:T(8,128)S(1)}, u32[]{:S(2)}, u32[]{:S(2)}) collective-permute-start(f32[128,128]{1,0:T(8,128)S(1)} %get-tuple-element.55), channel_id=1, source_target_pairs={{4,0},{8,4},{12,8},{16,12},{20,16},{24,20},{28,24},{0,28},{5,1},{9... | collective-permute-start | bytes 196616 | tf_op jit(solution)/shard_map/ppermute | solution.py:657
  21.5 0.1 copy.7
  21.6 0.1 broadcast_in_dim.5.scale_ref
  21.7 1.2 %hold.1 = (f32[16,8,384]{2,1,0:T(8,128)S(1)}, f32[16,8,384]{2,1,0:T(8,128)S(1)}, f32[16,8,384]{2,1,0:T(8,128)S(1)}, f32[16,8,384]{2,1,0:T(8,128)S(1)}, f32[16,8,...) custom-call(f32[3,64,256]{2,1,0:T(8,128)S(1)} %get-tuple-element.48., ...), custom_call_target="tpu_custom_call" | custom-call | bytes 62914560 | tf_op jit(solution)/shard_map/hold/pallas_call | solution.py:665
  22.9 0.5 %collective-permute-done.5.east_ref = f32[128,128]{1,0:T(8,128)S(1)} collective-permute-done((f32[128,128]{1,0:T(8,128)S(1)}, f32[128,128]{1,0:T(8,128)S(1)}, u32[]{:S(2)}, u32[]{:S(2)}) %collective-permute-start.5) | collective-permute-done | bytes 65568 | tf_op jit(solution)/shard_map/ppermute | solution.py:657
  23.4 0.8 %patch.1 = (f32[16,8,384]{2,1,0:T(8,128)S(1)}, f32[16,8,384]{2,1,0:T(8,128)S(1)}, f32[16,8,384]{2,1,0:T(8,128)S(1)}, f32[16,8,384]{2,1,0:T(8,128)S(1)}, f32[16,8...) custom-call(f32[3,16,8,128]{3,2,1,0:T(8,128)S(1)} %get-tuple-element, ...), custom_call_target="tpu_custom_call" | custom-call | tf_op jit(solution)/shard_map/patch/pallas_call | solution.py:676
  24.2 0.3 %all-to-all-done.blocks_ref = f32[32,8,128]{2,1,0:T(8,128)S(1)} async-done(((f32[32,8,128]{2,1,0:T(8,128)}), f32[32,8,128]{2,1,0:T(8,128)S(1)}, u32[]{:S(2)}, u32[]{:S(2)}) %all-to-all-start) | async-done | bytes 131104 | tf_op jit(solution)/shard_map/all_to_all | solution.py:658
  24.5 2.4 %ascend.1 = (f32[64,256]{1,0:T(8,128)}, f32[64,256]{1,0:T(8,128)}) custom-call(f32[32,8,128]{2,1,0:T(8,128)S(1)} %all-to-all-done.blocks_ref, f32[16,8,384]{2,1,0:T(8,128)S(1)} %get-tuple-element.75.rest_0_, f32[16,8,384]{2,1,0:T(8,128)S(1)} %get-tuple-element.76.rest_1_, f32[16,8,384]{2,1,0:T(8,128)S(1)} %get-tuple-element.77.rest_2_, ...), custom_call_target="tpu_custom_call" | custom-call | tf_op jit(solution)/shard_map/ascend/pallas_call | solution.py:686
  (8 shorter events, 0.1 us)
Async XLA Ops:
  1.7 8.0 %collective-permute-start.2 = (f32[64,128]{1,0:T(8,128)S(1)}, f32[64,128]{1,0:T(8,128)S(1)}, u32[]{:S(2)}, u32[]{:S(2)}) collective-permute-start(f32[64,128]{1,0:T(8,128)S(1)} %get-tuple-element.52.east_edge_ref), channel_id=1, source_target_pairs={{0,4},{4,8},{8,12},{12,16},{16,20},{20,24},{24,28},{28,0},{1,5},{5... | collective-permute-start | bytes 98312 | tf_op jit(solution)/shard_map/ppermute | solution.py:623
  4.8 6.1 %collective-permute-start.1 = (f32[32,896]{1,0:T(8,128)S(1)}, f32[32,896]{1,0:T(8,128)S(1)}, u32[]{:S(2)}, u32[]{:S(2)}) collective-permute-start(f32[32,896]{1,0:T(8,128)S(1)} %get-tuple-element.51.rows_ref), channel_id=1, source_target_pairs={{0,4},{1,2},{2,1},{3,7},{4,0},{5,6},{6,5},{7,3},{8,12},{9,10},{10,... | collective-permute-start | bytes 344072 | tf_op jit(solution)/shard_map/ppermute | solution.py:624
  6.3 4.1 %collective-permute-start.4 = (f32[32,128]{1,0:T(8,128)S(1)}, f32[32,128]{1,0:T(8,128)S(1)}, u32[]{:S(2)}, u32[]{:S(2)}) collective-permute-start(f32[32,128]{1,0:T(8,128)S(1)} %prepare_corner.1), channel_id=1, source_target_pairs={{0,4},{1,6},{2,5},{3,7},{4,0},{5,10},{6,9},{7,3},{8,12},{9,14},{10... | collective-permute-start | bytes 49160 | tf_op jit(solution)/shard_map/ppermute | solution.py:625
  6.9 4.0 %collective-permute-start = (f32[32,896]{1,0:T(8,128)S(1)}, f32[32,896]{1,0:T(8,128)S(1)}, u32[]{:S(2)}, u32[]{:S(2)}) collective-permute-start(f32[32,896]{1,0:T(8,128)S(1)} %get-tuple-element.50), channel_id=1, source_target_pairs={{0,1},{1,0},{2,3},{3,2},{4,5},{5,4},{6,7},{7,6},{8,9},{9,8},{10,11... | collective-permute-start | bytes 344072 | tf_op jit(solution)/shard_map/ppermute | solution.py:626
  9.7 1.2 %collective-permute-start.3 = (f32[32,128]{1,0:T(8,128)S(1)}, f32[32,128]{1,0:T(8,128)S(1)}, u32[]{:S(2)}, u32[]{:S(2)}) collective-permute-start(f32[32,128]{1,0:T(8,128)S(1)} %slice_select_fusion), channel_id=1, source_target_pairs={{0,1},{1,0},{2,3},{3,2},{4,5},{5,4},{6,7},{7,6},{8,9},{9,8},{10,11... | collective-permute-start | bytes 49160 | tf_op jit(solution)/shard_map/ppermute | solution.py:628
  12.7 11.9 %all-to-all-start = ((f32[32,8,128]{2,1,0:T(8,128)}), f32[32,8,128]{2,1,0:T(8,128)S(1)}, u32[]{:S(2)}, u32[]{:S(2)}) async-start(f32[32,8,128]{2,1,0:T(8,128)} %get-tuple-element.53), calls=%async_computation | async-start | bytes 262144 | tf_op jit(solution)/shard_map/all_to_all | solution.py:658
  16.9 6.5 %collective-permute-start.5 = (f32[128,128]{1,0:T(8,128)S(1)}, f32[128,128]{1,0:T(8,128)S(1)}, u32[]{:S(2)}, u32[]{:S(2)}) collective-permute-start(f32[128,128]{1,0:T(8,128)S(1)} %get-tuple-element.55), channel_id=1, source_target_pairs={{4,0},{8,4},{12,8},{16,12},{20,16},{24,20},{28,24},{0,28},{5,1},{9... | collective-permute-start | bytes 196616 | tf_op jit(solution)/shard_map/ppermute | solution.py:657

commit v9 on v8

--- a/solution.py
+++ b/solution.py
@@ -669,7 +669,6 @@
         out_specs=[vmem] * (1 + len(held_shapes)),
         scratch_shapes=[grid],
         compiler_params=params,
-        cost_estimate=pl.CostEstimate(flops=0, bytes_accessed=60 * 1024 * 1024, transcendentals=0),
         name="hold",
     )(own, lat_near, lat_far, west_halo, west_near, west_far, fine_scale)
     held, raw = held[:-1], held[-1]

time: 27.1 us -> 27.1 us (level)
  no operation moved by 1% of the time
where the time goes in v9:
time: 27.1 us; the launch traced here: 26.9 us
  starting transfers between devices  14.5 us (54%)
  Pallas kernels  7.11 us (26%)
  waiting for transfers between devices  4.02 us (15%)
  between operations  0.72 us (3%)
  local copies, waits for them, and re-layouts  0.33 us (1%)
  other arithmetic  0.28 us (1%)
    ppermute x1, starting transfers between devices, on_device(): east_halo = lax.ppermute(edges, 'lon', westward)  4.6 us
    all_to_all x1, starting transfers between devices, on_device(): blocks = lax.all_to_all(packed, ('lat', 'lon'), 0, 0, tiled=True)  4.12 us
    ppermute x1, starting transfers between devices, on_device(): west_halo = lax.ppermute(east_edge, 'lon', eastward)  3.02 us
    pallas_call x1, Pallas kernels, on_device(): pl.pallas_call(functools.partial(ascend, lat_count, lon_count), out_shape...  2.38 us
    ppermute x1, waiting for transfers between devices, on_device(): west_halo = lax.ppermute(east_edge, 'lon', eastward)  2.07 us
    pallas_call x1, Pallas kernels, on_device(): pl.pallas_call(functools.partial(descend, lat_count), out_shape=[jax.Shap...  1.67 us
    ppermute x1, starting transfers between devices, on_device(): lax.ppermute(lat_far, ('lon', 'lat'), far_pairs(lon_count, lat_count, 0))  1.58 us
    pallas_call x1, Pallas kernels, on_device(): pl.pallas_call(functools.partial(hold, lat_count), out_shape=held_shapes...  1.19 us
  transfers between devices with their start and end apart: 7, of which 5 were waited for; matrix products, arithmetic and copies ran while one was open for 2% of the time, Pallas kernels for 7%

profile of v9, /device:TPU:0, one launch (start us, length us, event | category | flops | bytes accessed | tf_op | source)
XLA Modules:
  0.0 26.9 jit_solution(8422706412472817478)
XLA Ops:
  0.6 1.1 %prepare.1 = (f32[3,64,256]{2,1,0:T(8,128)S(1)}, f32[64,128]{1,0:T(8,128)S(1)}, f32[64,128]{1,0:T(8,128)S(1)}) custom-call(f32[64,256]{1,0:T(8,128)} %forcing_ref.1, f32[64,256]{1,0:T(8,128)} %surface_ref.1, s32[64,256]{1,0:T(8,128)} %sea_ref.1, s32[64,256]{1,0:T(8,128)} %levels_ref.1), custom_call_target="tpu_custom_call" | custom-call | tf_op jit(solution)/shard_map/prepare/pallas_call | solution.py:584
  1.7 3.0 %collective-permute-start.2 = (f32[64,128]{1,0:T(8,128)S(1)}, f32[64,128]{1,0:T(8,128)S(1)}, u32[]{:S(2)}, u32[]{:S(2)}) collective-permute-start(f32[64,128]{1,0:T(8,128)S(1)} %get-tuple-element.52.east_edge_ref), channel_id=1, source_target_pairs={{0,4},{4,8},{8,12},{12,16},{16,20},{20,24},{24,28},{28,0},{1,5},{5... | collective-permute-start | bytes 98312 | tf_op jit(solution)/shard_map/ppermute | solution.py:623
  4.8 1.6 %collective-permute-start.1 = (f32[32,896]{1,0:T(8,128)S(1)}, f32[32,896]{1,0:T(8,128)S(1)}, u32[]{:S(2)}, u32[]{:S(2)}) collective-permute-start(f32[32,896]{1,0:T(8,128)S(1)} %get-tuple-element.51.rows_ref), channel_id=1, source_target_pairs={{0,4},{1,2},{2,1},{3,7},{4,0},{5,6},{6,5},{7,3},{8,12},{9,10},{10,... | collective-permute-start | bytes 344072 | tf_op jit(solution)/shard_map/ppermute | solution.py:624
  6.3 0.5 %collective-permute-start.4 = (f32[32,128]{1,0:T(8,128)S(1)}, f32[32,128]{1,0:T(8,128)S(1)}, u32[]{:S(2)}, u32[]{:S(2)}) collective-permute-start(f32[32,128]{1,0:T(8,128)S(1)} %prepare_corner.1), channel_id=1, source_target_pairs={{0,4},{1,6},{2,5},{3,7},{4,0},{5,10},{6,9},{7,3},{8,12},{9,14},{10... | collective-permute-start | bytes 49160 | tf_op jit(solution)/shard_map/ppermute | solution.py:625
  6.9 0.6 %collective-permute-start = (f32[32,896]{1,0:T(8,128)S(1)}, f32[32,896]{1,0:T(8,128)S(1)}, u32[]{:S(2)}, u32[]{:S(2)}) collective-permute-start(f32[32,896]{1,0:T(8,128)S(1)} %get-tuple-element.50), channel_id=1, source_target_pairs={{0,1},{1,0},{2,3},{3,2},{4,5},{5,4},{6,7},{7,6},{8,9},{9,8},{10,11... | collective-permute-start | bytes 344072 | tf_op jit(solution)/shard_map/ppermute | solution.py:626
  7.5 0.1 cosine_divide_fusion.1
  7.6 2.1 %collective-permute-done.2.west_ref = f32[64,128]{1,0:T(8,128)S(1)} collective-permute-done((f32[64,128]{1,0:T(8,128)S(1)}, f32[64,128]{1,0:T(8,128)S(1)}, u32[]{:S(2)}, u32[]{:S(2)}) %collective-permute-start.2) | collective-permute-done | bytes 32800 | tf_op jit(solution)/shard_map/ppermute | solution.py:623
  9.7 0.1 copy.6
  9.8 0.7 %collective-permute-done.4.west_far_ref = f32[32,128]{1,0:T(8,128)S(1)} collective-permute-done((f32[32,128]{1,0:T(8,128)S(1)}, f32[32,128]{1,0:T(8,128)S(1)}, u32[]{:S(2)}, u32[]{:S(2)}) %collective-permute-start.4) | collective-permute-done | bytes 16416 | tf_op jit(solution)/shard_map/ppermute | solution.py:625
  10.5 0.4 %collective-permute-done.3.west_near_ref = f32[32,128]{1,0:T(8,128)S(1)} collective-permute-done((f32[32,128]{1,0:T(8,128)S(1)}, f32[32,128]{1,0:T(8,128)S(1)}, u32[]{:S(2)}, u32[]{:S(2)}) %collective-permute-start.3) | collective-permute-done | bytes 16416 | tf_op jit(solution)/shard_map/ppermute | solution.py:628
  10.9 0.0 collective-permute-done.lat_near_ref
  10.9 0.0 collective-permute-done.1.lat_far_ref
  10.9 0.1 broadcast_in_dim.4.scale_ref
  11.0 1.7 %descend.1 = (f32[32,8,128]{2,1,0:T(8,128)}, f32[128,128]{1,0:T(8,128)S(1)}) custom-call(f32[3,64,256]{2,1,0:T(8,128)S(1)} %get-tuple-element.48.own_ref, f32[32,896]{1,0:T(8,128)S(1)} %collective-permute-done.lat_near_ref, f32[32,896]{1,0:T(8,128)S(1)} %collective-permute-done.1.lat_far_ref, f32[64,128]{1,0:T(8,128)S(1)} %collective-permute-done.2.west_ref, ...), custom_call_target="tpu_custom_call" | custom-call | tf_op jit(solution)/shard_map/descend/pallas_call | solution.py:642
  12.7 4.1 %all-to-all-start = ((f32[32,8,128]{2,1,0:T(8,128)}), f32[32,8,128]{2,1,0:T(8,128)S(1)}, u32[]{:S(2)}, u32[]{:S(2)}) async-start(f32[32,8,128]{2,1,0:T(8,128)} %get-tuple-element.53), calls=%async_computation | async-start | bytes 262144 | tf_op jit(solution)/shard_map/all_to_all | solution.py:658
  16.8 0.1 cosine_divide_fusion
  16.9 4.6 %collective-permute-start.5 = (f32[128,128]{1,0:T(8,128)S(1)}, f32[128,128]{1,0:T(8,128)S(1)}, u32[]{:S(2)}, u32[]{:S(2)}) collective-permute-start(f32[128,128]{1,0:T(8,128)S(1)} %get-tuple-element.55), channel_id=1, source_target_pairs={{4,0},{8,4},{12,8},{16,12},{20,16},{24,20},{28,24},{0,28},{5,1},{9... | collective-permute-start | bytes 196616 | tf_op jit(solution)/shard_map/ppermute | solution.py:657
  21.5 0.1 copy.7
  21.6 0.1 broadcast_in_dim.5.scale_ref
  21.7 1.2 %hold.1 = (f32[16,8,384]{2,1,0:T(8,128)S(1)}, f32[16,8,384]{2,1,0:T(8,128)S(1)}, f32[16,8,384]{2,1,0:T(8,128)S(1)}, f32[16,8,384]{2,1,0:T(8,128)S(1)}, f32[16,8,...) custom-call(f32[3,64,256]{2,1,0:T(8,128)S(1)} %get-tuple-element.48., ...), custom_call_target="tpu_custom_call" | custom-call | tf_op jit(solution)/shard_map/hold/pallas_call | solution.py:665
  22.9 0.5 %collective-permute-done.5.east_ref = f32[128,128]{1,0:T(8,128)S(1)} collective-permute-done((f32[128,128]{1,0:T(8,128)S(1)}, f32[128,128]{1,0:T(8,128)S(1)}, u32[]{:S(2)}, u32[]{:S(2)}) %collective-permute-start.5) | collective-permute-done | bytes 65568 | tf_op jit(solution)/shard_map/ppermute | solution.py:657
  23.4 0.8 %patch.1 = (f32[16,8,384]{2,1,0:T(8,128)S(1)}, f32[16,8,384]{2,1,0:T(8,128)S(1)}, f32[16,8,384]{2,1,0:T(8,128)S(1)}, f32[16,8,384]{2,1,0:T(8,128)S(1)}, f32[16,8...) custom-call(f32[3,16,8,128]{3,2,1,0:T(8,128)S(1)} %get-tuple-element, ...), custom_call_target="tpu_custom_call" | custom-call | tf_op jit(solution)/shard_map/patch/pallas_call | solution.py:675
  24.2 0.3 %all-to-all-done.blocks_ref = f32[32,8,128]{2,1,0:T(8,128)S(1)} async-done(((f32[32,8,128]{2,1,0:T(8,128)}), f32[32,8,128]{2,1,0:T(8,128)S(1)}, u32[]{:S(2)}, u32[]{:S(2)}) %all-to-all-start) | async-done | bytes 131104 | tf_op jit(solution)/shard_map/all_to_all | solution.py:658
  24.5 2.4 %ascend.1 = (f32[64,256]{1,0:T(8,128)}, f32[64,256]{1,0:T(8,128)}) custom-call(f32[32,8,128]{2,1,0:T(8,128)S(1)} %all-to-all-done.blocks_ref, f32[16,8,384]{2,1,0:T(8,128)S(1)} %get-tuple-element.75.rest_0_, f32[16,8,384]{2,1,0:T(8,128)S(1)} %get-tuple-element.76.rest_1_, f32[16,8,384]{2,1,0:T(8,128)S(1)} %get-tuple-element.77.rest_2_, ...), custom_call_target="tpu_custom_call" | custom-call | tf_op jit(solution)/shard_map/ascend/pallas_call | solution.py:685
  (8 shorter events, 0.1 us)
Async XLA Ops:
  1.7 8.0 %collective-permute-start.2 = (f32[64,128]{1,0:T(8,128)S(1)}, f32[64,128]{1,0:T(8,128)S(1)}, u32[]{:S(2)}, u32[]{:S(2)}) collective-permute-start(f32[64,128]{1,0:T(8,128)S(1)} %get-tuple-element.52.east_edge_ref), channel_id=1, source_target_pairs={{0,4},{4,8},{8,12},{12,16},{16,20},{20,24},{24,28},{28,0},{1,5},{5... | collective-permute-start | bytes 98312 | tf_op jit(solution)/shard_map/ppermute | solution.py:623
  4.8 6.1 %collective-permute-start.1 = (f32[32,896]{1,0:T(8,128)S(1)}, f32[32,896]{1,0:T(8,128)S(1)}, u32[]{:S(2)}, u32[]{:S(2)}) collective-permute-start(f32[32,896]{1,0:T(8,128)S(1)} %get-tuple-element.51.rows_ref), channel_id=1, source_target_pairs={{0,4},{1,2},{2,1},{3,7},{4,0},{5,6},{6,5},{7,3},{8,12},{9,10},{10,... | collective-permute-start | bytes 344072 | tf_op jit(solution)/shard_map/ppermute | solution.py:624
  6.3 4.1 %collective-permute-start.4 = (f32[32,128]{1,0:T(8,128)S(1)}, f32[32,128]{1,0:T(8,128)S(1)}, u32[]{:S(2)}, u32[]{:S(2)}) collective-permute-start(f32[32,128]{1,0:T(8,128)S(1)} %prepare_corner.1), channel_id=1, source_target_pairs={{0,4},{1,6},{2,5},{3,7},{4,0},{5,10},{6,9},{7,3},{8,12},{9,14},{10... | collective-permute-start | bytes 49160 | tf_op jit(solution)/shard_map/ppermute | solution.py:625
  6.9 4.0 %collective-permute-start = (f32[32,896]{1,0:T(8,128)S(1)}, f32[32,896]{1,0:T(8,128)S(1)}, u32[]{:S(2)}, u32[]{:S(2)}) collective-permute-start(f32[32,896]{1,0:T(8,128)S(1)} %get-tuple-element.50), channel_id=1, source_target_pairs={{0,1},{1,0},{2,3},{3,2},{4,5},{5,4},{6,7},{7,6},{8,9},{9,8},{10,11... | collective-permute-start | bytes 344072 | tf_op jit(solution)/shard_map/ppermute | solution.py:626
  9.7 1.2 %collective-permute-start.3 = (f32[32,128]{1,0:T(8,128)S(1)}, f32[32,128]{1,0:T(8,128)S(1)}, u32[]{:S(2)}, u32[]{:S(2)}) collective-permute-start(f32[32,128]{1,0:T(8,128)S(1)} %slice_select_fusion), channel_id=1, source_target_pairs={{0,1},{1,0},{2,3},{3,2},{4,5},{5,4},{6,7},{7,6},{8,9},{9,8},{10,11... | collective-permute-start | bytes 49160 | tf_op jit(solution)/shard_map/ppermute | solution.py:628
  12.7 11.9 %all-to-all-start = ((f32[32,8,128]{2,1,0:T(8,128)}), f32[32,8,128]{2,1,0:T(8,128)S(1)}, u32[]{:S(2)}, u32[]{:S(2)}) async-start(f32[32,8,128]{2,1,0:T(8,128)} %get-tuple-element.53), calls=%async_computation | async-start | bytes 262144 | tf_op jit(solution)/shard_map/all_to_all | solution.py:658
  16.9 6.5 %collective-permute-start.5 = (f32[128,128]{1,0:T(8,128)S(1)}, f32[128,128]{1,0:T(8,128)S(1)}, u32[]{:S(2)}, u32[]{:S(2)}) collective-permute-start(f32[128,128]{1,0:T(8,128)S(1)} %get-tuple-element.55), channel_id=1, source_target_pairs={{4,0},{8,4},{12,8},{16,12},{20,16},{24,20},{28,24},{0,28},{5,1},{9... | collective-permute-start | bytes 196616 | tf_op jit(solution)/shard_map/ppermute | solution.py:657

commit v10 on v8

--- a/solution.py
+++ b/solution.py
@@ -118,7 +118,7 @@
     west_edge_ref[...] = west_edge
 
 
-def prepare_corner(east_edge_ref, rows_ref, diagonal_edge_ref):
+def prepare_corner(east_edge_ref, diagonal_edge_ref):
     rows = east_edge_ref.shape[0]
     odd = jnp.broadcast_to(lax.rem(lax.axis_index("lat"), 2), diagonal_edge_ref.shape) > 0
     diagonal_edge_ref[...] = jnp.where(odd, east_edge_ref[pl.ds(rows - HALO, HALO), :], east_edge_ref[pl.ds(0, HALO), :])
@@ -132,12 +132,23 @@
         south_edge, north_edge = own_ref[f, south, :], own_ref[f, north, :]
         part = slice(f * cols, (f + 1) * cols)
         lat_near_ref[:, part] = jnp.where(odd, south_edge, north_edge)
-        lat_far_ref[:, part] = jnp.where(odd, north_edge, south_edge)
+        lat_far_ref[:, part] = jnp.where(odd[:REACH], north_edge[HALO - REACH :], south_edge[:REACH])
     odd = odd[:, :LANES]
     south_edge, north_edge = west_edge_ref[south, :], west_edge_ref[north, :]
-    part = slice(FIELDS * cols, FIELDS * cols + LANES)
-    lat_near_ref[:, part] = jnp.where(odd, south_edge, north_edge)
-    lat_far_ref[:, part] = jnp.where(odd, north_edge, south_edge)
+    edge = FIELDS * cols
+    lat_near_ref[:, edge : edge + LANES] = jnp.where(odd, south_edge, north_edge)
+    far_edge = jnp.where(odd, north_edge, south_edge)
+    lat_far_ref[:, edge : edge + LANES] = far_edge[:REACH]
+    lat_far_ref[:, edge + LANES :] = far_edge[REACH:]
+
+
+def prepare_rest(own_ref, corner_ref, lat_rest_ref):
+    rows, cols = own_ref.shape[1:]
+    odd = jnp.broadcast_to(lax.rem(lax.axis_index("lat"), 2), (HALO - REACH, cols)) > 0
+    for f in range(FIELDS):
+        north_part = own_ref[f, pl.ds(rows - HALO, HALO - REACH), :]
+        south_part = own_ref[f, pl.ds(REACH, HALO - REACH), :]
+        lat_rest_ref[:, f * cols : (f + 1) * cols] = jnp.where(odd, north_part, south_part)
 
 
 def fine_faces(depth, across, along):
@@ -213,7 +224,7 @@
     return source, (plus, minus)
 
 
-def lay_out(lat_count, own_ref, lat_near_ref, lat_far_ref, west_ref, west_near_ref, west_far_ref, scale_ref, grid_ref):
+def lay_out(lat_count, own_ref, lat_near_ref, lat_far_ref, lat_rest_ref, west_ref, west_near_ref, west_far_ref, scale_ref, grid_ref):
     rows, cols = own_ref.shape[1], own_ref.shape[2]
     columns, height = grid_ref.shape[1], grid_ref.shape[2]
     count = height // TILE
@@ -234,16 +245,23 @@
     parts = (
         (0, rows, None, west_ref[...], False),
         (near_row, halo, lat_near_ref.at[near_part], west_near_ref[near_part, :], False),
-        (far_row, halo, lat_far_ref.at[far_part], west_far_ref[far_part, :], True),
+        (far_row, halo, lat_far_ref, west_far_ref[far_part, :], True),
     )
     for first, size, body_ref, west, far in parts:
         slot = iota((size, LANES), 1) // HALO
         for f in range(FIELDS):
             for c in range(own_columns):
+                part = slice(f * cols + c * LANES, f * cols + (c + 1) * LANES)
+                if far and halo > REACH:
+                    seam = far_row + pl.multiple_of((1 - lat_odd) * (halo - REACH), TILE)
+                    rest = far_row + pl.multiple_of(lat_odd * REACH, TILE)
+                    grid_ref[f, c, pl.ds(seam, REACH), :] = inside(lat_far_ref[:, part], far)
+                    grid_ref[f, c, pl.ds(rest, halo - REACH), :] = inside(lat_rest_ref[:, part], far)
+                    continue
                 if body_ref is None:
                     value = own_ref[f, :, c * LANES : (c + 1) * LANES]
                 else:
-                    value = body_ref[:, f * cols + c * LANES : f * cols + (c + 1) * LANES]
+                    value = body_ref[:, part]
                 grid_ref[f, c, pl.ds(first, size), :] = inside(value, far)
             side = jnp.where(slot == (f + last) % (last + 1), west, 0.0)
             grid_ref[f, own_columns, pl.ds(first, size), :] = inside(lane_shift(side, f * HALO), far)
@@ -279,9 +297,9 @@
     return level_refs, rest[KEPT * LEVELS + 1 :]
 
 
-def hold(lat_count, own_ref, lat_near_ref, lat_far_ref, west_ref, west_near_ref, west_far_ref, scale_ref, *rest):
+def hold(lat_count, own_ref, lat_near_ref, lat_far_ref, lat_rest_ref, west_ref, west_near_ref, west_far_ref, scale_ref, *rest):
     level_refs, (raw_ref, grid_ref) = split_refs(rest)
-    values = lay_out(lat_count, own_ref, lat_near_ref, lat_far_ref, west_ref, west_near_ref, west_far_ref, scale_ref, grid_ref)
+    values = lay_out(lat_count, own_ref, lat_near_ref, lat_far_ref, lat_rest_ref, west_ref, west_near_ref, west_far_ref, scale_ref, grid_ref)
     cols = own_ref.shape[2]
     for f in range(FIELDS):
         for t, value in enumerate(values[f]):
@@ -341,13 +359,14 @@
     edge = slice(FIELDS * own_ref.shape[2], FIELDS * own_ref.shape[2] + LANES)
     edge_ref[pl.ds(0, rows), :] = west_edge_ref[...]
     edge_ref[pl.ds(rows, HALO), :] = lat_near_ref[:, edge]
-    edge_ref[pl.ds(rows + HALO, HALO), :] = lat_far_ref[:, edge]
+    edge_ref[pl.ds(rows + HALO, REACH), :] = lat_far_ref[:, edge]
+    edge_ref[pl.ds(rows + HALO + REACH, HALO - REACH), :] = lat_far_ref[:, edge.stop :]
     lon_index = lax.axis_index("lon")
     cols = own_ref.shape[2]
     own_columns = cols // LANES
     columns = grid_ref.shape[1]
     depth, source_term, source, across, along = lay_out(
-        lat_count, own_ref, lat_near_ref, lat_far_ref, west_ref, west_near_ref, west_far_ref, scale_ref, grid_ref
+        lat_count, own_ref, lat_near_ref, lat_far_ref, None, west_ref, west_near_ref, west_far_ref, scale_ref, grid_ref
     )
     levels = all_coefficients(depth, source_term, across, along)
     sides = None
@@ -603,7 +622,10 @@
 
     lat_near, lat_far = pl.pallas_call(
         prepare_rows,
-        out_shape=[jax.ShapeDtypeStruct((HALO, FIELDS * cols + LANES), f32)] * 2,
+        out_shape=[
+            jax.ShapeDtypeStruct((HALO, FIELDS * cols + LANES), f32),
+            jax.ShapeDtypeStruct((REACH, FIELDS * cols + 2 * LANES), f32),
+        ],
         in_specs=[vmem] * 2,
         out_specs=[vmem] * 2,
         compiler_params=params,
@@ -613,17 +635,28 @@
     diagonal_edge = pl.pallas_call(
         prepare_corner,
         out_shape=jax.ShapeDtypeStruct((HALO, LANES), f32),
+        in_specs=[vmem],
+        out_specs=vmem,
+        compiler_params=params,
+        name="prepare_corner",
+    )(east_edge)
+    lat_rest = pl.pallas_call(
+        prepare_rest,
+        out_shape=jax.ShapeDtypeStruct((HALO - REACH, FIELDS * cols), f32),
         in_specs=[vmem] * 2,
         out_specs=vmem,
         compiler_params=params,
-        name="prepare_corner",
-    )(east_edge, lat_far)
+        name="prepare_rest",
+    )(own, diagonal_edge)
+
     eastward = [(i, (i + 1) % lon_count) for i in range(lon_count)]
     westward = [(target, source) for source, target in eastward]
     west_halo = lax.ppermute(east_edge, "lon", eastward)
     lat_far = lax.ppermute(lat_far, ("lon", "lat"), far_pairs(lon_count, lat_count, 0))
     west_far = lax.ppermute(diagonal_edge, ("lon", "lat"), far_pairs(lon_count, lat_count, 1))
     lat_near = lax.ppermute(lat_near, "lat", near_pairs(lat_count))
+    lat_rest, west_halo = lax.optimization_barrier((lat_rest, west_halo))
+    lat_rest = lax.ppermute(lat_rest, ("lon", "lat"), far_pairs(lon_count, lat_count, 0))
     odd = lat_index % 2 == 1
     west_near = lax.ppermute(
         jnp.where(odd, west_halo[:HALO], west_halo[rows - HALO :]), "lat", near_pairs(lat_count)
@@ -655,6 +688,7 @@
         name="descend",
     )(own, lat_near, lat_far, west_halo, west_near, west_far, west_edge, scales(REACH))
     east_halo = lax.ppermute(edges, "lon", westward)
+    packed, lat_rest = lax.optimization_barrier((packed, lat_rest))
     blocks = lax.all_to_all(packed, ("lat", "lon"), 0, 0, tiled=True)
 
     level_shapes = []
@@ -665,13 +699,13 @@
     held = pl.pallas_call(
         functools.partial(hold, lat_count),
         out_shape=held_shapes + [jax.ShapeDtypeStruct((FIELDS, count, TILE, LANES), f32)],
-        in_specs=[vmem] * 7,
+        in_specs=[vmem] * 8,
         out_specs=[vmem] * (1 + len(held_shapes)),
         scratch_shapes=[grid],
         compiler_params=params,
         cost_estimate=pl.CostEstimate(flops=0, bytes_accessed=60 * 1024 * 1024, transcendentals=0),
         name="hold",
-    )(own, lat_near, lat_far, west_halo, west_near, west_far, fine_scale)
+    )(own, lat_near, lat_far, lat_rest, west_halo, west_near, west_far, fine_scale)
     held, raw = held[:-1], held[-1]
     held = pl.pallas_call(
         functools.partial(patch, lat_count),

time: 27.1 us -> 27 us (level)
  starting transfers between devices: 14.5 us -> 13.2 us
  waiting for transfers between devices: 4.02 us -> 5.11 us
    all_to_all x1, starting transfers between devices: 4.12 us -> 2.85 us  [on_device(): blocks = lax.all_to_all(packed, ('lat', 'lon'), 0, 0, tiled=True)]
    ppermute x0 -> x1, waiting for transfers between devices: none -> 1.2 us  [on_device(): lax.ppermute(lat_rest, ('lon', 'lat'), far_pairs(lon_count, lat_count, 0))]
    ppermute x1, starting transfers between devices: 1.58 us -> 0.57 us  [on_device(): lax.ppermute(lat_far, ('lon', 'lat'), far_pairs(lon_count, lat_count, 0))]
    ppermute x1, starting transfers between devices: 0.51 us -> 1.52 us  [on_device(): lax.ppermute(diagonal_edge, ('lon', 'lat'), far_pairs(lon_count, lat_coun...]
    ppermute x1, waiting for transfers between devices: 0.68 us -> 0.01 us  [on_device(): lax.ppermute(diagonal_edge, ('lon', 'lat'), far_pairs(lon_count, lat_coun...]
    ppermute x1, waiting for transfers between devices: 0.4 us -> 1 us  [on_device(): lax.ppermute(jnp.where(odd, west_halo[:HALO], west_halo[rows - HALO:]), '...]
  transfers between devices with their start and end apart: 7 -> 8, of which waited for: 5 -> 5; matrix products, arithmetic and copies ran while one was open for 2% -> 2% of each run, Pallas kernels for 7% -> 14%
where the time goes in v10:
time: 27 us; the launch traced here: 26.8 us
  starting transfers between devices  13.2 us (49%)
  Pallas kernels  7.1 us (26%)
  waiting for transfers between devices  5.11 us (19%)
  between operations  0.74 us (3%)
  local copies, waits for them, and re-layouts  0.33 us (1%)
  other arithmetic  0.28 us (1%)
    ppermute x1, starting transfers between devices, on_device(): east_halo = lax.ppermute(edges, 'lon', westward)  4.6 us
    ppermute x1, starting transfers between devices, on_device(): west_halo = lax.ppermute(east_edge, 'lon', eastward)  3.02 us
    all_to_all x1, starting transfers between devices, on_device(): blocks = lax.all_to_all(packed, ('lat', 'lon'), 0, 0, tiled=True)  2.85 us
    pallas_call x1, Pallas kernels, on_device(): pl.pallas_call(functools.partial(ascend, lat_count, lon_count), out_shape...  2.38 us
    ppermute x1, waiting for transfers between devices, on_device(): west_halo = lax.ppermute(east_edge, 'lon', eastward)  2 us
    pallas_call x1, Pallas kernels, on_device(): pl.pallas_call(functools.partial(descend, lat_count), out_shape=[jax.Shap...  1.68 us
    ppermute x1, starting transfers between devices, on_device(): lax.ppermute(diagonal_edge, ('lon', 'lat'), far_pairs(lon_count, lat_coun...  1.52 us
    ppermute x1, waiting for transfers between devices, on_device(): lax.ppermute(lat_rest, ('lon', 'lat'), far_pairs(lon_count, lat_count, 0))  1.2 us
  transfers between devices with their start and end apart: 8, of which 5 were waited for; matrix products, arithmetic and copies ran while one was open for 2% of the time, Pallas kernels for 14%

profile of v10, /device:TPU:0, one launch (start us, length us, event | category | flops | bytes accessed | tf_op | source)
XLA Modules:
  0.0 26.8 jit_solution(17382039768783873505)
XLA Ops:
  0.6 1.1 %prepare.1 = (f32[3,64,256]{2,1,0:T(8,128)S(1)}, f32[64,128]{1,0:T(8,128)S(1)}, f32[64,128]{1,0:T(8,128)S(1)}) custom-call(f32[64,256]{1,0:T(8,128)} %forcing_ref.1, f32[64,256]{1,0:T(8,128)} %surface_ref.1, s32[64,256]{1,0:T(8,128)} %sea_ref.1, s32[64,256]{1,0:T(8,128)} %levels_ref.1), custom_call_target="tpu_custom_call" | custom-call | tf_op jit(solution)/shard_map/prepare/pallas_call | solution.py:603
  1.7 3.0 %collective-permute-start.2 = (f32[64,128]{1,0:T(8,128)S(1)}, f32[64,128]{1,0:T(8,128)S(1)}, u32[]{:S(2)}, u32[]{:S(2)}) collective-permute-start(f32[64,128]{1,0:T(8,128)S(1)} %get-tuple-element.56.east_edge_ref), channel_id=1, source_target_pairs={{0,4},{4,8},{8,12},{12,16},{16,20},{20,24},{24,28},{28,0},{1,5},{5... | collective-permute-start | bytes 98312 | tf_op jit(solution)/shard_map/ppermute | solution.py:654
  4.7 1.5 %collective-permute-start.4 = (f32[32,128]{1,0:T(8,128)S(1)}, f32[32,128]{1,0:T(8,128)S(1)}, u32[]{:S(2)}, u32[]{:S(2)}) collective-permute-start(f32[32,128]{1,0:T(8,128)S(1)} %prepare_corner.1.corner_ref), channel_id=1, source_target_pairs={{0,4},{1,6},{2,5},{3,7},{4,0},{5,10},{6,9},{7,3},{8,12},{9,14},{10... | collective-permute-start | bytes 49160 | tf_op jit(solution)/shard_map/ppermute | solution.py:656
  6.3 0.6 %collective-permute-start.1 = (f32[16,1024]{1,0:T(8,128)S(1)}, f32[16,1024]{1,0:T(8,128)S(1)}, u32[]{:S(2)}, u32[]{:S(2)}) collective-permute-start(f32[16,1024]{1,0:T(8,128)S(1)} %get-tuple-element.55), channel_id=1, source_target_pairs={{0,4},{1,2},{2,1},{3,7},{4,0},{5,6},{6,5},{7,3},{8,12},{9,10},{10,... | collective-permute-start | bytes 196616 | tf_op jit(solution)/shard_map/ppermute | solution.py:655
  6.9 0.6 %collective-permute-start = (f32[32,896]{1,0:T(8,128)S(1)}, f32[32,896]{1,0:T(8,128)S(1)}, u32[]{:S(2)}, u32[]{:S(2)}) collective-permute-start(f32[32,896]{1,0:T(8,128)S(1)} %get-tuple-element.54), channel_id=1, source_target_pairs={{0,1},{1,0},{2,3},{3,2},{4,5},{5,4},{6,7},{7,6},{8,9},{9,8},{10,11... | collective-permute-start | bytes 344072 | tf_op jit(solution)/shard_map/ppermute | solution.py:657
  7.5 0.1 cosine_divide_fusion.1
  7.7 2.0 %collective-permute-done.2.west_ref = f32[64,128]{1,0:T(8,128)S(1)} collective-permute-done((f32[64,128]{1,0:T(8,128)S(1)}, f32[64,128]{1,0:T(8,128)S(1)}, u32[]{:S(2)}, u32[]{:S(2)}) %collective-permute-start.2) | collective-permute-done | bytes 32800 | tf_op jit(solution)/shard_map/ppermute | solution.py:654
  9.7 0.0 collective-permute-start.3
  9.7 0.1 collective-permute-start.5
  9.8 0.1 copy.6
  9.9 1.0 %collective-permute-done.3.west_near_ref = f32[32,128]{1,0:T(8,128)S(1)} collective-permute-done((f32[32,128]{1,0:T(8,128)S(1)}, f32[32,128]{1,0:T(8,128)S(1)}, u32[]{:S(2)}, u32[]{:S(2)}) %collective-permute-start.3) | collective-permute-done | bytes 16416 | tf_op jit(solution)/shard_map/ppermute | solution.py:661
  10.9 0.1 broadcast_in_dim.4.scale_ref
  10.9 1.7 %descend.1 = (f32[32,8,128]{2,1,0:T(8,128)}, f32[128,128]{1,0:T(8,128)S(1)}) custom-call(f32[3,64,256]{2,1,0:T(8,128)S(1)} %get-tuple-element.52.own_ref, f32[32,896]{1,0:T(8,128)S(1)} %collective-permute-done.lat_near_ref, f32[16,1024]{1,0:T(8,128)S(1)} %collective-permute-done.1.lat_far_ref, f32[64,128]{1,0:T(8,128)S(1)} %collective-permute-done.2.west_ref, ...), custom_call_target="tpu_custom_call" | custom-call | tf_op jit(solution)/shard_map/descend/pallas_call | solution.py:675
  12.6 1.2 %collective-permute-done.5.lat_rest_ref = f32[16,768]{1,0:T(8,128)S(1)} collective-permute-done((f32[16,768]{1,0:T(8,128)S(1)}, f32[16,768]{1,0:T(8,128)S(1)}, u32[]{:S(2)}, u32[]{:S(2)}) %collective-permute-start.5) | collective-permute-done | bytes 49184 | tf_op jit(solution)/shard_map/ppermute | solution.py:659
  13.8 2.8 %all-to-all-start = ((f32[32,8,128]{2,1,0:T(8,128)}), f32[32,8,128]{2,1,0:T(8,128)S(1)}, u32[]{:S(2)}, u32[]{:S(2)}) async-start(f32[32,8,128]{2,1,0:T(8,128)} %get-tuple-element.60), calls=%async_computation | async-start | bytes 262144 | tf_op jit(solution)/shard_map/all_to_all | solution.py:692
  16.7 0.1 cosine_divide_fusion
  16.8 4.6 %collective-permute-start.6 = (f32[128,128]{1,0:T(8,128)S(1)}, f32[128,128]{1,0:T(8,128)S(1)}, u32[]{:S(2)}, u32[]{:S(2)}) collective-permute-start(f32[128,128]{1,0:T(8,128)S(1)} %get-tuple-element.63), channel_id=1, source_target_pairs={{4,0},{8,4},{12,8},{16,12},{20,16},{24,20},{28,24},{0,28},{5,1},{9... | collective-permute-start | bytes 196616 | tf_op jit(solution)/shard_map/ppermute | solution.py:690
  21.4 0.1 copy.7
  21.5 0.1 broadcast_in_dim.5.scale_ref
  21.6 1.2 %hold.1 = (f32[16,8,384]{2,1,0:T(8,128)S(1)}, f32[16,8,384]{2,1,0:T(8,128)S(1)}, f32[16,8,384]{2,1,0:T(8,128)S(1)}, f32[16,8,384]{2,1,0:T(8,128)S(1)}, f32[16,8,...) custom-call(f32[3,64,256]{2,1,0:T(8,128)S(1)} %get-tuple-element.52., ...), custom_call_target="tpu_custom_call" | custom-call | bytes 62914560 | tf_op jit(solution)/shard_map/hold/pallas_call | solution.py:699
  22.8 0.6 %collective-permute-done.6.east_ref = f32[128,128]{1,0:T(8,128)S(1)} collective-permute-done((f32[128,128]{1,0:T(8,128)S(1)}, f32[128,128]{1,0:T(8,128)S(1)}, u32[]{:S(2)}, u32[]{:S(2)}) %collective-permute-start.6) | collective-permute-done | bytes 65568 | tf_op jit(solution)/shard_map/ppermute | solution.py:690
  23.3 0.8 %patch.1 = (f32[16,8,384]{2,1,0:T(8,128)S(1)}, f32[16,8,384]{2,1,0:T(8,128)S(1)}, f32[16,8,384]{2,1,0:T(8,128)S(1)}, f32[16,8,384]{2,1,0:T(8,128)S(1)}, f32[16,8...) custom-call(f32[3,16,8,128]{3,2,1,0:T(8,128)S(1)} %get-tuple-element, ...), custom_call_target="tpu_custom_call" | custom-call | tf_op jit(solution)/shard_map/patch/pallas_call | solution.py:710
  24.1 0.3 %all-to-all-done.blocks_ref = f32[32,8,128]{2,1,0:T(8,128)S(1)} async-done(((f32[32,8,128]{2,1,0:T(8,128)}), f32[32,8,128]{2,1,0:T(8,128)S(1)}, u32[]{:S(2)}, u32[]{:S(2)}) %all-to-all-start) | async-done | bytes 131104 | tf_op jit(solution)/shard_map/all_to_all | solution.py:692
  24.4 2.4 %ascend.1 = (f32[64,256]{1,0:T(8,128)}, f32[64,256]{1,0:T(8,128)}) custom-call(f32[32,8,128]{2,1,0:T(8,128)S(1)} %all-to-all-done.blocks_ref, f32[16,8,384]{2,1,0:T(8,128)S(1)} %get-tuple-element.83.rest_0_, f32[16,8,384]{2,1,0:T(8,128)S(1)} %get-tuple-element.84.rest_1_, f32[16,8,384]{2,1,0:T(8,128)S(1)} %get-tuple-element.85.rest_2_, ...), custom_call_target="tpu_custom_call" | custom-call | tf_op jit(solution)/shard_map/ascend/pallas_call | solution.py:720
  (11 shorter events, 0.1 us)
Async XLA Ops:
  1.7 8.0 %collective-permute-start.2 = (f32[64,128]{1,0:T(8,128)S(1)}, f32[64,128]{1,0:T(8,128)S(1)}, u32[]{:S(2)}, u32[]{:S(2)}) collective-permute-start(f32[64,128]{1,0:T(8,128)S(1)} %get-tuple-element.56.east_edge_ref), channel_id=1, source_target_pairs={{0,4},{4,8},{8,12},{12,16},{16,20},{20,24},{24,28},{28,0},{1,5},{5... | collective-permute-start | bytes 98312 | tf_op jit(solution)/shard_map/ppermute | solution.py:654
  4.7 5.1 %collective-permute-start.4 = (f32[32,128]{1,0:T(8,128)S(1)}, f32[32,128]{1,0:T(8,128)S(1)}, u32[]{:S(2)}, u32[]{:S(2)}) collective-permute-start(f32[32,128]{1,0:T(8,128)S(1)} %prepare_corner.1.corner_ref), channel_id=1, source_target_pairs={{0,4},{1,6},{2,5},{3,7},{4,0},{5,10},{6,9},{7,3},{8,12},{9,14},{10... | collective-permute-start | bytes 49160 | tf_op jit(solution)/shard_map/ppermute | solution.py:656
  6.3 4.6 %collective-permute-start.1 = (f32[16,1024]{1,0:T(8,128)S(1)}, f32[16,1024]{1,0:T(8,128)S(1)}, u32[]{:S(2)}, u32[]{:S(2)}) collective-permute-start(f32[16,1024]{1,0:T(8,128)S(1)} %get-tuple-element.55), channel_id=1, source_target_pairs={{0,4},{1,2},{2,1},{3,7},{4,0},{5,6},{6,5},{7,3},{8,12},{9,10},{10,... | collective-permute-start | bytes 196616 | tf_op jit(solution)/shard_map/ppermute | solution.py:655
  6.9 4.0 %collective-permute-start = (f32[32,896]{1,0:T(8,128)S(1)}, f32[32,896]{1,0:T(8,128)S(1)}, u32[]{:S(2)}, u32[]{:S(2)}) collective-permute-start(f32[32,896]{1,0:T(8,128)S(1)} %get-tuple-element.54), channel_id=1, source_target_pairs={{0,1},{1,0},{2,3},{3,2},{4,5},{5,4},{6,7},{7,6},{8,9},{9,8},{10,11... | collective-permute-start | bytes 344072 | tf_op jit(solution)/shard_map/ppermute | solution.py:657
  9.7 1.2 %collective-permute-start.3 = (f32[32,128]{1,0:T(8,128)S(1)}, f32[32,128]{1,0:T(8,128)S(1)}, u32[]{:S(2)}, u32[]{:S(2)}) collective-permute-start(f32[32,128]{1,0:T(8,128)S(1)} %slice_select_fusion), channel_id=1, source_target_pairs={{0,1},{1,0},{2,3},{3,2},{4,5},{5,4},{6,7},{7,6},{8,9},{9,8},{10,11... | collective-permute-start | bytes 49160 | tf_op jit(solution)/shard_map/ppermute | solution.py:661
  9.7 4.2 %collective-permute-start.5 = (f32[16,768]{1,0:T(8,128)S(1)}, f32[16,768]{1,0:T(8,128)S(1)}, u32[]{:S(2)}, u32[]{:S(2)}) collective-permute-start(f32[16,768]{1,0:T(8,128)S(1)} %prepare_rest.1), channel_id=1, source_target_pairs={{0,4},{1,2},{2,1},{3,7},{4,0},{5,6},{6,5},{7,3},{8,12},{9,10},{10,... | collective-permute-start | bytes 147464 | tf_op jit(solution)/shard_map/ppermute | solution.py:659
  13.8 10.6 %all-to-all-start = ((f32[32,8,128]{2,1,0:T(8,128)}), f32[32,8,128]{2,1,0:T(8,128)S(1)}, u32[]{:S(2)}, u32[]{:S(2)}) async-start(f32[32,8,128]{2,1,0:T(8,128)} %get-tuple-element.60), calls=%async_computation | async-start | bytes 262144 | tf_op jit(solution)/shard_map/all_to_all | solution.py:692
  16.8 6.5 %collective-permute-start.6 = (f32[128,128]{1,0:T(8,128)S(1)}, f32[128,128]{1,0:T(8,128)S(1)}, u32[]{:S(2)}, u32[]{:S(2)}) collective-permute-start(f32[128,128]{1,0:T(8,128)S(1)} %get-tuple-element.63), channel_id=1, source_target_pairs={{4,0},{8,4},{12,8},{16,12},{20,16},{24,20},{28,24},{0,28},{5,1},{9... | collective-permute-start | bytes 196616 | tf_op jit(solution)/shard_map/ppermute | solution.py:690

commit v11 on v10

--- a/solution.py
+++ b/solution.py
@@ -353,14 +353,18 @@
     way_down(*fields, [scale_ref[0, t] for t in range(count)], [scale_ref[1, t] for t in range(count)], put)
 
 
-def descend(lat_count, own_ref, lat_near_ref, lat_far_ref, west_ref, west_near_ref, west_far_ref, west_edge_ref, scale_ref,
-            pack_ref, edge_ref, grid_ref, plain_ref):
-    rows = own_ref.shape[1]
-    edge = slice(FIELDS * own_ref.shape[2], FIELDS * own_ref.shape[2] + LANES)
+def gather_edges(lat_near_ref, lat_far_ref, west_edge_ref, edge_ref):
+    rows = west_edge_ref.shape[0]
+    edge = slice(lat_near_ref.shape[1] - LANES, lat_near_ref.shape[1])
     edge_ref[pl.ds(0, rows), :] = west_edge_ref[...]
     edge_ref[pl.ds(rows, HALO), :] = lat_near_ref[:, edge]
     edge_ref[pl.ds(rows + HALO, REACH), :] = lat_far_ref[:, edge]
     edge_ref[pl.ds(rows + HALO + REACH, HALO - REACH), :] = lat_far_ref[:, edge.stop :]
+
+
+def descend(lat_count, own_ref, lat_near_ref, lat_far_ref, west_ref, west_near_ref, west_far_ref, scale_ref,
+            pack_ref, grid_ref, plain_ref):
+    rows = own_ref.shape[1]
     lon_index = lax.axis_index("lon")
     cols = own_ref.shape[2]
     own_columns = cols // LANES
@@ -672,21 +676,28 @@
 
     devices = lat_count * lon_count
     grid = pltpu.VMEM((FIELDS, width // LANES, height, LANES), f32)
-    packed, edges = pl.pallas_call(
+    edges = pl.pallas_call(
+        gather_edges,
+        out_shape=jax.ShapeDtypeStruct((height, LANES), f32),
+        in_specs=[vmem] * 3,
+        out_specs=vmem,
+        compiler_params=params,
+        name="gather_edges",
+    )(lat_near, lat_far, west_edge)
+    packed = pl.pallas_call(
         functools.partial(descend, lat_count),
         out_shape=[
             jax.ShapeDtypeStruct((devices, rows >> LEVELS, LANES), f32),
-            jax.ShapeDtypeStruct((height, LANES), f32),
         ],
-        in_specs=[vmem] * 8,
-        out_specs=[vmem] * 2,
+        in_specs=[vmem] * 7,
+        out_specs=[vmem] * 1,
         scratch_shapes=[
             pltpu.VMEM((FIELDS, width // LANES, rows + 2 * REACH, LANES), f32),
             pltpu.VMEM((4, width // LANES, (rows + 2 * REACH) >> (LEVELS - 1), LANES), f32),
         ],
         compiler_params=params,
         name="descend",
-    )(own, lat_near, lat_far, west_halo, west_near, west_far, west_edge, scales(REACH))
+    )(own, lat_near, lat_far, west_halo, west_near, west_far, scales(REACH))[0]
     east_halo = lax.ppermute(edges, "lon", westward)
     packed, lat_rest = lax.optimization_barrier((packed, lat_rest))
     blocks = lax.all_to_all(packed, ("lat", "lon"), 0, 0, tiled=True)
@@ -703,7 +714,6 @@
         out_specs=[vmem] * (1 + len(held_shapes)),
         scratch_shapes=[grid],
         compiler_params=params,
-        cost_estimate=pl.CostEstimate(flops=0, bytes_accessed=60 * 1024 * 1024, transcendentals=0),
         name="hold",
     )(own, lat_near, lat_far, lat_rest, west_halo, west_near, west_far, fine_scale)
     held, raw = held[:-1], held[-1]

time: 27 us -> 27 us (level)
  no operation moved by 1% of the time
where the time goes in v11:
time: 27 us; the launch traced here: 26.8 us
  starting transfers between devices  13.2 us (49%)
  Pallas kernels  7.1 us (26%)
  waiting for transfers between devices  5.1 us (19%)
  between operations  0.75 us (3%)
  local copies, waits for them, and re-layouts  0.33 us (1%)
  other arithmetic  0.28 us (1%)
    ppermute x1, starting transfers between devices, on_device(): east_halo = lax.ppermute(edges, 'lon', westward)  4.6 us
    ppermute x1, starting transfers between devices, on_device(): west_halo = lax.ppermute(east_edge, 'lon', eastward)  3.02 us
    all_to_all x1, starting transfers between devices, on_device(): blocks = lax.all_to_all(packed, ('lat', 'lon'), 0, 0, tiled=True)  2.85 us
    pallas_call x1, Pallas kernels, on_device(): pl.pallas_call(functools.partial(ascend, lat_count, lon_count), out_shape...  2.38 us
    ppermute x1, waiting for transfers between devices, on_device(): west_halo = lax.ppermute(east_edge, 'lon', eastward)  2 us
    pallas_call x1, Pallas kernels, on_device(): pl.pallas_call(functools.partial(descend, lat_count), out_shape=[jax.Shap...  1.67 us
    ppermute x1, starting transfers between devices, on_device(): lax.ppermute(diagonal_edge, ('lon', 'lat'), far_pairs(lon_count, lat_coun...  1.52 us
    ppermute x1, waiting for transfers between devices, on_device(): lax.ppermute(lat_rest, ('lon', 'lat'), far_pairs(lon_count, lat_count, 0))  1.21 us
  transfers between devices with their start and end apart: 8, of which 5 were waited for; matrix products, arithmetic and copies ran while one was open for 2% of the time, Pallas kernels for 14%

profile of v11, /device:TPU:0, one launch (start us, length us, event | category | flops | bytes accessed | tf_op | source)
XLA Modules:
  0.0 26.8 jit_solution(17123029674400352192)
XLA Ops:
  0.6 1.1 %prepare.1 = (f32[3,64,256]{2,1,0:T(8,128)S(1)}, f32[64,128]{1,0:T(8,128)S(1)}, f32[64,128]{1,0:T(8,128)S(1)}) custom-call(f32[64,256]{1,0:T(8,128)} %forcing_ref.1, f32[64,256]{1,0:T(8,128)} %surface_ref.1, s32[64,256]{1,0:T(8,128)} %sea_ref.1, s32[64,256]{1,0:T(8,128)} %levels_ref.1), custom_call_target="tpu_custom_call" | custom-call | tf_op jit(solution)/shard_map/prepare/pallas_call | solution.py:607
  1.7 3.0 %collective-permute-start.2 = (f32[64,128]{1,0:T(8,128)S(1)}, f32[64,128]{1,0:T(8,128)S(1)}, u32[]{:S(2)}, u32[]{:S(2)}) collective-permute-start(f32[64,128]{1,0:T(8,128)S(1)} %get-tuple-element.54.east_edge_ref), channel_id=1, source_target_pairs={{0,4},{4,8},{8,12},{12,16},{16,20},{20,24},{24,28},{28,0},{1,5},{5... | collective-permute-start | bytes 98312 | tf_op jit(solution)/shard_map/ppermute | solution.py:658
  4.7 1.5 %collective-permute-start.4 = (f32[32,128]{1,0:T(8,128)S(1)}, f32[32,128]{1,0:T(8,128)S(1)}, u32[]{:S(2)}, u32[]{:S(2)}) collective-permute-start(f32[32,128]{1,0:T(8,128)S(1)} %prepare_corner.1.corner_ref), channel_id=1, source_target_pairs={{0,4},{1,6},{2,5},{3,7},{4,0},{5,10},{6,9},{7,3},{8,12},{9,14},{10... | collective-permute-start | bytes 49160 | tf_op jit(solution)/shard_map/ppermute | solution.py:660
  6.3 0.6 %collective-permute-start.1 = (f32[16,1024]{1,0:T(8,128)S(1)}, f32[16,1024]{1,0:T(8,128)S(1)}, u32[]{:S(2)}, u32[]{:S(2)}) collective-permute-start(f32[16,1024]{1,0:T(8,128)S(1)} %get-tuple-element.53), channel_id=1, source_target_pairs={{0,4},{1,2},{2,1},{3,7},{4,0},{5,6},{6,5},{7,3},{8,12},{9,10},{10,... | collective-permute-start | bytes 196616 | tf_op jit(solution)/shard_map/ppermute | solution.py:659
  6.9 0.6 %collective-permute-start = (f32[32,896]{1,0:T(8,128)S(1)}, f32[32,896]{1,0:T(8,128)S(1)}, u32[]{:S(2)}, u32[]{:S(2)}) collective-permute-start(f32[32,896]{1,0:T(8,128)S(1)} %get-tuple-element.52), channel_id=1, source_target_pairs={{0,1},{1,0},{2,3},{3,2},{4,5},{5,4},{6,7},{7,6},{8,9},{9,8},{10,11... | collective-permute-start | bytes 344072 | tf_op jit(solution)/shard_map/ppermute | solution.py:661
  7.5 0.1 cosine_divide_fusion.1
  7.7 2.0 %collective-permute-done.2.west_ref = f32[64,128]{1,0:T(8,128)S(1)} collective-permute-done((f32[64,128]{1,0:T(8,128)S(1)}, f32[64,128]{1,0:T(8,128)S(1)}, u32[]{:S(2)}, u32[]{:S(2)}) %collective-permute-start.2) | collective-permute-done | bytes 32800 | tf_op jit(solution)/shard_map/ppermute | solution.py:658
  9.7 0.0 collective-permute-start.3
  9.7 0.1 collective-permute-start.5
  9.8 0.1 copy.6
  9.9 1.0 %collective-permute-done.3.west_near_ref = f32[32,128]{1,0:T(8,128)S(1)} collective-permute-done((f32[32,128]{1,0:T(8,128)S(1)}, f32[32,128]{1,0:T(8,128)S(1)}, u32[]{:S(2)}, u32[]{:S(2)}) %collective-permute-start.3) | collective-permute-done | bytes 16416 | tf_op jit(solution)/shard_map/ppermute | solution.py:665
  10.9 0.1 broadcast_in_dim.4.scale_ref
  10.9 1.7 %descend.1 = f32[32,8,128]{2,1,0:T(8,128)} custom-call(f32[3,64,256]{2,1,0:T(8,128)S(1)} %get-tuple-element.50.own_ref, f32[32,896]{1,0:T(8,128)S(1)} %collective-permute-done.lat_near_ref, f32[16,1024]{1,0:T(8,128)S(1)} %collective-permute-done.1.lat_far_ref, f32[64,128]{1,0:T(8,128)S(1)} %collective-permute-done.2.west_ref, ...), custom_call_target="tpu_custom_call" | custom-call | tf_op jit(solution)/shard_map/descend/pallas_call | solution.py:687
  12.6 1.2 %collective-permute-done.5.lat_rest_ref = f32[16,768]{1,0:T(8,128)S(1)} collective-permute-done((f32[16,768]{1,0:T(8,128)S(1)}, f32[16,768]{1,0:T(8,128)S(1)}, u32[]{:S(2)}, u32[]{:S(2)}) %collective-permute-start.5) | collective-permute-done | bytes 49184 | tf_op jit(solution)/shard_map/ppermute | solution.py:663
  13.8 2.8 %all-to-all-start = ((f32[32,8,128]{2,1,0:T(8,128)}), f32[32,8,128]{2,1,0:T(8,128)S(1)}, u32[]{:S(2)}, u32[]{:S(2)}) async-start(f32[32,8,128]{2,1,0:T(8,128)} %descend.1), calls=%async_computation | async-start | bytes 262144 | tf_op jit(solution)/shard_map/all_to_all | solution.py:703
  16.7 0.1 cosine_divide_fusion
  16.8 4.6 %collective-permute-start.6 = (f32[128,128]{1,0:T(8,128)S(1)}, f32[128,128]{1,0:T(8,128)S(1)}, u32[]{:S(2)}, u32[]{:S(2)}) collective-permute-start(f32[128,128]{1,0:T(8,128)S(1)} %gather_edges.1), channel_id=1, source_target_pairs={{4,0},{8,4},{12,8},{16,12},{20,16},{24,20},{28,24},{0,28},{5,1},{9... | collective-permute-start | bytes 196616 | tf_op jit(solution)/shard_map/ppermute | solution.py:701
  21.4 0.1 copy.7
  21.5 0.1 broadcast_in_dim.5.scale_ref
  21.6 1.2 %hold.1 = (f32[16,8,384]{2,1,0:T(8,128)S(1)}, f32[16,8,384]{2,1,0:T(8,128)S(1)}, f32[16,8,384]{2,1,0:T(8,128)S(1)}, f32[16,8,384]{2,1,0:T(8,128)S(1)}, f32[16,8,...) custom-call(f32[3,64,256]{2,1,0:T(8,128)S(1)} %get-tuple-element.50., ...), custom_call_target="tpu_custom_call" | custom-call | tf_op jit(solution)/shard_map/hold/pallas_call | solution.py:710
  22.8 0.6 %collective-permute-done.6.east_ref = f32[128,128]{1,0:T(8,128)S(1)} collective-permute-done((f32[128,128]{1,0:T(8,128)S(1)}, f32[128,128]{1,0:T(8,128)S(1)}, u32[]{:S(2)}, u32[]{:S(2)}) %collective-permute-start.6) | collective-permute-done | bytes 65568 | tf_op jit(solution)/shard_map/ppermute | solution.py:701
  23.3 0.8 %patch.1 = (f32[16,8,384]{2,1,0:T(8,128)S(1)}, f32[16,8,384]{2,1,0:T(8,128)S(1)}, f32[16,8,384]{2,1,0:T(8,128)S(1)}, f32[16,8,384]{2,1,0:T(8,128)S(1)}, f32[16,8...) custom-call(f32[3,16,8,128]{3,2,1,0:T(8,128)S(1)} %get-tuple-element, ...), custom_call_target="tpu_custom_call" | custom-call | tf_op jit(solution)/shard_map/patch/pallas_call | solution.py:720
  24.1 0.3 %all-to-all-done.blocks_ref = f32[32,8,128]{2,1,0:T(8,128)S(1)} async-done(((f32[32,8,128]{2,1,0:T(8,128)}), f32[32,8,128]{2,1,0:T(8,128)S(1)}, u32[]{:S(2)}, u32[]{:S(2)}) %all-to-all-start) | async-done | bytes 131104 | tf_op jit(solution)/shard_map/all_to_all | solution.py:703
  24.4 2.4 %ascend.1 = (f32[64,256]{1,0:T(8,128)}, f32[64,256]{1,0:T(8,128)}) custom-call(f32[32,8,128]{2,1,0:T(8,128)S(1)} %all-to-all-done.blocks_ref, f32[16,8,384]{2,1,0:T(8,128)S(1)} %get-tuple-element.79.rest_0_, f32[16,8,384]{2,1,0:T(8,128)S(1)} %get-tuple-element.80.rest_1_, f32[16,8,384]{2,1,0:T(8,128)S(1)} %get-tuple-element.81.rest_2_, ...), custom_call_target="tpu_custom_call" | custom-call | tf_op jit(solution)/shard_map/ascend/pallas_call | solution.py:730
  (12 shorter events, 0.1 us)
Async XLA Ops:
  1.7 8.0 %collective-permute-start.2 = (f32[64,128]{1,0:T(8,128)S(1)}, f32[64,128]{1,0:T(8,128)S(1)}, u32[]{:S(2)}, u32[]{:S(2)}) collective-permute-start(f32[64,128]{1,0:T(8,128)S(1)} %get-tuple-element.54.east_edge_ref), channel_id=1, source_target_pairs={{0,4},{4,8},{8,12},{12,16},{16,20},{20,24},{24,28},{28,0},{1,5},{5... | collective-permute-start | bytes 98312 | tf_op jit(solution)/shard_map/ppermute | solution.py:658
  4.7 5.1 %collective-permute-start.4 = (f32[32,128]{1,0:T(8,128)S(1)}, f32[32,128]{1,0:T(8,128)S(1)}, u32[]{:S(2)}, u32[]{:S(2)}) collective-permute-start(f32[32,128]{1,0:T(8,128)S(1)} %prepare_corner.1.corner_ref), channel_id=1, source_target_pairs={{0,4},{1,6},{2,5},{3,7},{4,0},{5,10},{6,9},{7,3},{8,12},{9,14},{10... | collective-permute-start | bytes 49160 | tf_op jit(solution)/shard_map/ppermute | solution.py:660
  6.3 4.6 %collective-permute-start.1 = (f32[16,1024]{1,0:T(8,128)S(1)}, f32[16,1024]{1,0:T(8,128)S(1)}, u32[]{:S(2)}, u32[]{:S(2)}) collective-permute-start(f32[16,1024]{1,0:T(8,128)S(1)} %get-tuple-element.53), channel_id=1, source_target_pairs={{0,4},{1,2},{2,1},{3,7},{4,0},{5,6},{6,5},{7,3},{8,12},{9,10},{10,... | collective-permute-start | bytes 196616 | tf_op jit(solution)/shard_map/ppermute | solution.py:659
  6.9 4.0 %collective-permute-start = (f32[32,896]{1,0:T(8,128)S(1)}, f32[32,896]{1,0:T(8,128)S(1)}, u32[]{:S(2)}, u32[]{:S(2)}) collective-permute-start(f32[32,896]{1,0:T(8,128)S(1)} %get-tuple-element.52), channel_id=1, source_target_pairs={{0,1},{1,0},{2,3},{3,2},{4,5},{5,4},{6,7},{7,6},{8,9},{9,8},{10,11... | collective-permute-start | bytes 344072 | tf_op jit(solution)/shard_map/ppermute | solution.py:661
  9.7 1.2 %collective-permute-start.3 = (f32[32,128]{1,0:T(8,128)S(1)}, f32[32,128]{1,0:T(8,128)S(1)}, u32[]{:S(2)}, u32[]{:S(2)}) collective-permute-start(f32[32,128]{1,0:T(8,128)S(1)} %slice_select_fusion), channel_id=1, source_target_pairs={{0,1},{1,0},{2,3},{3,2},{4,5},{5,4},{6,7},{7,6},{8,9},{9,8},{10,11... | collective-permute-start | bytes 49160 | tf_op jit(solution)/shard_map/ppermute | solution.py:665
  9.7 4.2 %collective-permute-start.5 = (f32[16,768]{1,0:T(8,128)S(1)}, f32[16,768]{1,0:T(8,128)S(1)}, u32[]{:S(2)}, u32[]{:S(2)}) collective-permute-start(f32[16,768]{1,0:T(8,128)S(1)} %prepare_rest.1), channel_id=1, source_target_pairs={{0,4},{1,2},{2,1},{3,7},{4,0},{5,6},{6,5},{7,3},{8,12},{9,10},{10,... | collective-permute-start | bytes 147464 | tf_op jit(solution)/shard_map/ppermute | solution.py:663
  13.8 10.6 %all-to-all-start = ((f32[32,8,128]{2,1,0:T(8,128)}), f32[32,8,128]{2,1,0:T(8,128)S(1)}, u32[]{:S(2)}, u32[]{:S(2)}) async-start(f32[32,8,128]{2,1,0:T(8,128)} %descend.1), calls=%async_computation | async-start | bytes 262144 | tf_op jit(solution)/shard_map/all_to_all | solution.py:703
  16.8 6.5 %collective-permute-start.6 = (f32[128,128]{1,0:T(8,128)S(1)}, f32[128,128]{1,0:T(8,128)S(1)}, u32[]{:S(2)}, u32[]{:S(2)}) collective-permute-start(f32[128,128]{1,0:T(8,128)S(1)} %gather_edges.1), channel_id=1, source_target_pairs={{4,0},{8,4},{12,8},{16,12},{20,16},{24,20},{28,24},{0,28},{5,1},{9... | collective-permute-start | bytes 196616 | tf_op jit(solution)/shard_map/ppermute | solution.py:701
